TPU v7x, 32 devices: a whole 2x2x4 slice. The times are simulated.
32 devices in a mesh: section: 2 (over core), dp: 16 (over z, y, x).
Axes of the slice: x: 2, y: 2, z: 4, core: 2. Of those that a mesh axis runs over, the one named last changes fastest.
Arguments:
- features: bfloat16 [64, 28, 12544], P('dp', 'section'), may hold values from -6 to 6
- crop_side: int32 [64], P('dp'), may hold values from 14 to 28, as said below
- upstream: bfloat16 [64, 14, 12544], P('dp', 'section'), may hold values from -6 to 6
- entry_in: bfloat16 [401408], P(('section', 'dp')), may hold values from -0.25 to 0.25
- entry_group: bfloat16 [451584], P(('section', 'dp')), may hold values from -0.25 to 0.25
- entry_out: bfloat16 [802816], P(('section', 'dp')), may hold values from -0.1875 to 0.1875
- entry_down: bfloat16 [100352], P(('section', 'dp')), may hold values from -0.75 to 0.75
- entry_up: bfloat16 [100352], P(('section', 'dp')), may hold values from -2 to 2
- shortcut_weight: bfloat16 [401408], P(('section', 'dp')), may hold values from -0.25 to 0.25
- body_in: bfloat16 [802816], P(('section', 'dp')), may hold values from -0.1875 to 0.1875
- body_group: bfloat16 [451584], P(('section', 'dp')), may hold values from -0.25 to 0.25
- body_out: bfloat16 [802816], P(('section', 'dp')), may hold values from -0.1875 to 0.1875
- body_down: bfloat16 [200704], P(('section', 'dp')), may hold values from -0.75 to 0.75
- body_up: bfloat16 [200704], P(('section', 'dp')), may hold values from -1.5 to 1.5
- norm_gain: float32 [2, 3, 896], P('section'), may hold values from 0.25 to 1.75
- norm_shift: float32 [2, 3, 896], P('section'), may hold values from -3 to 3
- shortcut_gain: bfloat16 [896], P('section'), may hold values from 0.25 to 1.75
- shortcut_shift: bfloat16 [896], P('section'), may hold values from -3 to 3
Outputs:
- output: bfloat16 [64, 14, 12544], P('dp', 'section')
- grad_features: bfloat16 [64, 28, 12544], P('dp', 'section')
- grad_entry_in: float32 [401408], P(('section', 'dp'))
- grad_entry_group: float32 [451584], P(('section', 'dp'))
- grad_entry_out: float32 [802816], P(('section', 'dp'))
- grad_entry_down: float32 [100352], P(('section', 'dp'))
- grad_entry_up: float32 [100352], P(('section', 'dp'))
- grad_shortcut_weight: float32 [401408], P(('section', 'dp'))
- grad_body_in: float32 [802816], P(('section', 'dp'))
- grad_body_group: float32 [451584], P(('section', 'dp'))
- grad_body_out: float32 [802816], P(('section', 'dp'))
- grad_body_down: float32 [200704], P(('section', 'dp'))
- grad_body_up: float32 [200704], P(('section', 'dp'))
- grad_norm_gain: float32 [2, 3, 896], P('section')
- grad_norm_shift: float32 [2, 3, 896], P('section')
- grad_shortcut_gain: float32 [896], P('section')
- grad_shortcut_shift: float32 [896], P('section')
Inputs may be any that keep to these rules, and one draw needn't show every extreme that they name: `crop_side`: each crop has side 28 or 14; among the 4 crops of every index of dp at least one has side 28.
All inputs are finite; a program needn't handle non-finite values.
Results may differ from a plain program's by a relative error of at most 0.017.
Values may be sent and summed in bfloat16 or wider, within the bound.
A program may use at most 320 MiB of HBM per device.

v0:
```python
import jax
import jax.numpy as jnp
from jax import lax
from jax.sharding import PartitionSpec as P

D = 896
DIN = 448
GROUPS = 16
GW = 56
SE0 = 112
SE1 = 224
OUT = 14
MICRO = 4
CROP_MB = 1
IN = 28


EPSILON = 1e-05
HIGHEST = lax.Precision.HIGHEST


def shifted(block, axis, distance):
    devices = range(lax.axis_size(axis))
    route = [(i - distance, i) for i in devices if i - distance in devices]
    return lax.ppermute(block, axis, route)


def smooth_gate(values):
    return values * jax.nn.sigmoid(values)


def gate_slope(values):
    logistic = jax.nn.sigmoid(values)
    return logistic * (1.0 + values * (1.0 - logistic))


def moments_of(totals, population):
    center = totals[0] / population
    scaling = lax.rsqrt(totals[1] / population - center * center + EPSILON)
    return (center, scaling)


def masked_moments(values, masking):
    weighted = masking * values
    return jnp.stack(
        [jnp.sum(weighted, axis=(0, 1, 2)), jnp.sum(weighted * values, axis=(0, 1, 2))]
    )


def column_sums(values):
    return jnp.sum(values, axis=(0, 1, 2))


def forward_sums(local_sums, population):
    return lax.psum((local_sums, population), "dp")


def backward_sums(local_sums):
    return lax.psum(local_sums, "dp")


def widen(values):
    margin = IN - OUT
    return jnp.pad(values, ((0, 0), (0, margin), (0, margin), (0, 0)))


def pixel_dot(values, weight):
    flattened = values.reshape(-1, weight.shape[0])
    result = jnp.dot(flattened, weight, preferred_element_type=jnp.float32)
    return result.reshape(values.shape[:3] + (weight.shape[1],))


def pixel_back(values, weight):
    flattened = values.reshape(-1, weight.shape[1])
    result = lax.dot_general(
        flattened, weight, (((1,), (1,)), ((), ())), preferred_element_type=jnp.float32
    )
    return result.reshape(values.shape[:3] + (weight.shape[0],))


def pixel_outer(inputs, cotangents):
    return lax.dot_general(
        inputs.reshape(-1, inputs.shape[-1]),
        cotangents.reshape(-1, cotangents.shape[-1]),
        (((0,), (0,)), ((), ())),
        preferred_element_type=jnp.float32,
    )


def tap_patches(activated, stride, size):
    padded = jnp.pad(activated, ((0, 0), (1, 1), (1, 1), (0, 0)))
    extent = size * stride
    fragments = [
        padded[:, row_tap : row_tap + extent : stride, col_tap : col_tap + extent : stride]
        for row_tap in range(3)
        for col_tap in range(3)
    ]
    return jnp.stack(fragments, 0).reshape(9, -1, GROUPS, GW)


def grouped_apply(activated, kernel, stride, size):
    patches = tap_patches(activated, stride, size)
    result = jnp.einsum(
        "tpgi,tigo->pgo",
        patches,
        kernel.reshape(9, GW, GROUPS, GW),
        preferred_element_type=jnp.float32,
    )
    return result.reshape(activated.shape[0], size, size, GROUPS * GW)


def grouped_back(activated, kernel, grad_conv, stride, size):
    patches = tap_patches(activated, stride, size)
    grad_rows = grad_conv.reshape(-1, GROUPS, GW)
    kernel_grad = jnp.einsum(
        "tpgi,pgo->tigo", patches, grad_rows, preferred_element_type=jnp.float32
    ).reshape(9, GW, GROUPS * GW)
    patch_grad = jnp.einsum(
        "pgo,tigo->tpgi",
        grad_rows,
        kernel.reshape(9, GW, GROUPS, GW),
        preferred_element_type=jnp.float32,
    )
    patch_grad = patch_grad.reshape(9, activated.shape[0], size, size, GROUPS * GW)
    extent = size * stride
    padded = jnp.zeros((activated.shape[0], extent + 2, extent + 2, GROUPS * GW), jnp.float32)
    for row_tap in range(3):
        for col_tap in range(3):
            padded = padded.at[
                :, row_tap : row_tap + extent : stride, col_tap : col_tap + extent : stride
            ].add(patch_grad[row_tap * 3 + col_tap])
    return (padded[:, 1 : extent + 1, 1 : extent + 1], kernel_grad)


def section_forward(
    use_first, first_part, last_part, mask_wide, mask_out, crop_count, weights, norm_set, statistics
):
    first_in, last_in, kernel, weight_out, squeeze, expand, shortcut_full = weights
    gains, shifts, short_gain, short_shift = norm_set

    def input_first(unused):
        return pixel_dot(first_part, first_in)

    def input_last(unused):
        return widen(pixel_dot(last_part, last_in))

    inner_raw = lax.cond(use_first, input_first, input_last, 0)
    if statistics is None:
        sums_in, count_in = forward_sums(masked_moments(inner_raw, mask_wide), jnp.sum(mask_wide))
    else:
        sums_in, count_in = statistics[0]
    count_out = jnp.where(use_first, count_in / 4.0, count_in)
    center_a, scaling_a = moments_of(sums_in, count_in)
    normed_a = (inner_raw - center_a) * scaling_a * gains[0] + shifts[0]
    activated = (mask_wide * smooth_gate(normed_a)).astype(jnp.bfloat16)

    def conv_first(unused):
        return grouped_apply(activated, kernel, 2, OUT)

    def conv_last(unused):
        return grouped_apply(activated[:, :OUT, :OUT], kernel, 1, OUT)

    convolved = lax.cond(use_first, conv_first, conv_last, 0)
    if statistics is None:
        sums_mid, unused_mid = forward_sums(masked_moments(convolved, mask_out), jnp.sum(mask_out))
    else:
        sums_mid = statistics[1]
    center_b, scaling_b = moments_of(sums_mid, count_out)
    normed_b = (convolved - center_b) * scaling_b * gains[1] + shifts[1]
    excited = mask_out * smooth_gate(normed_b)
    pooled = jnp.sum(excited, axis=(1, 2)) / crop_count[:, None]
    squeeze_raw = jnp.dot(pooled, squeeze, precision=HIGHEST)
    squeezed = smooth_gate(squeeze_raw)
    gating = jax.nn.sigmoid(jnp.dot(squeezed, expand, precision=HIGHEST))
    gated = (excited * gating[:, None, None, :]).astype(jnp.bfloat16)
    projected = pixel_dot(gated, weight_out)

    def short_first(unused):
        return pixel_dot(first_part[:, ::2, ::2], shortcut_full)

    def short_last(unused):
        return jnp.zeros_like(projected)

    strided = lax.cond(use_first, short_first, short_last, 0)
    if statistics is None:
        both_moments = jnp.concatenate(
            [masked_moments(projected, mask_out), masked_moments(strided, mask_out)], 0
        )
        sums_out, unused_out = forward_sums(both_moments, jnp.sum(mask_out))
    else:
        sums_out = statistics[2]
    center_c, scaling_c = moments_of(sums_out[0:2], count_out)
    center_s, scaling_s = moments_of(sums_out[2:4], count_out)
    normed_s = (strided - center_s) * scaling_s * short_gain + short_shift
    residual = jnp.where(use_first, normed_s, last_part.astype(jnp.float32))
    summed = (projected - center_c) * scaling_c * gains[2] + shifts[2] + residual
    output = mask_out * smooth_gate(summed)
    statistics = ((sums_in, count_in), sums_mid, sums_out)
    kept_values = (
        inner_raw,
        activated,
        convolved,
        excited,
        pooled,
        squeeze_raw,
        squeezed,
        gating,
        gated,
        projected,
        strided,
        summed,
    )
    return (output, statistics, kept_values)


def section_backward(
    use_first,
    first_part,
    last_part,
    mask_wide,
    mask_out,
    crop_count,
    weights,
    norm_set,
    statistics,
    kept_values,
    grad_output,
):
    first_in, last_in, kernel, weight_out, squeeze, expand, shortcut_full = weights
    gains, shifts, short_gain, short_shift = norm_set
    (
        inner_raw,
        activated,
        convolved,
        excited,
        pooled,
        squeeze_raw,
        squeezed,
        gating,
        gated,
        projected,
        strided,
        summed,
    ) = kept_values
    (sums_in, count_in), sums_mid, sums_out = statistics
    count_out = jnp.where(use_first, count_in / 4.0, count_in)
    center_a, scaling_a = moments_of(sums_in, count_in)
    center_b, scaling_b = moments_of(sums_mid, count_out)
    center_c, scaling_c = moments_of(sums_out[0:2], count_out)
    center_s, scaling_s = moments_of(sums_out[2:4], count_out)
    grad_summed = grad_output * mask_out * gate_slope(summed)
    hat_c = (projected - center_c) * scaling_c
    hat_s = (strided - center_s) * scaling_s
    totals_out = backward_sums(
        jnp.stack(
            [
                column_sums(grad_summed),
                column_sums(grad_summed * hat_c),
                column_sums(grad_summed * hat_s),
            ]
        )
    )
    centered = grad_summed - totals_out[0] / count_out
    grad_projected = (
        gains[2] * scaling_c * (centered - hat_c * totals_out[1] / count_out) * mask_out
    ).astype(jnp.bfloat16)
    grad_strided = (
        short_gain * scaling_s * (centered - hat_s * totals_out[2] / count_out) * mask_out
    ).astype(jnp.bfloat16)
    weight_out_grad = pixel_outer(gated, grad_projected)
    grad_gated = pixel_back(grad_projected, weight_out)
    grad_excited = grad_gated * gating[:, None, None, :]
    grad_gating = jnp.sum(grad_gated * excited, axis=(1, 2))
    grad_gate_raw = grad_gating * gating * (1.0 - gating)
    expand_grad = jnp.dot(squeezed.T, grad_gate_raw, precision=HIGHEST)
    grad_squeeze_raw = jnp.dot(grad_gate_raw, expand.T, precision=HIGHEST) * gate_slope(squeeze_raw)
    squeeze_grad = jnp.dot(pooled.T, grad_squeeze_raw, precision=HIGHEST)
    grad_pooled = jnp.dot(grad_squeeze_raw, squeeze.T, precision=HIGHEST) / crop_count[:, None]
    grad_excited = grad_excited + grad_pooled[:, None, None, :]
    hat_b = (convolved - center_b) * scaling_b
    grad_normed_b = grad_excited * mask_out * gate_slope(hat_b * gains[1] + shifts[1])
    totals_mid = backward_sums(
        jnp.stack([column_sums(grad_normed_b), column_sums(grad_normed_b * hat_b)])
    )
    grad_convolved = (
        gains[1]
        * scaling_b
        * (grad_normed_b - totals_mid[0] / count_out - hat_b * totals_mid[1] / count_out)
        * mask_out
    ).astype(jnp.bfloat16)

    def conv_first(unused):
        return grouped_back(activated, kernel, grad_convolved, 2, OUT)

    def conv_last(unused):
        grad_narrow, kernel_grad = grouped_back(
            activated[:, :OUT, :OUT], kernel, grad_convolved, 1, OUT
        )
        return (widen(grad_narrow), kernel_grad)

    grad_activated, kernel_grad = lax.cond(use_first, conv_first, conv_last, 0)
    hat_a = (inner_raw - center_a) * scaling_a
    grad_normed_a = grad_activated * mask_wide * gate_slope(hat_a * gains[0] + shifts[0])
    totals_in = backward_sums(
        jnp.stack([column_sums(grad_normed_a), column_sums(grad_normed_a * hat_a)])
    )
    grad_inner = (
        gains[0]
        * scaling_a
        * (grad_normed_a - totals_in[0] / count_in - hat_a * totals_in[1] / count_in)
        * mask_wide
    ).astype(jnp.bfloat16)

    def input_first(unused):
        entry_grad = pixel_outer(first_part, grad_inner)
        grad_first = pixel_back(grad_inner, first_in)
        shortcut_grad = pixel_outer(first_part[:, ::2, ::2], grad_strided)
        grad_first = grad_first.at[:, ::2, ::2].add(pixel_back(grad_strided, shortcut_full))
        return (
            entry_grad,
            jnp.zeros(last_in.shape, jnp.float32),
            shortcut_grad,
            grad_first,
            jnp.zeros(last_part.shape, jnp.float32),
        )

    def input_last(unused):
        narrow = grad_inner[:, :OUT, :OUT]
        body_grad = pixel_outer(last_part, narrow)
        grad_last = pixel_back(narrow, last_in) + grad_summed
        return (
            jnp.zeros(first_in.shape, jnp.float32),
            body_grad,
            jnp.zeros(shortcut_full.shape, jnp.float32),
            jnp.zeros(first_part.shape, jnp.float32),
            grad_last,
        )

    entry_grad, body_grad, shortcut_grad, grad_first, grad_last = lax.cond(
        use_first, input_first, input_last, 0
    )
    weight_grads = (
        entry_grad,
        body_grad,
        kernel_grad,
        weight_out_grad,
        squeeze_grad,
        expand_grad,
        shortcut_grad,
    )
    norm_grads = (
        jnp.stack([totals_in[1], totals_mid[1], totals_out[1]]),
        jnp.stack([totals_in[0], totals_mid[0], totals_out[0]]),
        totals_out[2],
        totals_out[0],
    )
    return (grad_first, grad_last, weight_grads, norm_grads)


def spread_grads(weight_grads, lead):
    entry_grad, body_grad, kernel_grad, out_grad, squeeze_grad, expand_grad, shortcut_grad = (
        weight_grads
    )
    rest = 1.0 - lead
    return (
        entry_grad.reshape(-1),
        (lead * kernel_grad).reshape(-1),
        (lead * out_grad).reshape(-1),
        (lead * squeeze_grad[:, :SE0]).reshape(-1),
        (lead * expand_grad[:SE0]).reshape(-1),
        shortcut_grad.reshape(-1),
        body_grad.reshape(-1),
        (rest * kernel_grad).reshape(-1),
        (rest * out_grad).reshape(-1),
        (rest * squeeze_grad).reshape(-1),
        (rest * expand_grad).reshape(-1),
    )


def local(
    features,
    crop_side,
    upstream,
    entry_in,
    entry_group,
    entry_out,
    entry_down,
    entry_up,
    shortcut_weight,
    body_in,
    body_group,
    body_out,
    body_down,
    body_up,
    norm_gain,
    norm_shift,
    shortcut_gain,
    shortcut_shift,
):
    leading = lax.axis_index("section") == 0
    lead_value = leading.astype(jnp.float32)
    row_in = features.shape[1]
    row_out = upstream.shape[1]
    gain_half = shortcut_gain.shape[0]
    slot_count = features.shape[0]
    other_features, other_gain, other_shift = shifted(
        (features, shortcut_gain, shortcut_shift), "section", -1
    )
    other_upstream = shifted(upstream, "section", 1)
    whole_features = jnp.concatenate([features, other_features], 1).reshape(slot_count, IN, IN, DIN)
    whole_upstream = jnp.concatenate([other_upstream, upstream], 1).reshape(slot_count, OUT, OUT, D)
    short_gain = jnp.concatenate([shortcut_gain, other_gain], 0).astype(jnp.float32)
    short_shift = jnp.concatenate([shortcut_shift, other_shift], 0).astype(jnp.float32)
    gathered = (
        lax.all_gather(entry_in, ("section", "dp"), axis=0, tiled=True),
        lax.all_gather(entry_group, ("section", "dp"), axis=0, tiled=True),
        lax.all_gather(entry_out, ("section", "dp"), axis=0, tiled=True),
        lax.all_gather(entry_down, ("section", "dp"), axis=0, tiled=True),
        lax.all_gather(entry_up, ("section", "dp"), axis=0, tiled=True),
        lax.all_gather(shortcut_weight, ("section", "dp"), axis=0, tiled=True),
        lax.all_gather(body_in, ("section", "dp"), axis=0, tiled=True),
        lax.all_gather(body_group, ("section", "dp"), axis=0, tiled=True),
        lax.all_gather(body_out, ("section", "dp"), axis=0, tiled=True),
        lax.all_gather(body_down, ("section", "dp"), axis=0, tiled=True),
        lax.all_gather(body_up, ("section", "dp"), axis=0, tiled=True),
    )
    first_in = gathered[0].reshape(DIN, D)
    kernel = jnp.where(leading, gathered[1], gathered[7]).reshape(9, GW, D)
    weight_out = jnp.where(leading, gathered[2], gathered[8]).reshape(D, D)
    entry_squeeze = jnp.pad(
        gathered[3].reshape(D, SE0).astype(jnp.float32), ((0, 0), (0, SE1 - SE0))
    )
    entry_expand = jnp.pad(
        gathered[4].reshape(SE0, D).astype(jnp.float32), ((0, SE1 - SE0), (0, 0))
    )
    squeeze = jnp.where(leading, entry_squeeze, gathered[9].reshape(D, SE1).astype(jnp.float32))
    expand = jnp.where(leading, entry_expand, gathered[10].reshape(SE1, D).astype(jnp.float32))
    shortcut_full = gathered[5].reshape(DIN, D)
    last_in = gathered[6].reshape(D, D)
    weights = (first_in, last_in, kernel, weight_out, squeeze, expand, shortcut_full)
    norm_set = (norm_gain[0], norm_shift[0], short_gain, short_shift)
    side_in = jnp.arange(IN, dtype=jnp.int32)
    boundary = crop_side[:, None, None]
    mask_in = ((side_in[None, :, None] < boundary) & (side_in[None, None, :] < boundary)).astype(
        jnp.float32
    )[..., None]
    half_side = crop_side // 2
    side_out = jnp.arange(OUT, dtype=jnp.int32)
    half_bound = half_side[:, None, None]
    mask_out = (
        (side_out[None, :, None] < half_bound) & (side_out[None, None, :] < half_bound)
    ).astype(jnp.float32)[..., None]
    crop_count = (half_side * half_side).astype(jnp.float32)

    def tick_inputs(moment):
        use_first = jnp.logical_and(leading, moment < MICRO)
        first_start = min(moment, MICRO - 1) * CROP_MB
        last_start = max(moment - 1, 0) * CROP_MB
        offset = jnp.where(leading, first_start, last_start).astype(jnp.int32)
        inside = lax.dynamic_slice_in_dim(mask_in, offset, CROP_MB, 0)
        outside = lax.dynamic_slice_in_dim(mask_out, offset, CROP_MB, 0)
        counts = lax.dynamic_slice_in_dim(crop_count, offset, CROP_MB, 0)
        mask_wide = jnp.where(use_first, inside, widen(outside))
        first_part = whole_features[first_start : first_start + CROP_MB]
        return (use_first, offset, first_part, mask_wide, outside, counts)

    hand_on = jnp.zeros((CROP_MB, OUT, OUT, D), jnp.bfloat16)
    record = []
    results = []
    for moment in range(MICRO + 1):
        use_first, offset, first_part, mask_wide, outside, counts = tick_inputs(moment)
        if moment == 0:
            last_part = jnp.zeros((CROP_MB, OUT, OUT, D), jnp.bfloat16)
        else:
            last_part = shifted(hand_on, "section", 1)
        output, statistics, kept_values = section_forward(
            use_first, first_part, last_part, mask_wide, outside, counts, weights, norm_set, None
        )
        hand_on = output.astype(jnp.bfloat16)
        stored = None
        record.append((last_part, statistics, stored))
        results.append(hand_on)
    flat_sizes = (
        DIN * D,
        9 * GW * D,
        D * D,
        D * SE0,
        SE0 * D,
        DIN * D,
        D * D,
        9 * GW * D,
        D * D,
        D * SE1,
        SE1 * D,
    )
    weight_totals = tuple((jnp.zeros((length,), jnp.float32) for length in flat_sizes))
    norm_totals = (
        jnp.zeros((3, D), jnp.float32),
        jnp.zeros((3, D), jnp.float32),
        jnp.zeros((D,), jnp.float32),
        jnp.zeros((D,), jnp.float32),
    )
    source_grads = [None] * MICRO
    grad_hand = jnp.zeros((CROP_MB, OUT, OUT, D), jnp.bfloat16)
    for section_step in range(MICRO + 1):
        moment = MICRO - section_step
        use_first, offset, first_part, mask_wide, outside, counts = tick_inputs(moment)
        last_part, statistics, stored = record[moment]
        if section_step == 0:
            arrived = jnp.zeros((CROP_MB, OUT, OUT, D), jnp.bfloat16)
        else:
            arrived = shifted(grad_hand, "section", -1)
        up_part = lax.dynamic_slice_in_dim(whole_upstream, offset, CROP_MB, 0)
        grad_output = jnp.where(leading, arrived, up_part).astype(jnp.float32)
        unused_output, unused_stats, kept_values = section_forward(
            use_first,
            first_part,
            last_part,
            mask_wide,
            outside,
            counts,
            weights,
            norm_set,
            statistics,
        )
        grad_first, grad_last, weight_grads, norm_grads = section_backward(
            use_first,
            first_part,
            last_part,
            mask_wide,
            outside,
            counts,
            weights,
            norm_set,
            statistics,
            kept_values,
            grad_output,
        )
        useful = jnp.where(leading, moment < MICRO, moment >= 1).astype(jnp.float32)
        scaled = tuple((useful * gradient for gradient in spread_grads(weight_grads, lead_value)))
        weight_totals = tuple((running + addend for running, addend in zip(weight_totals, scaled)))
        norm_totals = tuple(
            (running + useful * addend for running, addend in zip(norm_totals, norm_grads))
        )
        grad_hand = grad_last.astype(jnp.bfloat16)
        if moment < MICRO:
            source_grads[moment] = grad_first.astype(jnp.bfloat16)
    shards = (
        lax.psum_scatter(weight_totals[0], ("section", "dp"), scatter_dimension=0, tiled=True),
        lax.psum_scatter(weight_totals[1], ("section", "dp"), scatter_dimension=0, tiled=True),
        lax.psum_scatter(weight_totals[2], ("section", "dp"), scatter_dimension=0, tiled=True),
        lax.psum_scatter(weight_totals[3], ("section", "dp"), scatter_dimension=0, tiled=True),
        lax.psum_scatter(weight_totals[4], ("section", "dp"), scatter_dimension=0, tiled=True),
        lax.psum_scatter(weight_totals[5], ("section", "dp"), scatter_dimension=0, tiled=True),
        lax.psum_scatter(weight_totals[6], ("section", "dp"), scatter_dimension=0, tiled=True),
        lax.psum_scatter(weight_totals[7], ("section", "dp"), scatter_dimension=0, tiled=True),
        lax.psum_scatter(weight_totals[8], ("section", "dp"), scatter_dimension=0, tiled=True),
        lax.psum_scatter(weight_totals[9], ("section", "dp"), scatter_dimension=0, tiled=True),
        lax.psum_scatter(weight_totals[10], ("section", "dp"), scatter_dimension=0, tiled=True),
    )
    source_whole = jnp.concatenate(source_grads, 0).reshape(slot_count, IN, IN * DIN)
    sent_grad = shifted(source_whole[:, row_in:], "section", 1)
    sent_gain, sent_shift = shifted(
        (norm_totals[2][gain_half:], norm_totals[3][gain_half:]), "section", 1
    )
    grad_features = jnp.where(leading, source_whole[:, :row_in], sent_grad)
    output_whole = jnp.concatenate(results[1:], 0).reshape(slot_count, OUT, OUT * D)
    sent_output = shifted(output_whole[:, :row_out], "section", -1)
    output = jnp.where(leading, sent_output, output_whole[:, row_out:])
    grad_short_gain = jnp.where(leading, norm_totals[2][:gain_half], sent_gain)
    grad_short_shift = jnp.where(leading, norm_totals[3][:gain_half], sent_shift)
    return (
        output,
        grad_features,
        shards[0],
        shards[1],
        shards[2],
        shards[3],
        shards[4],
        shards[5],
        shards[6],
        shards[7],
        shards[8],
        shards[9],
        shards[10],
        norm_totals[0][None],
        norm_totals[1][None],
        grad_short_gain,
        grad_short_shift,
    )


def solution(mesh):
    in_specs = (
        P("dp", "section", None),
        P("dp"),
        P("dp", "section", None),
        P(("section", "dp")),
        P(("section", "dp")),
        P(("section", "dp")),
        P(("section", "dp")),
        P(("section", "dp")),
        P(("section", "dp")),
        P(("section", "dp")),
        P(("section", "dp")),
        P(("section", "dp")),
        P(("section", "dp")),
        P(("section", "dp")),
        P("section", None, None),
        P("section", None, None),
        P("section"),
        P("section"),
    )
    out_specs = (
        P("dp", "section", None),
        P("dp", "section", None),
        P(("section", "dp")),
        P(("section", "dp")),
        P(("section", "dp")),
        P(("section", "dp")),
        P(("section", "dp")),
        P(("section", "dp")),
        P(("section", "dp")),
        P(("section", "dp")),
        P(("section", "dp")),
        P(("section", "dp")),
        P(("section", "dp")),
        P("section", None, None),
        P("section", None, None),
        P("section"),
        P("section"),
    )
    return jax.shard_map(local, mesh=mesh, in_specs=in_specs, out_specs=out_specs, check_vma=False)
```

profile of v0, /device:TPU:0, one launch (start us, length us, event | category | flops | bytes accessed | tf_op | source)
XLA Modules:
  0.0 5196.7 jit_solution(392561825674974474)
XLA Ops:
  29.0 79.3 %all-gather.6 = bf16[32,1,12544]{2,1,0:T(2,128)(2,1)S(1)} all-gather(bf16[1,1,12544]{2,1,0:T(2,128)(2,1)S(1)} %reshape.6236), channel_id=1, replica_groups=mesh['section'=2,'dp'=16] {'section','dp'}, dimensions={0}, use_global_device_ids=true | all-gather | bytes 827904 | tf_op jit(solution)/shard_map/all_gather | solution.py:420
  108.4 82.3 %all-gather.1 = bf16[32,1,12544]{2,1,0:T(2,128)(2,1)S(1)} all-gather(bf16[1,1,12544]{2,1,0:T(2,128)(2,1)S(1)} %reshape.6226), channel_id=1, replica_groups=mesh['section'=2,'dp'=16] {'section','dp'}, dimensions={0}, use_global_device_ids=true | all-gather | bytes 827904 | tf_op jit(solution)/shard_map/all_gather | solution.py:415
  190.8 70.2 %all-gather.2 = bf16[32,1,6272]{2,1,0:T(2,128)(2,1)S(1)} all-gather(bf16[1,1,6272]{2,1,0:T(2,128)(2,1)S(1)} %reshape.6228), channel_id=1, replica_groups=mesh['section'=2,'dp'=16] {'section','dp'}, dimensions={0}, use_global_device_ids=true | all-gather | bytes 413952 | tf_op jit(solution)/shard_map/all_gather | solution.py:424
  264.1 72.5 %all-gather.3 = bf16[32,1,6272]{2,1,0:T(2,128)(2,1)S(1)} all-gather(bf16[1,1,6272]{2,1,0:T(2,128)(2,1)S(1)} %reshape.6230), channel_id=1, replica_groups=mesh['section'=2,'dp'=16] {'section','dp'}, dimensions={0}, use_global_device_ids=true | all-gather | bytes 413952 | tf_op jit(solution)/shard_map/all_gather | solution.py:425
  431.8 42.8 all-reduce.59
  480.8 168.2 %conditional.25 = (f32[1,14,14,896]{3,2,1,0:T(8,128)}) conditional(s32[]{:T(128)} %convert_element_type.369, (bf16[1,28,28,896]{3,2,1,0:T(8,128)(2,1)S(1)}, bf16[451584]{0:T(1024)(128)(2,1)S(1)}) %tuple.400, (bf16[1,28,28,896]{3,2,1,0:T(8,128)(2,1)S(1)}, bf16[451584]{0:T(1024)(128)(2,1)S(1)}) %tuple.400), branch_computations={%region_7.8_spmd, %region_8.9_spmd} | conditional | flops 177020928 | bytes 39517192 | solution.py:163
  744.0 73.7 %psum.248 = f32[4,896]{1,0:T(4,128)} all-reduce(f32[4,896]{1,0:T(4,128)} %pad_maximum_fusion.2), channel_id=1, replica_groups=mesh['section'=2,'dp'=16] {'dp'}, use_global_device_ids=true, to_apply=%region_19.20 | all-reduce | flops 3584 | bytes 28672 | tf_op jit(solution)/shard_map/psum | solution.py:55
  901.1 168.4 %conditional.28 = (f32[1,14,14,896]{3,2,1,0:T(8,128)}) conditional(s32[]{:T(128)} %convert_element_type.369, (bf16[1,28,28,896]{3,2,1,0:T(8,128)(2,1)S(1)}, bf16[451584]{0:T(1024)(128)(2,1)S(1)}) %tuple.405, (bf16[1,28,28,896]{3,2,1,0:T(8,128)(2,1)S(1)}, bf16[451584]{0:T(1024)(128)(2,1)S(1)}) %tuple.405), branch_computations={%region_27.28_spmd, %region_28.29_spmd} | conditional | flops 177020928 | bytes 39517192 | solution.py:163
  1071.3 39.1 psum.251
  1123.9 71.8 %psum.252 = f32[4,896]{1,0:T(4,128)} all-reduce(f32[4,896]{1,0:T(4,128)S(1)} %pad_maximum_fusion.3), channel_id=1, replica_groups=mesh['section'=2,'dp'=16] {'dp'}, use_global_device_ids=true, to_apply=%region_39.40 | all-reduce | flops 3584 | bytes 28672 | tf_op jit(solution)/shard_map/psum | solution.py:55
  1269.1 168.1 %conditional.31 = (f32[1,14,14,896]{3,2,1,0:T(8,128)}) conditional(s32[]{:T(128)} %convert_element_type.369, (bf16[1,28,28,896]{3,2,1,0:T(8,128)(2,1)S(1)}, bf16[451584]{0:T(1024)(128)(2,1)S(1)}) %tuple.410, (bf16[1,28,28,896]{3,2,1,0:T(8,128)(2,1)S(1)}, bf16[451584]{0:T(1024)(128)(2,1)S(1)}) %tuple.410), branch_computations={%region_47.48_spmd, %region_48.49_spmd} | conditional | flops 177020928 | bytes 39517192 | solution.py:163
  1439.0 39.0 psum.255
  1490.5 71.8 %psum.256 = f32[4,896]{1,0:T(4,128)S(1)} all-reduce(f32[4,896]{1,0:T(4,128)S(1)} %pad_maximum_fusion.4), channel_id=1, replica_groups=mesh['section'=2,'dp'=16] {'dp'}, use_global_device_ids=true, to_apply=%region_59.60 | all-reduce | flops 3584 | bytes 28672 | tf_op jit(solution)/shard_map/psum | solution.py:55
  1634.6 168.5 %conditional.34 = (f32[1,14,14,896]{3,2,1,0:T(8,128)}) conditional(s32[]{:T(128)} %convert_element_type.369, (bf16[1,28,28,896]{3,2,1,0:T(8,128)(2,1)S(1)}, bf16[451584]{0:T(1024)(128)(2,1)S(1)}) %tuple.415, (bf16[1,28,28,896]{3,2,1,0:T(8,128)(2,1)S(1)}, bf16[451584]{0:T(1024)(128)(2,1)S(1)}) %tuple.415), branch_computations={%region_67.68_spmd, %region_68.69_spmd} | conditional | flops 177020928 | bytes 39517192 | solution.py:163
  1856.2 71.8 %psum.260 = f32[4,896]{1,0:T(4,128)S(1)} all-reduce(f32[4,896]{1,0:T(4,128)S(1)} %pad_maximum_fusion.5), channel_id=1, replica_groups=mesh['section'=2,'dp'=16] {'dp'}, use_global_device_ids=true, to_apply=%region_79.80 | all-reduce | flops 3584 | bytes 28672 | tf_op jit(solution)/shard_map/psum | solution.py:55
  2120.8 39.8 psum.263
  2184.4 71.8 %psum.264 = f32[4,896]{1,0:T(4,128)} all-reduce(f32[4,896]{1,0:T(4,128)} %pad_maximum_fusion.6), channel_id=1, replica_groups=mesh['section'=2,'dp'=16] {'dp'}, use_global_device_ids=true, to_apply=%region_93.94 | all-reduce | flops 3584 | bytes 28672 | tf_op jit(solution)/shard_map/psum | solution.py:55
  2267.4 71.8 %psum.265 = f32[3,896]{1,0:T(4,128)} all-reduce(f32[3,896]{1,0:T(4,128)} %pad_maximum_fusion.7), channel_id=1, replica_groups=mesh['section'=2,'dp'=16] {'dp'}, use_global_device_ids=true, to_apply=%region_97.98 | all-reduce | flops 2688 | bytes 21504 | tf_op jit(solution)/shard_map/psum | solution.py:59
  2568.6 39.7 psum.267
  2664.0 72.3 %psum.268 = f32[3,896]{1,0:T(4,128)S(1)} all-reduce(f32[3,896]{1,0:T(4,128)S(1)} %pad_maximum_fusion.8), channel_id=1, replica_groups=mesh['section'=2,'dp'=16] {'dp'}, use_global_device_ids=true, to_apply=%region_111.112 | all-reduce | flops 2688 | bytes 21504 | tf_op jit(solution)/shard_map/psum | solution.py:59
  2789.3 314.9 %conditional.37 = (f32[1,28,28,896]{3,2,1,0:T(8,128)S(1)}, f32[9,56,896]{2,1,0:T(8,128)}) conditional(s32[]{:T(128)} %convert_element_type.369, (bf16[451584]{0:T(1024)(128)(2,1)S(1)}, bf16[1,14,14,896]{3,2,1,0:T(8,128)(2,1)S(1)}, bf16[1,28,28,896]{3,2,1,0:T(8,128)(2,1)}) %tuple.979, (bf16[451584]{0:T(1024)(128)(2,1)S(1)}, ...), branch_computations={%region_116.118_spmd, %region_118.128_spmd} | conditional | flops 355628096 | bytes 131862904 | solution.py:301
  3108.8 39.1 psum.270
  3198.3 72.2 %psum.271 = f32[3,896]{1,0:T(4,128)S(1)} all-reduce(f32[3,896]{1,0:T(4,128)S(1)} %pad_maximum_fusion.9), channel_id=1, replica_groups=mesh['section'=2,'dp'=16] {'dp'}, use_global_device_ids=true, to_apply=%region_139.140 | all-reduce | flops 2688 | bytes 21504 | tf_op jit(solution)/shard_map/psum | solution.py:59
  3322.5 314.7 %conditional.40 = (f32[1,28,28,896]{3,2,1,0:T(8,128)S(1)}, f32[9,56,896]{2,1,0:T(8,128)}) conditional(s32[]{:T(128)} %convert_element_type.369, (bf16[451584]{0:T(1024)(128)(2,1)S(1)}, bf16[1,14,14,896]{3,2,1,0:T(8,128)(2,1)S(1)}, bf16[1,28,28,896]{3,2,1,0:T(8,128)(2,1)}) %tuple.977, (bf16[451584]{0:T(1024)(128)(2,1)S(1)}, ...), branch_computations={%region_144.146_spmd, %region_146.156_spmd} | conditional | flops 355628096 | bytes 131862904 | solution.py:301
  3641.8 39.0 psum.273
  3731.6 72.2 %psum.274 = f32[3,896]{1,0:T(4,128)S(1)} all-reduce(f32[3,896]{1,0:T(4,128)S(1)} %pad_maximum_fusion.10), channel_id=1, replica_groups=mesh['section'=2,'dp'=16] {'dp'}, use_global_device_ids=true, to_apply=%region_167.168 | all-reduce | flops 2688 | bytes 21504 | tf_op jit(solution)/shard_map/psum | solution.py:59
  3855.7 315.5 %conditional.43 = (f32[1,28,28,896]{3,2,1,0:T(8,128)S(1)}, f32[9,56,896]{2,1,0:T(8,128)}) conditional(s32[]{:T(128)} %convert_element_type.369, (bf16[451584]{0:T(1024)(128)(2,1)S(1)}, bf16[1,14,14,896]{3,2,1,0:T(8,128)(2,1)S(1)}, bf16[1,28,28,896]{3,2,1,0:T(8,128)(2,1)}) %tuple.975, (bf16[451584]{0:T(1024)(128)(2,1)S(1)}, ...), branch_computations={%region_172.174_spmd, %region_174.184_spmd} | conditional | flops 355628096 | bytes 131862904 | solution.py:301
  4175.8 39.0 psum.276
  4265.4 72.2 %psum.277 = f32[3,896]{1,0:T(4,128)S(1)} all-reduce(f32[3,896]{1,0:T(4,128)S(1)} %pad_maximum_fusion.11), channel_id=1, replica_groups=mesh['section'=2,'dp'=16] {'dp'}, use_global_device_ids=true, to_apply=%region_195.196 | all-reduce | flops 2688 | bytes 21504 | tf_op jit(solution)/shard_map/psum | solution.py:59
  4390.9 315.3 %conditional.46 = (f32[1,28,28,896]{3,2,1,0:T(8,128)S(1)}, f32[9,56,896]{2,1,0:T(8,128)}) conditional(s32[]{:T(128)} %convert_element_type.369, (bf16[451584]{0:T(1024)(128)(2,1)S(1)}, bf16[1,14,14,896]{3,2,1,0:T(8,128)(2,1)S(1)}, bf16[1,28,28,896]{3,2,1,0:T(8,128)(2,1)}) %tuple.973, (bf16[451584]{0:T(1024)(128)(2,1)S(1)}, ...), branch_computations={%region_200.202_spmd, %region_202.212_spmd} | conditional | flops 355628096 | bytes 131862904 | solution.py:301
  4710.8 39.0 psum.279
  4873.1 300.2 %all-reduce.64.cloned.1.call-done = (f32[401408]{0:T(1024)}, f32[451584]{0:T(1024)}, f32[802816]{0:T(1024)}, f32[100352]{0:T(1024)}, f32[100352]{0:T(1024)}, /*i...) async-done(((f32[401408]{0:T(1024)}, f32[451584]{0:T(1024)}, f32[802816]{0:T(1024)}, ...) | async-done | bytes 18866192
  (1954 shorter events, 3645.7 us)
Async XLA Ops:
  7.2 359.6 %all-reduce.66.cloned.1.call-start = ((), (), s32[]{:S(2)}) async-start(), calls=%async_computation.4 | async-start | bytes 4415488
  12.4 395.0 %all-gather.11.cloned.1.call-start = ((), (), s32[]{:S(2)}) async-start(), calls=%async_computation | async-start | bytes 3311616 | tf_op jit(solution)/shard_map/all_gather | solution.py:421
  13.2 682.9 %all-gather.13.cloned.1.call-start = ((), (), s32[]{:S(2)}) async-start(), calls=%async_computation.1 | async-start | bytes 3311616 | tf_op jit(solution)/shard_map/all_gather | solution.py:417
  14.0 682.2 %all-gather.15.cloned.1.call-start = ((), (), s32[]{:S(2)}) async-start(), calls=%async_computation.2 | async-start | bytes 3311616 | tf_op jit(solution)/shard_map/all_gather | solution.py:423
  14.1 359.6 %collective-permute-start = (bf16[4,14,12544]{2,0,1:T(4,128)(2,1)}, bf16[4,14,12544]{2,0,1:T(4,128)(2,1)}, u32[]{:S(2)}, u32[]{:S(2)}) collective-permute-start(bf16[4,14,12544]{2,0,1:T(4,128)(2,1)} %param.156), channel_id=1, source_target_pairs={{16,0},{17,1},{18,2},{19,3},{20,4},{21,5},{22,6},{23,7},{24,8},{25... | collective-permute-start | bytes 4214792 | tf_op jit(solution)/shard_map/ppermute | solution.py:25
  15.4 349.2 %collective-permute-start.2 = (bf16[448]{0:T(512)(128)(2,1)}, bf16[448]{0:T(512)(128)(2,1)}, u32[]{:S(2)}, u32[]{:S(2)}) collective-permute-start(bf16[448]{0:T(512)(128)(2,1)} %param.173), channel_id=1, source_target_pairs={{16,0},{17,1},{18,2},{19,3},{20,4},{21,5},{22,6},{23,7},{24,8},{25... | collective-permute-start | bytes 2696 | tf_op jit(solution)/shard_map/ppermute | solution.py:25
  16.7 348.8 %collective-permute-start.1 = (bf16[448]{0:T(512)(128)(2,1)}, bf16[448]{0:T(512)(128)(2,1)}, u32[]{:S(2)}, u32[]{:S(2)}) collective-permute-start(bf16[448]{0:T(512)(128)(2,1)} %param.172), channel_id=1, source_target_pairs={{16,0},{17,1},{18,2},{19,3},{20,4},{21,5},{22,6},{23,7},{24,8},{25... | collective-permute-start | bytes 2696 | tf_op jit(solution)/shard_map/ppermute | solution.py:25
  18.0 1185.3 %collective-permute-start.8 = (bf16[4,7,12544]{2,0,1:T(4,128)(2,1)}, bf16[4,7,12544]{2,0,1:T(4,128)(2,1)}, u32[]{:S(2)}, u32[]{:S(2)}) collective-permute-start(bf16[4,7,12544]{2,0,1:T(4,128)(2,1)} %param.158), channel_id=1, source_target_pairs={{0,16},{1,17},{2,18},{3,19},{4,20},{5,21},{6,22},{7,23},{8,24},{9,... | collective-permute-start | bytes 2107400 | tf_op jit(solution)/shard_map/ppermute | solution.py:25
  24.8 5148.5 %all-reduce.64.cloned.1.call-start = ((), (), s32[]{:S(2)}) async-start(), calls=%async_computation.3 | async-start | bytes 37732352
  339.8 1590.2 %copy-start.183 = (f32[896]{0:T(1024)}, f32[896]{0:T(1024)S(1)}, u32[]{:S(2)}) copy-start(f32[896]{0:T(1024)S(1)} %get-tuple-element.1219) | copy-start | bytes 10756
  339.8 1714.2 %copy-start.173 = (f32[896]{0:T(1024)}, f32[896]{0:T(1024)S(1)}, u32[]{:S(2)}) copy-start(f32[896]{0:T(1024)S(1)} %get-tuple-element.1220) | copy-start | bytes 10756
  339.8 2321.1 %copy-start.159 = (f32[896]{0:T(1024)}, f32[896]{0:T(1024)S(1)}, u32[]{:S(2)}) copy-start(f32[896]{0:T(1024)S(1)} %get-tuple-element.1730) | copy-start | bytes 10756
  339.8 2410.9 %copy-start.155 = (f32[896]{0:T(1024)}, f32[896]{0:T(1024)S(1)}, u32[]{:S(2)}) copy-start(f32[896]{0:T(1024)S(1)} %get-tuple-element.1728) | copy-start | bytes 10756
  339.8 2764.4 %copy-start.151 = (f32[896]{0:T(1024)}, f32[896]{0:T(1024)S(1)}, u32[]{:S(2)}) copy-start(f32[896]{0:T(1024)S(1)} %get-tuple-element.1729) | copy-start | bytes 10756
  341.1 1588.9 %copy-start.167 = (f32[1,14,14]{2,1,0:T(8,128)}, f32[1,14,14]{2,1,0:T(8,128)S(1)}, u32[]{:S(2)}) copy-start(f32[1,14,14]{2,1,0:T(8,128)S(1)} %get-tuple-element.1602) | copy-start | bytes 2356
  350.7 1635.7 %copy-start.4 = (bf16[448,896]{1,0:T(8,128)(2,1)}, bf16[448,896]{1,0:T(8,128)(2,1)S(1)}, u32[]{:S(2)}) copy-start(bf16[448,896]{1,0:T(8,128)(2,1)S(1)} %reshape.5631) | copy-start | bytes 2408452
  365.4 1564.6 %copy-start.196 = (f32[896]{0:T(1024)}, f32[896]{0:T(1024)S(1)}, u32[]{:S(2)}) copy-start(f32[896]{0:T(1024)S(1)} %maximum_convert_fusion) | copy-start | bytes 10756
  368.1 2421.2 %copy-start = (bf16[451584]{0:T(1024)(128)(2,1)}, bf16[451584]{0:T(1024)(128)(2,1)S(1)}, u32[]{:S(2)}) copy-start(bf16[451584]{0:T(1024)(128)(2,1)S(1)} %broadcast_select_fusion.6) | copy-start | bytes 2709508
  372.3 2375.5 %copy-start.16 = (f32[224,896]{1,0:T(8,128)}, f32[224,896]{1,0:T(8,128)S(1)}, u32[]{:S(2)}) copy-start(f32[224,896]{1,0:T(8,128)S(1)} %convert_select_fusion.7) | copy-start | bytes 2408452
  373.6 2375.1 %copy-start.9 = (f32[896,224]{1,0:T(8,128)}, f32[896,224]{1,0:T(8,128)S(1)}, u32[]{:S(2)}) copy-start(f32[896,224]{1,0:T(8,128)S(1)} %convert_select_fusion.6) | copy-start | bytes 2408452
  823.2 27.7 collective-permute-start.3
  1201.2 17.2 collective-permute-start.4
  1567.0 17.2 collective-permute-start.5
  1932.7 79.5 %collective-permute-start.6 = (bf16[1,14,14,896]{3,2,1,0:T(8,128)(2,1)}, bf16[1,14,14,896]{3,2,1,0:T(8,128)(2,1)}, u32[]{:S(2)}, u32[]{:S(2)}) collective-permute-start(bf16[1,14,14,896]{3,2,1,0:T(8,128)(2,1)} %multiply_convert_fusion.24), channel_id=1, source_target_pairs={{0,16},{1,17},{2,18},{3,19},{4,20},{5,21},{6,22},{7,23},{8,24},{9,... | collective-permute-start | bytes 1053704 | tf_op jit(solution)/shard_map/ppermute | solution.py:25
  2375.8 2487.0 %collective-permute-start.7 = (bf16[4,7,12544]{2,0,1:T(4,128)(2,1)}, bf16[4,7,12544]{2,0,1:T(4,128)(2,1)}, u32[]{:S(2)}, u32[]{:S(2)}) collective-permute-start(bf16[4,7,12544]{2,0,1:T(4,128)(2,1)} %copy.1465), channel_id=1, source_target_pairs={{16,0},{17,1},{18,2},{19,3},{20,4},{21,5},{22,6},{23,7},{24,8},{25... | collective-permute-start | bytes 2107400 | tf_op jit(solution)/shard_map/ppermute | solution.py:25
  2616.3 44.5 collective-permute-start.9
  3183.5 12.5 collective-permute-start.10
  3716.8 12.5 collective-permute-start.11
  4250.5 12.5 collective-permute-start.12
  4861.4 9.3 collective-permute-start.13
  4865.4 4.8 collective-permute-start.14
  4866.8 2.7 collective-permute-start.15
  (382 other events, 17926.9 us)
Sparse Core Ops, SparseCore 0:
  14.7 142.1 all-reduce.65
  160.8 59.3 all-gather.10
  224.1 60.8 all-gather.12
  288.7 58.7 all-gather.14
  4860.0 313.1 all-reduce.63
where the time goes:
time: 5260 us; the launch traced here: 5200 us
  blocking collectives  1800 us (34%)
  local copies, waits for them, and re-layouts  1640 us (31%)
  other arithmetic  1140 us (22%)
  waiting for transfers between devices  300 us (6%)
  matrix products  197 us (4%)
  loops' own time  71.7 us (1%)
    psum x15, blocking collectives, forward_sums(): return lax.psum((local_sums, population), 'dp')  748 us
    psum x15, blocking collectives, backward_sums(): return lax.psum(local_sums, 'dp')  743 us
    scatter-add x36, other arithmetic, grouped_back(): padded = padded.at[:, row_tap:row_tap + extent:stride, col_tap:col_tap +...  737 us
    slice x73, local copies, waits for them, and re-layouts, tap_patches(): padded[:, row_tap:row_tap + extent:stride, col_tap:col_tap + extent:stride]  512 us
    another operation x171, local copies, waits for them, and re-layouts, tap_patches(): return jnp.stack(fragments, 0).reshape(9, -1, GROUPS, GW)  332 us
    unnamed x7, waiting for transfers between devices  300 us
  transfers between devices with their start and end apart: 21, of which 1 were waited for; matrix products, arithmetic and copies ran while one was open for 47% of the time, Pallas kernels for 0%

commit v1 on v0

v1 whole, which is shorter than its diff:
```python
import jax
import jax.numpy as jnp
from jax import lax
from jax.sharding import PartitionSpec as P

D = 896
DIN = 448
GROUPS = 16
GW = 56
SE0 = 112
SE1 = 224
OUT = 14
IN = 28
EPSILON = 1e-05
HIGHEST = lax.Precision.HIGHEST
F32 = jnp.float32
BF16 = jnp.bfloat16


def silu(v):
    return v * jax.nn.sigmoid(v)


def slope(v):
    g = jax.nn.sigmoid(v)
    return g * (1.0 + v * (1.0 - g))


def px_dot(values, weight):
    return jnp.einsum("khwc,cd->khwd", values, weight, preferred_element_type=F32)


def px_back(values, weight):
    return jnp.einsum("khwd,cd->khwc", values, weight, preferred_element_type=F32)


def px_outer(a, b):
    return jnp.einsum("khwc,khwd->cd", a, b, preferred_element_type=F32)


def crop_sums(values):
    return jnp.sum(values, axis=(1, 2))


def moments(sums, count):
    center = sums[:, 0] / count
    scaling = lax.rsqrt(sums[:, 1] / count - center * center + EPSILON)
    return center[:, None, None], scaling[:, None, None]


def conv(x, kernel, stride):
    return lax.conv_general_dilated(
        x,
        kernel,
        (stride, stride),
        ((1, 1), (1, 1)),
        dimension_numbers=("NHWC", "HWIO", "NHWC"),
        feature_group_count=GROUPS,
        preferred_element_type=F32,
    )


def two_sums(values, mask):
    weighted = mask * values
    return jnp.stack([crop_sums(weighted), crop_sums(weighted * values)], 1)


def block_forward(u, weights, gains, shifts, mask_u, mask_out, n_u, n_out, crop_count, stride, short):
    wa, kernel, wc, wd, wu = weights
    inner = px_dot(u, wa)
    sums_a = lax.psum(two_sums(inner, mask_u), "dp")
    center_a, scaling_a = moments(sums_a, n_u)
    hat_a = (inner - center_a) * scaling_a
    activated = (mask_u * silu(hat_a * gains[0] + shifts[0])).astype(BF16)
    convolved = conv(activated, kernel, stride)
    sums_b = lax.psum(two_sums(convolved, mask_out), "dp")
    center_b, scaling_b = moments(sums_b, n_out)
    hat_b = (convolved - center_b) * scaling_b
    excited = mask_out * silu(hat_b * gains[1] + shifts[1])
    pooled = crop_sums(excited) / crop_count
    squeeze_raw = jnp.dot(pooled, wd, precision=HIGHEST)
    squeezed = silu(squeeze_raw)
    gating = jax.nn.sigmoid(jnp.dot(squeezed, wu, precision=HIGHEST))
    gated = (excited * gating[:, None, None]).astype(BF16)
    projected = px_dot(gated, wc)
    sums_c = two_sums(projected, mask_out)
    hat_s = None
    scaling_s = None
    if short is not None:
        weight_s, gain_s, shift_s = short
        strided = px_dot(u[:, ::2, ::2], weight_s)
        sums_c = lax.psum(jnp.concatenate([sums_c, two_sums(strided, mask_out)], 1), "dp")
        center_s, scaling_s = moments(sums_c[:, 2:], n_out)
        hat_s = (strided - center_s) * scaling_s
        residual = hat_s * gain_s + shift_s
    else:
        sums_c = lax.psum(sums_c, "dp")
        residual = u.astype(F32)
    center_c, scaling_c = moments(sums_c[:, :2], n_out)
    hat_c = (projected - center_c) * scaling_c
    summed = hat_c * gains[2] + shifts[2] + residual
    output = (mask_out * silu(summed)).astype(BF16)
    kept = (
        hat_a, scaling_a, activated, hat_b, scaling_b, excited, pooled, squeeze_raw, squeezed,
        gating, gated, hat_c, scaling_c, hat_s, scaling_s, summed,
    )
    return output, kept


def norm_back(dz, hat, scaling, gain, totals, n, mask):
    mean_dz = (totals[:, 0] / n)[:, None, None]
    mean_hat = (totals[:, 1] / n)[:, None, None]
    return (mask * gain * scaling * (dz - mean_dz - hat * mean_hat)).astype(BF16)


def block_backward(
    d_out, u, weights, gains, shifts, mask_u, mask_out, n_u, n_out, crop_count, stride, short, kept
):
    wa, kernel, wc, wd, wu = weights
    (
        hat_a, scaling_a, activated, hat_b, scaling_b, excited, pooled, squeeze_raw, squeezed,
        gating, gated, hat_c, scaling_c, hat_s, scaling_s, summed,
    ) = kept
    d_pre = d_out * mask_out * slope(summed)
    terms = [crop_sums(d_pre), crop_sums(d_pre * hat_c)]
    if short is not None:
        terms.append(crop_sums(d_pre * hat_s))
    tot_c = lax.psum(jnp.stack(terms, 1), "dp")
    d_proj = norm_back(d_pre, hat_c, scaling_c, gains[2], tot_c, n_out, mask_out)
    g_wc = px_outer(gated, d_proj)
    d_gated = px_back(d_proj, wc)
    d_gate = crop_sums(d_gated * excited)
    d_gate_raw = d_gate * gating * (1.0 - gating)
    g_wu = jnp.dot(squeezed.T, d_gate_raw, precision=HIGHEST)
    d_sq = jnp.dot(d_gate_raw, wu.T, precision=HIGHEST) * slope(squeeze_raw)
    g_wd = jnp.dot(pooled.T, d_sq, precision=HIGHEST)
    d_pool = jnp.dot(d_sq, wd.T, precision=HIGHEST) / crop_count
    d_exc = d_gated * gating[:, None, None] + d_pool[:, None, None]
    dz_b = d_exc * mask_out * slope(hat_b * gains[1] + shifts[1])
    tot_b = lax.psum(jnp.stack([crop_sums(dz_b), crop_sums(dz_b * hat_b)], 1), "dp")
    d_conv = norm_back(dz_b, hat_b, scaling_b, gains[1], tot_b, n_out, mask_out)
    back = jax.vjp(
        lambda x, k: conv(x, k, stride), activated.astype(F32), kernel.astype(F32)
    )[1]
    d_act, g_k = back(d_conv.astype(F32))
    dz_a = d_act * mask_u * slope(hat_a * gains[0] + shifts[0])
    tot_a = lax.psum(jnp.stack([crop_sums(dz_a), crop_sums(dz_a * hat_a)], 1), "dp")
    d_inner = norm_back(dz_a, hat_a, scaling_a, gains[0], tot_a, n_u, mask_u)
    g_wa = px_outer(u, d_inner)
    d_u = px_back(d_inner, wa)
    g_ws = None
    if short is not None:
        weight_s, gain_s, shift_s = short
        tot_s = jnp.stack([tot_c[:, 0], tot_c[:, 2]], 1)
        d_strided = norm_back(d_pre, hat_s, scaling_s, gain_s, tot_s, n_out, mask_out)
        g_ws = px_outer(u[:, ::2, ::2], d_strided)
        d_u = d_u.at[:, ::2, ::2].add(px_back(d_strided, weight_s))
    else:
        d_u = d_u + d_pre
    return d_u.astype(BF16), (g_wa, g_k, g_wc, g_wd, g_wu, g_ws), (tot_a, tot_b, tot_c)


def local(
    features, crop_side, upstream,
    entry_in, entry_group, entry_out, entry_down, entry_up, shortcut_weight,
    body_in, body_group, body_out, body_down, body_up,
    norm_gain, norm_shift, shortcut_gain, shortcut_shift,
):
    section = lax.axis_index("section")
    first = section == 0
    slots = features.shape[0]
    half = slots // 2
    swap = [(0, 1), (1, 0)]

    def halves_in(rows):
        sent = lax.dynamic_slice_in_dim(rows, (1 - section) * half, half, 0)
        kept = lax.dynamic_slice_in_dim(rows, section * half, half, 0)
        got = lax.ppermute(sent, "section", swap)
        return jnp.where(
            first, jnp.concatenate([kept, got], 1), jnp.concatenate([got, kept], 1)
        )

    def halves_out(whole):
        rows = whole.shape[1] // 2
        top, low = whole[:, :rows], whole[:, rows:]
        got = lax.ppermute(jnp.where(first, low, top), "section", swap)
        kept = jnp.where(first, top, low)
        return jnp.where(
            first, jnp.concatenate([kept, got], 0), jnp.concatenate([got, kept], 0)
        )

    u = halves_in(features).reshape(half, IN, IN, DIN)
    d_out = halves_in(upstream).reshape(half, OUT, OUT, D).astype(F32)
    shards = (
        entry_in, entry_group, entry_out, entry_down, entry_up, shortcut_weight,
        body_in, body_group, body_out, body_down, body_up,
    )
    shapes = (
        (DIN, D), (3, 3, GW, D), (D, D), (D, SE0), (SE0, D), (DIN, D),
        (D, D), (3, 3, GW, D), (D, D), (D, SE1), (SE1, D),
    )
    together = lax.all_gather(jnp.concatenate(shards), ("section", "dp"), axis=0, tiled=False)
    weights = []
    start = 0
    for shard, shape in zip(shards, shapes):
        weights.append(together[:, start : start + shard.shape[0]].reshape(shape))
        start += shard.shape[0]
    (w_in, w_group, w_out, w_down, w_up, w_short, b_in, b_group, b_out, b_down, b_up) = weights
    entry = (w_in, w_group, w_out, w_down.astype(F32), w_up.astype(F32))
    body = (b_in, b_group, b_out, b_down.astype(F32), b_up.astype(F32))
    gains, shifts, short_gain, short_shift = (
        lax.all_gather(part, "section", axis=0, tiled=True)
        for part in (norm_gain, norm_shift, shortcut_gain, shortcut_shift)
    )
    short = (w_short, short_gain.astype(F32), short_shift.astype(F32))
    side = lax.dynamic_slice_in_dim(crop_side, section * half, half, 0)

    def grid_mask(extent, bound):
        at = jnp.arange(extent, dtype=jnp.int32)
        inside = at[None] < bound[:, None]
        return (inside[:, :, None] & inside[:, None, :]).astype(F32)[..., None]

    mask_in = grid_mask(IN, side)
    mask_out = grid_mask(OUT, side // 2)
    crop_count = ((side // 2) * (side // 2)).astype(F32)[:, None]
    n_out = lax.psum(crop_count, "dp")
    n_in = n_out * 4.0

    hidden, kept0 = block_forward(
        u, entry, gains[0], shifts[0], mask_in, mask_out, n_in, n_out, crop_count, 2, short
    )
    output, kept1 = block_forward(
        hidden, body, gains[1], shifts[1], mask_out, mask_out, n_out, n_out, crop_count, 1, None
    )
    d_hidden, grads1, totals1 = block_backward(
        d_out, hidden, body, gains[1], shifts[1], mask_out, mask_out, n_out, n_out, crop_count, 1,
        None, kept1,
    )
    d_features, grads0, totals0 = block_backward(
        d_hidden.astype(F32), u, entry, gains[0], shifts[0], mask_in, mask_out, n_in, n_out,
        crop_count, 2, short, kept0,
    )
    order = (
        grads0[0], grads0[1], grads0[2], grads0[3], grads0[4], grads0[5],
        grads1[0], grads1[1], grads1[2], grads1[3], grads1[4],
    )
    devices = lax.axis_size("section") * lax.axis_size("dp")
    packed = jnp.concatenate([grad.reshape(devices, -1) for grad in order], 1)
    summed = lax.psum_scatter(packed, ("section", "dp"), scatter_dimension=0, tiled=False)
    weight_out = []
    start = 0
    for shard in shards:
        weight_out.append(summed[start : start + shard.shape[0]])
        start += shard.shape[0]

    norms = [
        jnp.stack(
            [
                jnp.stack([jnp.sum(totals[at][:, kind], 0) for at in range(3)])
                for totals in (totals0, totals1)
            ]
        )
        for kind in (1, 0)
    ]
    short_grads = jnp.stack([jnp.sum(totals0[2][:, 2], 0), jnp.sum(totals0[2][:, 0], 0)])
    norms = lax.psum(jnp.concatenate([norms[0], norms[1]], 1), "section")
    own = lax.dynamic_slice_in_dim(norms, section, 1, 0)
    short_grads = lax.psum(short_grads, "section")
    width = shortcut_gain.shape[0]
    own_short = lax.dynamic_slice_in_dim(short_grads, section * width, width, 1)
    return (
        halves_out(output.reshape(half, OUT, OUT * D)),
        halves_out(d_features.reshape(half, IN, IN * DIN)),
        *weight_out,
        own[:, :3],
        own[:, 3:],
        own_short[0],
        own_short[1],
    )


def solution(mesh):
    rows = P("dp", "section", None)
    flat = P(("section", "dp"))
    params = (P("section", None, None), P("section", None, None), P("section"), P("section"))
    return jax.shard_map(
        local,
        mesh=mesh,
        in_specs=(rows, P("dp"), rows) + (flat,) * 11 + params,
        out_specs=(rows, rows) + (flat,) * 11 + params,
        check_vma=False,
    )
```

time: 5260 us -> 1980 us (0.38)
  local copies, waits for them, and re-layouts: 1640 us -> 354 us
  other arithmetic: 1140 us -> 110 us
  blocking collectives: 1800 us -> 877 us
  waiting for transfers between devices: 300 us -> 407 us
  loops' own time: 71.7 us -> 0 us
    scatter-add x40 -> x1, other arithmetic: 786 us -> 18.5 us  [block_backward(): d_u = d_u.at[:, ::2, ::2].add(px_back(d_strided, weight_s))]
    slice x115 -> x18, local copies, waits for them, and re-layouts: 661 us -> 39 us  [the longest x5 13.6 us: local(): weights.append(together[:, start:start + shard.shape[0]].reshape(shape))]
    psum x30 -> x13, blocking collectives: 1490 us -> 871 us  [the longest x2 148 us: block_forward(): sums_a = lax.psum(two_sums(inner, mask_u), 'dp')]
    another operation x272 -> x21, local copies, waits for them, and re-layouts: 407 us -> 3.07 us  [the longest x4 2.98 us: two_sums(): return jnp.stack([crop_sums(weighted), crop_sums(weighted * values)], 1)]
    all_gather x4 -> x2, blocking collectives: 304 us -> 3.76 us  [local(): lax.all_gather(part, 'section', axis=0, tiled=True)]
    conv_general_dilated x0 -> x6, matrix products: none -> 144 us  [conv(): lax.conv_general_dilated(x, kernel, (stride, stride), ((1, 1), (1, 1)), d...]
    dot_general x81 -> x27, matrix products: 197 us -> 54.9 us  [the longest x5 15 us: px_dot(): jnp.einsum('khwc,cd->khwd', values, weight, preferred_element_type=F32)]
    unnamed x7 -> x4, waiting for transfers between devices: 300 us -> 407 us
  transfers between devices with their start and end apart: 21 -> 6, of which waited for: 1 -> 2; matrix products, arithmetic and copies ran while one was open for 47% -> 4% of each run, Pallas kernels for 0% -> 0%
where the time goes in v1:
time: 1980 us; the launch traced here: 1960 us
  blocking collectives  877 us (44%)
  waiting for transfers between devices  407 us (21%)
  local copies, waits for them, and re-layouts  354 us (18%)
  matrix products  199 us (10%)
  other arithmetic  110 us (6%)
    unnamed x4, waiting for transfers between devices  407 us
    psum x2, blocking collectives, block_forward(): sums_a = lax.psum(two_sums(inner, mask_u), 'dp')  148 us
    psum x2, blocking collectives, block_forward(): sums_b = lax.psum(two_sums(convolved, mask_out), 'dp')  144 us
    conv_general_dilated x6, matrix products, conv(): lax.conv_general_dilated(x, kernel, (stride, stride), ((1, 1), (1, 1)), d...  144 us
    psum x2, blocking collectives, block_backward(): lax.psum(jnp.stack([crop_sums(dz_b), crop_sums(dz_b * hat_b)], 1), 'dp')  144 us
    psum x2, blocking collectives, block_backward(): tot_c = lax.psum(jnp.stack(terms, 1), 'dp')  144 us
    psum x2, blocking collectives, block_backward(): lax.psum(jnp.stack([crop_sums(dz_a), crop_sums(dz_a * hat_a)], 1), 'dp')  144 us
    unnamed x245, local copies, waits for them, and re-layouts  84.8 us
  transfers between devices with their start and end apart: 6, of which 2 were waited for; matrix products, arithmetic and copies ran while one was open for 4% of the time, Pallas kernels for 0%

profile of v1, /device:TPU:0, one launch (start us, length us, event | category | flops | bytes accessed | tf_op | source)
XLA Modules:
  0.0 1963.8 jit_solution(5859753982279871982)
XLA Ops:
  7.2 10.0 concatenate.55
  56.3 9.4 slice.324
  65.7 155.4 %all-reduce.10.cloned.1.call-done = bf16[4716544]{0:T(1024)(128)(2,1)} async-done(((bf16[4716544]{0:T(1024)(128)(2,1)}), bf16[4716544]{0:T(1024)(128)(2,1)}) %all-reduce.10.cloned.1.call-update) | async-done | bytes 9433104
  221.1 16.1 reshape.1045
  265.6 76.4 %all-reduce.4 = (f32[2,2,896]{2,0,1:T(2,128)S(1)}, f32[2,1]{0,1:T(1,128)S(1)}) all-reduce(f32[2,2,896]{2,0,1:T(2,128)S(1)} %pad_maximum_fusion.4, f32[2,1]{0,1:T(1,128)S(1)} %copy-done.110), channel_id=1, replica_groups=mesh['section'=2,'dp'=16] {'dp'}, use_global_device_ids=true, to_apply=%region_2.3 | all-reduce | flops 3586 | bytes 28688 | tf_op jit(solution)/shard_map/psum | solution.py:71
  346.4 11.5 reshape.1081
  357.9 24.7 %multiply_reduce_fusion.3 = (f32[2,16,56]{2,0,1:T(2,128)}, f32[2,16,56]{2,0,1:T(2,128)S(1)}, f32[2,14,14,16,56]{4,0,3,2,1:T(2,128)S(1)}) fusion(f32[2,14,14]{0,2,1:T(8,128)S(1)} %and_convert_fusion, bf16[3,3,56,16,56]{4,3,2,1,0:T(8,128)(2,1)} %reshape.1004, bf16[2,28,28,16,56]{4,3,2,1,0:T(8,128)(2,1)} %reshape.1081), kind=kOutput, calls=%fused_computation.16 | convolution fusion | flops 338784768 | bytes 5133856 | tf_op jit(solution)/shard_map/conv_general_dilated | solution.py:52
  388.6 72.0 %psum.107 = f32[2,2,896]{2,0,1:T(2,128)} all-reduce(f32[2,2,896]{2,0,1:T(2,128)} %pad_maximum_fusion.5), channel_id=1, replica_groups=mesh['section'=2,'dp'=16] {'dp'}, use_global_device_ids=true, to_apply=%region_6.7 | all-reduce | flops 3584 | bytes 28672 | tf_op jit(solution)/shard_map/psum | solution.py:76
  493.9 71.8 %psum.108 = f32[2,4,896]{2,0,1:T(2,128)S(1)} all-reduce(f32[2,4,896]{2,0,1:T(2,128)S(1)} %pad_maximum_fusion.2), channel_id=1, replica_groups=mesh['section'=2,'dp'=16] {'dp'}, use_global_device_ids=true, to_apply=%region_12.13 | all-reduce | flops 7168 | bytes 57344 | tf_op jit(solution)/shard_map/psum | solution.py:92
  572.9 72.0 %psum.109 = f32[2,2,896]{2,0,1:T(2,128)S(1)} all-reduce(f32[2,2,896]{2,0,1:T(2,128)S(1)} %pad_maximum_fusion.6), channel_id=1, replica_groups=mesh['section'=2,'dp'=16] {'dp'}, use_global_device_ids=true, to_apply=%region_15.16 | all-reduce | flops 3584 | bytes 28672 | tf_op jit(solution)/shard_map/psum | solution.py:71
  650.9 17.5 multiply_reduce_fusion.2
  668.7 72.2 %psum.110 = f32[2,2,896]{2,0,1:T(2,128)S(1)} all-reduce(f32[2,2,896]{2,0,1:T(2,128)S(1)} %pad_maximum_fusion.7), channel_id=1, replica_groups=mesh['section'=2,'dp'=16] {'dp'}, use_global_device_ids=true, to_apply=%region_18.19 | all-reduce | flops 3584 | bytes 28672 | tf_op jit(solution)/shard_map/psum | solution.py:76
  777.4 71.9 %psum.111 = f32[2,2,896]{2,0,1:T(2,128)S(1)} all-reduce(f32[2,2,896]{2,0,1:T(2,128)S(1)} %pad_maximum_fusion.8), channel_id=1, replica_groups=mesh['section'=2,'dp'=16] {'dp'}, use_global_device_ids=true, to_apply=%region_22.23 | all-reduce | flops 3584 | bytes 28672 | tf_op jit(solution)/shard_map/psum | solution.py:97
  868.9 71.8 %psum.112 = f32[2,2,896]{2,0,1:T(2,128)S(1)} all-reduce(f32[2,2,896]{2,0,1:T(2,128)S(1)} %pad_maximum_fusion.9), channel_id=1, replica_groups=mesh['section'=2,'dp'=16] {'dp'}, use_global_device_ids=true, to_apply=%region_25.26 | all-reduce | flops 3584 | bytes 28672 | tf_op jit(solution)/shard_map/psum | solution.py:128
  953.1 71.8 %psum.113 = f32[2,2,896]{2,0,1:T(2,128)S(1)} all-reduce(f32[2,2,896]{2,0,1:T(2,128)S(1)} %pad_maximum_fusion.10), channel_id=1, replica_groups=mesh['section'=2,'dp'=16] {'dp'}, use_global_device_ids=true, to_apply=%region_29.30 | all-reduce | flops 3584 | bytes 28672 | tf_op jit(solution)/shard_map/psum | solution.py:140
  1033.2 22.8 %fusion.48 = f32[2,14,14,16,56]{4,0,3,2,1:T(2,128)S(1)} fusion(bf16[3,3,16,56,56]{4,3,2,1,0:T(8,128)(2,1)} %bitcast.271, bf16[2,14,14,16,56]{4,3,2,1,0:T(8,128)(2,1)} %reshape.1083), kind=kOutput, calls=%fused_computation.128 | convolution fusion | flops 321126400 | bytes 3010560 | tf_op jit(solution)/shard_map/transpose(jvp())/conv_general_dilated | solution.py:52
  1066.0 71.8 %psum.114 = f32[2,2,896]{2,0,1:T(2,128)S(1)} all-reduce(f32[2,2,896]{2,0,1:T(2,128)S(1)} %pad_maximum_fusion.11), channel_id=1, replica_groups=mesh['section'=2,'dp'=16] {'dp'}, use_global_device_ids=true, to_apply=%region_32.33 | all-reduce | flops 3584 | bytes 28672 | tf_op jit(solution)/shard_map/psum | solution.py:147
  1145.3 71.8 %psum.115 = f32[2,3,896]{2,0,1:T(2,128)S(1)} all-reduce(f32[2,3,896]{2,0,1:T(2,128)S(1)} %pad_maximum_fusion.3), channel_id=1, replica_groups=mesh['section'=2,'dp'=16] {'dp'}, use_global_device_ids=true, to_apply=%region_36.37 | all-reduce | flops 5376 | bytes 43008 | tf_op jit(solution)/shard_map/psum | solution.py:128
  1232.2 17.6 fusion.46
  1270.7 71.9 %psum.116 = f32[2,2,896]{2,0,1:T(2,128)S(1)} all-reduce(f32[2,2,896]{2,0,1:T(2,128)S(1)} %pad_maximum_fusion.12), channel_id=1, replica_groups=mesh['section'=2,'dp'=16] {'dp'}, use_global_device_ids=true, to_apply=%region_40.41 | all-reduce | flops 3584 | bytes 28672 | tf_op jit(solution)/shard_map/psum | solution.py:140
  1348.0 28.8 %fusion.1 = f32[3,3,56,16,56]{4,2,3,1,0:T(8,128)} fusion(bf16[2,28,28,16,56]{4,3,2,1,0:T(8,128)(2,1)} %reshape.1081, bf16[2,14,14,16,56]{4,3,2,1,0:T(8,128)(2,1)S(1)} %reshape.1084), kind=kOutput, calls=%fused_computation.17 | convolution fusion | flops 337383424 | bytes 5318656 | tf_op jit(solution)/shard_map/transpose(jvp())/conv_general_dilated | solution.py:52
  1376.8 32.5 %fusion.53 = f32[2,28,28,16,56]{4,0,3,2,1:T(2,128)} fusion(bf16[3,3,16,56,56]{4,3,2,1,0:T(8,128)(2,1)S(1)} %bitcast.272, bf16[2,14,14,16,56]{4,3,2,1,0:T(8,128)(2,1)S(1)} %reshape.1084), kind=kOutput, calls=%fused_computation.133 | convolution fusion | flops 337383424 | bytes 7225344 | tf_op jit(solution)/shard_map/transpose(jvp())/conv_general_dilated | solution.py:52
  1409.3 11.0 copy.441
  1420.3 12.7 reshape.1080
  1433.1 8.3 fusion.92
  1441.4 71.8 %psum.117 = f32[2,2,896]{2,0,1:T(2,128)S(1)} all-reduce(f32[2,2,896]{2,0,1:T(2,128)S(1)} %pad_maximum_fusion.13), channel_id=1, replica_groups=mesh['section'=2,'dp'=16] {'dp'}, use_global_device_ids=true, to_apply=%region_43.44 | all-reduce | flops 3584 | bytes 28672 | tf_op jit(solution)/shard_map/psum | solution.py:147
  1582.9 11.5 dynamic-update-slice.5
  1608.7 11.4 dynamic-update-slice.9
  1620.1 6.8 dynamic-update-slice.10
  1626.9 11.5 dynamic-update-slice.11
  1657.2 18.5 scatter_fusion
  1694.2 251.5 %all-reduce.12.cloned.1.call-done = f32[32,147392]{1,0:T(8,128)} async-done(((f32[32,147392]{1,0:T(8,128)}), f32[32,147392]{1,0:T(8,128)}) %all-reduce.12.cloned.1.call-update) | async-done | bytes 18866192
  (480 shorter events, 390.7 us)
Async XLA Ops:
  7.2 213.9 %all-reduce.10.cloned.1.call-start = ((), (), s32[]{:S(2)}) async-start(), calls=%async_computation | async-start | bytes 18866176
  27.4 1918.3 %all-reduce.12.cloned.1.call-start = ((), (), s32[]{:S(2)}) async-start(), calls=%async_computation.1 | async-start | bytes 37748736
  30.3 8.9 copy-start.111
  30.3 10.2 copy-start.107
  30.3 10.4 copy-start.108
  30.3 22.5 %collective-permute-start = (bf16[2,14,12544]{2,1,0:T(8,128)(2,1)S(1)}, bf16[2,14,12544]{2,1,0:T(8,128)(2,1)}, u32[]{:S(2)}, u32[]{:S(2)}) collective-permute-start(bf16[2,14,12544]{2,1,0:T(8,128)(2,1)S(1)} %copy.456), channel_id=1, source_target_pairs={{0,16},{16,0},{1,17},{17,1},{2,18},{18,2},{3,19},{19,3},{4,20},{20... | collective-permute-start | bytes 2107400 | tf_op jit(solution)/shard_map/ppermute | solution.py:178
  31.6 18.8 collective-permute-start.2
  36.9 15.9 copy-start.81
  36.9 15.9 copy-start.83
  37.6 15.1 copy-start.68
  37.7 15.1 copy-start.70
  56.3 164.8 %copy-start.18 = (bf16[2,28,28,448]{3,2,1,0:T(8,128)(2,1)}, bf16[2,28,28,448]{3,2,1,0:T(8,128)(2,1)S(1)}, u32[]{:S(2)}) copy-start(bf16[2,28,28,448]{3,2,1,0:T(8,128)(2,1)S(1)} %copy_select_fusion) | copy-start | bytes 4214788
  342.1 399.0 %copy-start.75 = (f32[2,1]{0,1:T(1,128)}, f32[2,1]{0,1:T(1,128)S(1)}, u32[]{:S(2)}) copy-start(f32[2,1]{0,1:T(1,128)S(1)} %get-tuple-element.83) | copy-start | bytes 28
  357.9 108.9 %copy-start.33 = (bf16[32,3136]{1,0:T(8,128)(2,1)S(1)}, bf16[32,3136]{1,0:T(8,128)(2,1)}, u32[]{:S(2)}) copy-start(bf16[32,3136]{1,0:T(8,128)(2,1)} %get-tuple-element.124) | copy-start | bytes 602116
  491.3 74.5 %copy-start.5 = (bf16[32,25088]{1,0:T(8,128)(2,1)S(1)}, bf16[32,25088]{1,0:T(8,128)(2,1)}, u32[]{:S(2)}) copy-start(bf16[32,25088]{1,0:T(8,128)(2,1)} %get-tuple-element.115) | copy-start | bytes 4816900
  571.6 73.3 %copy-start.67 = (f32[896]{0:T(1024)S(1)}, f32[896]{0:T(1024)}, u32[]{:S(2)}) copy-start(f32[896]{0:T(1024)} %get-tuple-element.57) | copy-start | bytes 10756
  571.7 73.3 %copy-start.78 = (f32[896]{0:T(1024)S(1)}, f32[896]{0:T(1024)}, u32[]{:S(2)}) copy-start(f32[896]{0:T(1024)} %get-tuple-element.63) | copy-start | bytes 10756
  773.4 75.9 %copy-start.76 = (f32[2,1]{0,1:T(1,128)S(1)}, f32[2,1]{0,1:T(1,128)}, u32[]{:S(2)}) copy-start(f32[2,1]{0,1:T(1,128)} %copy-done.75) | copy-start | bytes 28
  1140.3 77.4 %copy-start.58 = (f32[2,2,896]{2,0,1:T(2,128)S(1)}, f32[2,2,896]{2,0,1:T(2,128)}, u32[]{:S(2)}) copy-start(f32[2,2,896]{2,0,1:T(2,128)} %psum.107) | copy-start | bytes 43012
  1228.0 38.7 %copy-start.105 = (f32[2,112]{1,0:T(2,128)}, f32[2,112]{1,0:T(2,128)S(1)}, u32[]{:S(2)}) copy-start(f32[2,112]{1,0:T(2,128)S(1)} %convolution_multiply_fusion.1) | copy-start | bytes 2692
  1232.2 19.5 copy-start.12
  1348.0 28.8 %copy-start.20 = (bf16[3,3,896,56]{3,2,1,0:T(8,128)(2,1)S(1)}, bf16[3,3,896,56]{3,2,1,0:T(8,128)(2,1)}, u32[]{:S(2)}) copy-start(bf16[3,3,896,56]{3,2,1,0:T(8,128)(2,1)} %copy.440) | copy-start | bytes 2709508
  1420.3 12.7 copy-start.46
  1420.3 12.7 copy-start.60
  1420.3 12.7 copy-start.62
  1420.3 12.7 copy-start.72
  1420.3 12.8 copy-start.85
  1433.1 80.1 %copy-start.104 = (f32[2]{0:T(128)S(1)}, f32[2]{0:T(128)}, u32[]{:S(2)}) copy-start(f32[2]{0:T(128)} %copy-done.103) | copy-start | bytes 28
  1513.2 7.5 copy-start.19
  1649.2 38.3 %collective-permute-start.1 = (bf16[2,7,12544]{2,0,1:T(2,128)(2,1)}, bf16[2,7,12544]{2,0,1:T(2,128)(2,1)}, u32[]{:S(2)}, u32[]{:S(2)}) collective-permute-start(bf16[2,7,12544]{2,0,1:T(2,128)(2,1)} %get-tuple-element.137), channel_id=1, source_target_pairs={{0,16},{16,0},{1,17},{17,1},{2,18},{18,2},{3,19},{19,3},{4,20},{20... | collective-permute-start | bytes 1053704 | tf_op jit(solution)/shard_map/ppermute | solution.py:186
  1679.5 8.0 copy-start.30
  1681.5 9.3 collective-permute-start.3
  (86 other events, 281.7 us)
Sparse Core Ops, SparseCore 0:
  27.5 193.5 all-reduce.9
  1646.4 299.2 all-reduce.11

commit v2 on v1

v2 whole, which is shorter than its diff:
```python
import functools

import jax
import jax.numpy as jnp
import numpy as np
from jax import lax
from jax.experimental import pallas as pl
from jax.experimental.pallas import tpu as pltpu
from jax.sharding import PartitionSpec as P

D = 896
DIN = 448
OUT = 14
IN = 28
SE0 = 112
SE1 = 224
EPSILON = 1e-05
F32 = jnp.float32
BF16 = jnp.bfloat16
MESH = pl.DeviceIdType.MESH
C = 1024
PX = 224
GUARD = 16
MEMBERS = 16
SHARDS = 32


def dot(a, b, dims):
    return lax.dot_general(a, b, ((dims[:1], dims[1:]), ((), ())), preferred_element_type=F32)


def nn(a, b):
    return dot(a, b, (1, 0))


def nt(a, b):
    return dot(a, b, (1, 1))


def tn(a, b):
    return dot(a, b, (0, 0))


def sig(z):
    return jnp.tanh(z * 0.5) * 0.5 + 0.5


def slope_of(z, s):
    return s * (1.0 + z * (1.0 - s))


def split_rows(rows):
    high = [r.astype(BF16).astype(F32) for r in rows]
    low = [r - h for r, h in zip(rows, high)]
    return high, low


def stacked(rows):
    pad = jnp.zeros((16 - len(rows), rows[0].shape[1]), F32)
    return jnp.concatenate(list(rows) + [pad], 0).astype(BF16)


def row_dot(row, weight, mul):
    high, low = split_rows([row])
    both = mul(stacked(high + low), weight)
    return both[0:1] + both[1:2]


def col(n, width=256):
    return pl.ds(pl.multiple_of(n * width, width), width)


def chunk(j, base=0):
    return pl.ds(pl.multiple_of(j * 16 + base, 16), 16)


def loop(count, body):
    def step(i, carry):
        body(i)
        return carry

    lax.fori_loop(0, count, step, 0)


def main_kernel(
    n_dp, features, upstream, side_ref, expand, wa0, ws, k0, wc0, wd0, wu0, wa1, k1, wc1, wd1,
    wu1, params, out, grad, g_wa0, g_ws, g_k0, g_wc0, g_wd0, g_wu0, g_wa1, g_k1, g_wc1, g_wd1,
    g_wu1, norms,
    inn, pool, u_buf, a0, a1, d_buf, ga, hid, dp_buf, ds_buf, x_buf, up_buf, fs, kd, kr, e_buf,
    wg, st, sv, cn, ng, ng_in, ar2, ar4, arv, asend, arecv, vsend, vrecv, xsend, xrecv, lsem,
):
    section = lax.axis_index("section")
    me = lax.axis_index("dp")
    v = n_dp // MEMBERS
    digit, rest = me // v, lax.rem(me, v)
    other = 1 - section

    def member(hop):
        return lax.rem(digit + hop, MEMBERS) * v + rest

    def near(hop):
        return digit * v + lax.rem(rest + hop, v)

    barrier = pltpu.get_barrier_semaphore()

    def greet(hop):
        pl.semaphore_signal(barrier, inc=1, device_id=(section, member(hop + 1)), device_id_type=MESH)

    def greet_near(hop):
        pl.semaphore_signal(barrier, inc=1, device_id=(section, near(hop + 1)), device_id_type=MESH)

    loop(MEMBERS - 1, greet)
    if v > 1:
        loop(v - 1, greet_near)
    pl.semaphore_signal(barrier, inc=1, device_id=(other, me), device_id_type=MESH)
    pl.semaphore_wait(barrier, MEMBERS + v - 1)

    def local_copy(src, dst, sem=0):
        return pltpu.make_async_copy(src, dst, lsem.at[sem])

    def to_sibling(src, dst, at):
        return pltpu.make_async_remote_copy(
            src_ref=src, dst_ref=dst, send_sem=xsend.at[at], recv_sem=xrecv.at[at],
            device_id=(other, me), device_id_type=MESH,
        )

    mine = pl.ds(2 * section, 2)
    theirs = pl.ds(2 * other, 2)
    copies = [
        to_sibling(features.at[theirs], x_buf.at[section], 0),
        to_sibling(upstream.at[theirs], up_buf.at[section], 1),
        local_copy(features.at[mine], x_buf.at[section], 0),
        local_copy(upstream.at[mine], up_buf.at[section], 1),
        local_copy(expand.at[0], e_buf, 2),
        local_copy(k0, kr, 3),
    ]
    for copy in copies:
        copy.start()

    fs[...] = jnp.zeros_like(fs)
    ng[...] = jnp.zeros_like(ng)
    guard = jnp.zeros((GUARD, C), BF16)
    for ref, count in ((a0, 4), (d_buf, 3)):
        for c in range(2):
            for k in range(count):
                ref[c, k, 0:GUARD] = guard
                ref[c, k, GUARD + PX :] = guard
    for c in range(2):
        a1[c, 0:GUARD] = guard
        a1[c, GUARD + PX :] = guard

    def half_side(c):
        return side_ref[2 * section + c] // 2

    def keep(c, j):
        half = half_side(c)
        bound = jnp.where(j < half, half, 0)
        tile = (lax.broadcasted_iota(jnp.int32, (16, 128), 0) < bound).astype(F32)
        return jnp.concatenate([tile] * (C // 128), 1)

    def crop_count(c):
        half = half_side(c)
        return (half * half).astype(F32)

    def ar_slots(rows, n):
        return (ar2 if rows == 2 else ar4).at[n % 2]

    def ar_start(n, c, rows):
        slots = ar_slots(len(rows), n).at[c]
        slots[digit] = jnp.concatenate(rows, 0)

        def send(hop):
            pltpu.make_async_remote_copy(
                src_ref=slots.at[digit], dst_ref=slots.at[digit], send_sem=asend.at[n % 2, c],
                recv_sem=arecv.at[n % 2, c], device_id=(section, member(hop + 1)),
                device_id_type=MESH,
            ).start()

        loop(MEMBERS - 1, send)

    def ar_wait(n, c, rows):
        slots = ar_slots(rows, n).at[c]
        arrived = slots.at[pl.ds(0, MEMBERS - 1)]
        pltpu.make_async_copy(arrived, arrived, asend.at[n % 2, c]).wait()
        pltpu.make_async_copy(arrived, arrived, arecv.at[n % 2, c]).wait()
        total = slots[0]
        for k in range(1, MEMBERS):
            total = total + slots[k]
        if v > 1:
            again = arv.at[n % 2, c]
            spare = [jnp.zeros((4 - rows, C), F32)] if rows < 4 else []
            again[rest] = jnp.concatenate([total] + spare, 0)

            def send(hop):
                pltpu.make_async_remote_copy(
                    src_ref=again.at[rest], dst_ref=again.at[rest], send_sem=vsend.at[n % 2, c],
                    recv_sem=vrecv.at[n % 2, c], device_id=(section, near(hop + 1)),
                    device_id_type=MESH,
                ).start()

            loop(v - 1, send)
            arrived = again.at[pl.ds(0, v - 1)]
            pltpu.make_async_copy(arrived, arrived, vsend.at[n % 2, c]).wait()
            pltpu.make_async_copy(arrived, arrived, vrecv.at[n % 2, c]).wait()
            total = again[0]
            for k in range(1, v):
                total = total + again[k]
        return [total[k : k + 1] for k in range(rows)]

    def down(sums):
        return jnp.sum(sums, axis=0, keepdims=True)

    def fold(value):
        return value[0:8] + value[8:16]

    def zeros(count):
        return tuple(jnp.zeros((8, C), F32) for _ in range(count))

    def each_column(count, body):
        sums = lax.fori_loop(0, 14, body, zeros(count))
        return [down(one) for one in sums]

    def moment_sums(c, value_of):
        def body(j, sums):
            value = value_of(j)
            weighted = value * keep(c, j)
            return (sums[0] + fold(weighted), sums[1] + fold(weighted * value))

        return each_column(2, body)

    def set_stats(c, index, totals, inverse, gain_row):
        center = totals[0] * inverse
        scaling = lax.rsqrt(totals[1] * inverse - center * center + EPSILON)
        gain = params[gain_row : gain_row + 1] * scaling
        shift_row = gain_row + 6 if gain_row < 6 else gain_row + 1
        st[c, index, 0:1] = center
        st[c, index, 1:2] = scaling
        st[c, index, 2:3] = gain
        st[c, index, 3:4] = params[shift_row : shift_row + 1] - center * gain

    def affine(c, index):
        return st[c, index, 2:3], st[c, index, 3:4]

    def hat_of(c, index):
        return st[c, index, 0:1], st[c, index, 1:2]

    def inverse_out(c):
        return cn[c, 1:2]

    def inverse_in(c):
        return cn[c, 2:3]

    def build_conv(raw):
        def shard(s):
            for k in range(2):
                fs[pl.ds(2048 * k + 63 * s, 64)] = raw[
                    pl.ds(pl.multiple_of(64 * s, 64), 64), 128 * k : 128 * k + 128
                ].astype(F32)

        loop(SHARDS, shard)
        lane = lax.broadcasted_iota(jnp.int32, (64, 256), 1) // 64

        def block(a):
            for tap in range(9):
                tiles = []
                for k in range(2):
                    at = 2048 * k + 224 * tap
                    tiles.append(
                        jnp.concatenate(
                            [
                                fs[pl.ds(at + a, 28, stride=4)],
                                jnp.zeros((4, 128), F32),
                                fs[pl.ds(at + 112 + a, 28, stride=4)],
                                jnp.zeros((4, 128), F32),
                            ],
                            0,
                        )
                    )
                dense = jnp.concatenate(tiles, 1)
                for g in range(4):
                    kd[a, 256 * tap + 64 * g : 256 * tap + 64 * g + 64] = jnp.where(
                        lane == g, dense, 0.0
                    ).astype(BF16)

        loop(4, block)

    def taps0():
        for a in range(3):
            for b in range(3):
                yield a * 3 + b, (0 if a == 1 else 1), (0 if b == 1 else 1), a, b

    def emit(dst, shape):
        copy = local_copy(wg.at[pl.ds(0, shape)], dst, 4)
        copy.start()
        copy.wait()

    def both(ref_of):
        return jnp.concatenate([ref_of(0), ref_of(1)], 0)

    def squeeze(c, b, pooled, wd, wu):
        width = wd.shape[1]
        raw = row_dot(pooled, wd[...], nn)
        squeezed = raw * sig(raw)
        gating = sig(row_dot(squeezed, wu[...], nn))
        sv[b, c, 0:1] = pooled
        sv[b, c, 1:2, 0:width] = raw
        sv[b, c, 2:3, 0:width] = squeezed
        sv[b, c, 3:4] = gating
        return gating

    def gate(c, b, index, conv_k, wd, wu, wc, proj_k):
        a, shift = affine(c, index)

        def pool_chunk(j, sums):
            z = pool[c, conv_k, chunk(j)] * a + shift
            excited = keep(c, j) * (z * sig(z))
            pool[c, 7, chunk(j)] = excited
            return (sums[0] + fold(excited),)

        pooled = each_column(1, pool_chunk)[0] / crop_count(c)
        gating = squeeze(c, b, pooled, wd, wu)

        def gate_chunk(j):
            ga[b, c, chunk(j)] = (pool[c, 7, chunk(j)] * gating).astype(BF16)

        loop(14, gate_chunk)

        def project(n):
            pool[c, proj_k, :, col(n)] = nn(ga[b, c], wc[:, col(n)])

        loop(4, project)
        return moment_sums(c, lambda j: pool[c, proj_k, chunk(j)])

    def ungate(c, b, index, conv_k, wd, wu, wc):
        width = wd.shape[1]

        def back(n):
            pool[c, 7, :, col(n)] = nt(dp_buf[c], wc[col(n)])

        loop(4, back)
        a, shift = affine(c, index)

        def gate_chunk(j, sums):
            z = pool[c, conv_k, chunk(j)] * a + shift
            excited = keep(c, j) * (z * sig(z))
            return (sums[0] + fold(pool[c, 7, chunk(j)] * excited),)

        d_gate = each_column(1, gate_chunk)[0]
        gating = sv[b, c, 3:4]
        d_raw = d_gate * gating * (1.0 - gating)
        raw = sv[b, c, 1:2, 0:width]
        d_squeeze = row_dot(d_raw, wu[...], nt) * slope_of(raw, sig(raw))
        d_pool = row_dot(d_squeeze, wd[...], nt) / crop_count(c)
        sv[b, c, 4:5] = d_raw
        sv[b, c, 5:6, 0:width] = d_squeeze
        center, scaling = hat_of(c, index)

        def slope_chunk(j, sums):
            value = pool[c, conv_k, chunk(j)]
            z = value * a + shift
            d = (pool[c, 7, chunk(j)] * gating + d_pool) * (keep(c, j) * slope_of(z, sig(z)))
            pool[c, 7, chunk(j)] = d
            return (sums[0] + fold(d), sums[1] + fold(d * ((value - center) * scaling)))

        return each_column(2, slope_chunk)

    def small_grads(b, wd, g_wd, g_wu):
        width = wd.shape[1]

        def pairs(x_row, x_width, y_row, y_width):
            xs, ys = [], []
            for c in range(2):
                xh, xl = split_rows([sv[b, c, x_row : x_row + 1, 0:x_width]])
                yh, yl = split_rows([sv[b, c, y_row : y_row + 1, 0:y_width]])
                xs += [xh[0], xh[0], xl[0]]
                ys += [yh[0], yl[0], yh[0]]
            return tn(stacked(xs), stacked(ys))

        wg[:, 0:width] = pairs(0, C, 5, width).astype(BF16)
        copy = local_copy(wg.at[:, pl.ds(0, width)], g_wd, 4)
        copy.start()
        grad_up = pairs(2, width, 4, C)
        rows = SE0 if b == 0 else SE1
        per = 2 * rows // SHARDS
        for h in range(2):
            for k in range(4):
                fs[pl.ds(512 * k + h, rows, stride=2)] = grad_up[
                    0:rows, 512 * h + 128 * k : 512 * h + 128 * k + 128
                ]
        copy.wait()
        for s in range(SHARDS):
            for k in range(4):
                wg[16 * s : 16 * s + 16, 128 * k : 128 * k + 128] = fs[
                    512 * k + per * s : 512 * k + per * s + 16
                ].astype(BF16)
        copy = local_copy(wg.at[pl.ds(0, 512), pl.ds(0, 512)], g_wu, 4)
        copy.start()
        copy.wait()

    def norm_coefficients(c, index, totals, inverse, gain_row, kind):
        center, scaling = hat_of(c, index)
        ng[gain_row : gain_row + 1] += totals[1]
        shift_row = gain_row + 6 if gain_row < 6 else gain_row + 1
        ng[shift_row : shift_row + 1] += totals[0]
        a = st[c, index, 2:3]
        slope = -a * scaling * (totals[1] * inverse)
        offset = -a * (totals[0] * inverse) - slope * center
        return a, slope, offset

    def conv_grad(act_of, v_of, dst):
        lane = lax.broadcasted_iota(jnp.int32, (64, 256), 1) // 64

        def block(a):
            for tap in range(9):
                dense = tn(
                    both(lambda c: act_of(c, tap, col(a))), both(lambda c: v_of(c, tap, col(a)))
                )
                own = jnp.where(lane == 0, dense[0:64], 0.0)
                for g in range(1, 4):
                    own = own + jnp.where(lane == g, dense[64 * g : 64 * g + 64], 0.0)
                for k in range(2):
                    at = 2048 * k + 224 * tap
                    fs[pl.ds(at + a, 28, stride=4)] = own[0:28, 128 * k : 128 * k + 128]
                    fs[pl.ds(at + 112 + a, 28, stride=4)] = own[32:60, 128 * k : 128 * k + 128]

        loop(4, block)

        def shard(s):
            for k in range(2):
                kr[pl.ds(pl.multiple_of(64 * s, 64), 64), 128 * k : 128 * k + 128] = fs[
                    pl.ds(2048 * k + 63 * s, 64)
                ].astype(BF16)

        loop(SHARDS, shard)
        copy = local_copy(kr, dst, 3)
        copy.start()
        copy.wait()

    def outer(left_of, right_of, tiles, dst):
        def tile(m):
            wg[col(m)] = tn(both(lambda c: left_of(c, col(m))), both(right_of)).astype(BF16)

        loop(tiles, tile)
        emit(dst, tiles * 256)

    for copy in copies:
        copy.wait()

    def gather_slices(ref, rows):
        pad = jnp.zeros((16 - rows, D), BF16)
        return jnp.concatenate(
            [
                jnp.concatenate([ref[:, D * j : D * j + D], pad], 0)
                for j in range(OUT)
            ],
            0,
        )

    def phases(c):
        for h in range(2):
            x = gather_slices(x_buf.at[h, c], 14)
            for n in range(4):
                y = nn(x, e_buf[:, 256 * n : 256 * n + 256])
                for j in range(OUT):
                    for k in range(2):
                        fs[pl.ds(512 * (2 * n + k) + 32 * j + 14 * h, 14)] = y[
                            16 * j : 16 * j + 14, 128 * k : 128 * k + 128
                        ]
        for q in range(2):
            def take(j):
                for k in range(8):
                    u_buf[c, q, chunk(j), 128 * k : 128 * k + 128] = fs[
                        pl.ds(512 * k + 32 * j + q, 16, stride=2)
                    ].astype(BF16)

            loop(14, take)

        for q in range(2):
            for r in range(2):
                def product(n):
                    inn[c, 2 * q + r, :, col(n)] = nn(
                        u_buf[c, q, :, 512 * r : 512 * r + 512], wa0[:, col(n)]
                    )

                loop(4, product)

        def body(j, sums):
            mask = keep(c, j)
            first, second = sums
            for k in range(4):
                value = inn[c, k, chunk(j)]
                weighted = value * mask
                first = first + fold(weighted)
                second = second + fold(weighted * value)
            return (first, second)

        sums = each_column(2, body)
        own = jnp.zeros((1, C), F32) + crop_count(c)
        ar_start(0, c, [sums[0], sums[1], own, own])

    loop(2, phases)
    load = local_copy(expand.at[1], e_buf, 2)
    load.start()
    build_conv(kr)
    again = local_copy(k1, kr, 3)
    again.start()
    load.wait()

    def cotangent(c):
        for h in range(2):
            x = gather_slices(up_buf.at[h, c], 7)
            for n in range(4):
                y = nn(x, e_buf[:, 256 * n : 256 * n + 256])
                for j in range(OUT):
                    count = 16 if h == 0 else 7
                    pool[c, 3, 16 * j + 7 * h : 16 * j + 7 * h + count, 256 * n : 256 * n + 256] = y[
                        16 * j : 16 * j + count
                    ]

    loop(2, cotangent)

    def entry_conv(c):
        totals = ar_wait(0, c, 4)
        cn[c, 0:1] = totals[2]
        cn[c, 1:2] = 1.0 / totals[2]
        cn[c, 2:3] = 0.25 / totals[2]
        set_stats(c, 0, totals, inverse_in(c), 0)
        a, shift = affine(c, 0)

        def activate(j):
            mask = keep(c, j)
            for q in range(2):
                for r in range(2):
                    z = inn[c, 2 * q + r, chunk(j)] * a + shift
                    act = mask * (z * sig(z))
                    a0[c, 2 * q + r, chunk(j, GUARD)] = act.astype(BF16)
                    if q == 1:
                        d_buf[c, r, chunk(j, GUARD)] = pltpu.roll(act, 1, 0).astype(BF16)

        loop(14, activate)

        def convolve(n):
            patches = []
            for tap, q, r, ta, tb in taps0():
                at = GUARD - 16 if tb == 0 else GUARD
                src = d_buf.at[c, r] if ta == 0 else a0.at[c, 2 * q + r]
                patches.append(src[at : at + PX, col(n)])
            pool[c, 0, :, col(n)] = nn(jnp.concatenate(patches, 1), kd[n])

        loop(4, convolve)
        ar_start(1, c, moment_sums(c, lambda j: pool[c, 0, chunk(j)]))

    loop(2, entry_conv)

    def strided(c):
        def product(n):
            pool[c, 2, :, col(n)] = nn(u_buf[c, 0, :, 0:512], ws[:, col(n)])

        loop(4, product)

    loop(2, strided)
    again.wait()

    def entry_gate(c):
        totals = ar_wait(1, c, 2)
        set_stats(c, 1, totals, inverse_out(c), 1)
        sums = gate(c, 0, 1, 0, wd0, wu0, wc0, 1)
        ar_start(2, c, sums + moment_sums(c, lambda j: pool[c, 2, chunk(j)]))

    loop(2, entry_gate)
    build_conv(kr)

    def entry_pre(c, j):
        a, shift = affine(c, 2)
        short_a, short_shift = affine(c, 3)
        return (
            pool[c, 1, chunk(j)] * a + pool[c, 2, chunk(j)] * short_a + (shift + short_shift)
        )

    def entry_out(c):
        totals = ar_wait(2, c, 4)
        set_stats(c, 2, totals[0:2], inverse_out(c), 2)
        set_stats(c, 3, totals[2:4], inverse_out(c), 12)

        def finish(j):
            z = entry_pre(c, j)
            hid[c, chunk(j)] = (keep(c, j) * (z * sig(z))).astype(BF16)

        loop(14, finish)

        def product(n):
            pool[c, 4, :, col(n)] = nn(hid[c], wa1[:, col(n)])

        loop(4, product)
        ar_start(3, c, moment_sums(c, lambda j: pool[c, 4, chunk(j)]))

    loop(2, entry_out)

    def body_conv(c):
        set_stats(c, 4, ar_wait(3, c, 2), inverse_out(c), 3)
        a, shift = affine(c, 4)

        def activate(j):
            z = pool[c, 4, chunk(j)] * a + shift
            act = keep(c, j) * (z * sig(z))
            a1[c, chunk(j, GUARD)] = act.astype(BF16)
            d_buf[c, 0, chunk(j, GUARD)] = pltpu.roll(act, 1, 0).astype(BF16)
            d_buf[c, 1, chunk(j, GUARD)] = pltpu.roll(act, 15, 0).astype(BF16)

        loop(14, activate)

        def convolve(n):
            rows = (d_buf.at[c, 0], a1.at[c], d_buf.at[c, 1])
            patches = [
                rows[ta][16 * tb : 16 * tb + PX, col(n)] for ta in range(3) for tb in range(3)
            ]
            pool[c, 5, :, col(n)] = nn(jnp.concatenate(patches, 1), kd[n])

        loop(4, convolve)
        ar_start(4, c, moment_sums(c, lambda j: pool[c, 5, chunk(j)]))

    loop(2, body_conv)

    def body_gate(c):
        set_stats(c, 5, ar_wait(4, c, 2), inverse_out(c), 4)
        ar_start(5, c, gate(c, 1, 5, 5, wd1, wu1, wc1, 6))

    loop(2, body_gate)

    def body_out(c):
        set_stats(c, 6, ar_wait(5, c, 2), inverse_out(c), 5)
        a, shift = affine(c, 6)
        center, scaling = hat_of(c, 6)

        def finish(j, sums):
            value = pool[c, 6, chunk(j)]
            z = value * a + shift + hid[c, chunk(j)].astype(F32)
            mask = keep(c, j)
            s = sig(z)
            dp_buf[c, chunk(j)] = (mask * (z * s)).astype(BF16)
            d_pre = pool[c, 3, chunk(j)] * (mask * slope_of(z, s))
            pool[c, 3, chunk(j)] = d_pre
            return (sums[0] + fold(d_pre), sums[1] + fold(d_pre * ((value - center) * scaling)))

        ar_start(6, c, each_column(2, finish))

    loop(2, body_out)

    def narrow(value, store):
        for start, width in ((0, 256), (256, 256), (512, 256), (768, 128)):
            store(start, width, nt(value, e_buf[start : start + width]))

    def body_emit(c):
        def store(start, width, y):
            for j in range(OUT):
                for h in range(2):
                    up_buf[h, c, :, D * j + start : D * j + start + width] = y[
                        16 * j + 7 * h : 16 * j + 7 * h + 7
                    ].astype(BF16)

        narrow(dp_buf[c], store)

    loop(2, body_emit)
    out_copies = [
        to_sibling(up_buf.at[other], out.at[mine], 2),
        local_copy(up_buf.at[section], out.at[mine], 1),
        local_copy(expand.at[0], e_buf, 2),
    ]
    for copy in out_copies:
        copy.start()

    def body_back_out(c):
        a, slope, offset = norm_coefficients(c, 6, ar_wait(6, c, 2), inverse_out(c), 5, 0)

        def project(j):
            value = pool[c, 6, chunk(j)]
            dp_buf[c, chunk(j)] = (
                keep(c, j) * (a * pool[c, 3, chunk(j)] + slope * value + offset)
            ).astype(BF16)

        loop(14, project)
        ar_start(7, c, ungate(c, 1, 5, 5, wd1, wu1, wc1))

    loop(2, body_back_out)
    outer(lambda c, l: ga[1, c, :, l], lambda c: dp_buf[c], 4, g_wc1)
    small_grads(1, wd1, g_wd1, g_wu1)

    def conv_cotangent(c, index, conv_k, a, slope, offset, versions):
        def body(j):
            d = keep(c, j) * (a * pool[c, 7, chunk(j)] + slope * pool[c, conv_k, chunk(j)] + offset)
            d_buf[c, 0, chunk(j, GUARD)] = d.astype(BF16)
            d_buf[c, 1, chunk(j, GUARD)] = pltpu.roll(d, 15, 0).astype(BF16)
            if versions == 3:
                d_buf[c, 2, chunk(j, GUARD)] = pltpu.roll(d, 1, 0).astype(BF16)

        loop(14, body)

    def v_body(c, tap, lanes):
        ta, tb = tap // 3, tap % 3
        return d_buf[c, (1, 0, 2)[ta], 32 - 16 * tb : 32 - 16 * tb + PX, lanes]

    def v_entry(c, tap, lanes):
        ta, tb = tap // 3, tap % 3
        at = 32 if tb == 0 else 16
        return d_buf[c, 1 if ta == 0 else 0, at : at + PX, lanes]

    def body_back_conv(c):
        a, slope, offset = norm_coefficients(c, 5, ar_wait(7, c, 2), inverse_out(c), 4, 0)
        conv_cotangent(c, 5, 5, a, slope, offset, 3)

        def back(n):
            total = nt(v_body(c, 0, col(n)), kd[n, 0:256])
            for tap in range(1, 9):
                total = total + nt(v_body(c, tap, col(n)), kd[n, 256 * tap : 256 * tap + 256])
            pool[c, 7, :, col(n)] = total

        loop(4, back)
        a, shift = affine(c, 4)
        center, scaling = hat_of(c, 4)

        def body(j, sums):
            value = pool[c, 4, chunk(j)]
            z = value * a + shift
            d = pool[c, 7, chunk(j)] * (keep(c, j) * slope_of(z, sig(z)))
            pool[c, 7, chunk(j)] = d
            return (sums[0] + fold(d), sums[1] + fold(d * ((value - center) * scaling)))

        ar_start(8, c, each_column(2, body))

    loop(2, body_back_conv)
    again = local_copy(k0, kr, 3)
    conv_grad(lambda c, tap, l: a1[c, GUARD : GUARD + PX, l], v_body, g_k1)
    again.start()

    def body_back_in(c):
        a, slope, offset = norm_coefficients(c, 4, ar_wait(8, c, 2), inverse_out(c), 3, 0)

        def body(j):
            dp_buf[c, chunk(j)] = (
                keep(c, j) * (a * pool[c, 7, chunk(j)] + slope * pool[c, 4, chunk(j)] + offset)
            ).astype(BF16)

        loop(14, body)

        def back(n):
            pool[c, 3, :, col(n)] = (
                (nt(dp_buf[c], wa1[col(n)]) + pool[c, 3, :, col(n)]).astype(BF16).astype(F32)
            )

        loop(4, back)
        center, scaling = hat_of(c, 2)
        short_center, short_scaling = hat_of(c, 3)

        def pre(j, sums):
            z = entry_pre(c, j)
            d = pool[c, 3, chunk(j)] * (keep(c, j) * slope_of(z, sig(z)))
            pool[c, 3, chunk(j)] = d
            return (
                sums[0] + fold(d),
                sums[1] + fold(d * ((pool[c, 1, chunk(j)] - center) * scaling)),
                sums[2] + fold(d * ((pool[c, 2, chunk(j)] - short_center) * short_scaling)),
            )

        sums = each_column(3, pre)
        ar_start(9, c, sums + [sums[0]])

    loop(2, body_back_in)
    outer(lambda c, l: hid[c, :, l], lambda c: dp_buf[c], 4, g_wa1)
    again.wait()
    build_conv(kr)

    def entry_back_out(c):
        totals = ar_wait(9, c, 4)
        a, slope, offset = norm_coefficients(c, 2, totals[0:2], inverse_out(c), 2, 0)
        short = norm_coefficients(c, 3, [totals[0], totals[2]], inverse_out(c), 12, 0)

        def project(j):
            mask = keep(c, j)
            d = pool[c, 3, chunk(j)]
            dp_buf[c, chunk(j)] = (
                mask * (a * d + slope * pool[c, 1, chunk(j)] + offset)
            ).astype(BF16)
            ds_buf[c, chunk(j)] = (
                mask * (short[0] * d + short[1] * pool[c, 2, chunk(j)] + short[2])
            ).astype(BF16)

        loop(14, project)
        ar_start(10, c, ungate(c, 0, 1, 0, wd0, wu0, wc0))

    loop(2, entry_back_out)
    outer(lambda c, l: ga[0, c, :, l], lambda c: dp_buf[c], 4, g_wc0)
    outer(lambda c, l: u_buf[c, 0, :, l], lambda c: ds_buf[c], 2, g_ws)
    small_grads(0, wd0, g_wd0, g_wu0)

    def entry_back_conv(c):
        a, slope, offset = norm_coefficients(c, 1, ar_wait(10, c, 2), inverse_out(c), 1, 0)
        conv_cotangent(c, 1, 0, a, slope, offset, 2)
        for q in range(2):
            for r in range(2):
                def back(n):
                    total = None
                    for tap, tq, tr, ta, tb in taps0():
                        if (tq, tr) == (q, r):
                            term = nt(v_entry(c, tap, col(n)), kd[n, 256 * tap : 256 * tap + 256])
                            total = term if total is None else total + term
                    pool[c, 4 + 2 * q + r, :, col(n)] = total

                loop(4, back)
        a, shift = affine(c, 0)
        center, scaling = hat_of(c, 0)

        def body(j, sums):
            mask = keep(c, j)
            first, second = sums
            for k in range(4):
                value = inn[c, k, chunk(j)]
                z = value * a + shift
                d = pool[c, 4 + k, chunk(j)] * (mask * slope_of(z, sig(z)))
                pool[c, 4 + k, chunk(j)] = d
                first = first + fold(d)
                second = second + fold(d * ((value - center) * scaling))
            return (first, second)

        ar_start(11, c, each_column(2, body))

    loop(2, entry_back_conv)

    def act_entry(c, tap, lanes):
        q = 0 if tap // 3 == 1 else 1
        r = 0 if tap % 3 == 1 else 1
        return a0[c, 2 * q + r, GUARD : GUARD + PX, lanes]

    conv_grad(act_entry, v_entry, g_k0)
    for copy in out_copies:
        copy.wait()

    def entry_back_in(c):
        a, slope, offset = norm_coefficients(c, 0, ar_wait(11, c, 2), inverse_in(c), 0, 0)

        def body(j):
            mask = keep(c, j)
            for k in range(4):
                a0[c, k, chunk(j, GUARD)] = (
                    mask * (a * pool[c, 4 + k, chunk(j)] + slope * inn[c, k, chunk(j)] + offset)
                ).astype(BF16)

        loop(14, body)
        for q in range(2):
            for r in range(2):
                def back(n):
                    total = nt(a0[c, 2 * q + r, GUARD : GUARD + PX], wa0[col(n)])
                    if q == 0 and r == 0:
                        total = total + nt(ds_buf[c], ws[col(n)])
                    at = pl.ds(pl.multiple_of(512 * r + 256 * n, 256), 256)
                    ga[0, c, :, at] = total.astype(BF16)

                loop(2, back)

            def store(start, width, y):
                for j in range(OUT):
                    for k in range(width // 128):
                        fs[pl.ds(512 * (start // 128 + k) + 32 * j + q, 14, stride=2)] = y[
                            16 * j : 16 * j + 14, 128 * k : 128 * k + 128
                        ]

            narrow(ga[0, c], store)
        for h in range(2):
            for j in range(OUT):
                for k in range(7):
                    x_buf[h, c, :, D * j + 128 * k : D * j + 128 * k + 128] = fs[
                        512 * k + 32 * j + 14 * h : 512 * k + 32 * j + 14 * h + 14
                    ].astype(BF16)

    loop(2, entry_back_in)
    last = [
        to_sibling(x_buf.at[other], grad.at[mine], 4),
        local_copy(x_buf.at[section], grad.at[mine], 0),
        to_sibling(ng, ng_in, 3),
    ]
    for copy in last:
        copy.start()

    def input_grad(m):
        total = None
        for q in range(2):
            for r in range(2):
                at = pl.ds(pl.multiple_of(512 * r + 256 * m, 256), 256)
                term = tn(
                    both(lambda c: u_buf[c, q, :, at]),
                    both(lambda c: a0[c, 2 * q + r, GUARD : GUARD + PX]),
                )
                total = term if total is None else total + term
        wg[col(m)] = total.astype(BF16)

    loop(2, input_grad)
    emit(g_wa0, 512)
    for copy in last:
        copy.wait()
    norms[...] = ng[...] + ng_in[...]


def lane_maps():
    at = np.arange(D)
    first = np.zeros((D, C), np.float32)
    first[at, at // 14 * 16 + at % 14] = 1
    second = np.zeros((D, C), np.float32)
    second[at, at // 28 * 32 + at % 28] = 1
    return np.stack([first, second])


def main_call(n_dp, *args):
    v = n_dp // MEMBERS
    any_space = pl.BlockSpec(memory_space=pl.ANY)
    vmem = pl.BlockSpec(memory_space=pltpu.VMEM)
    smem = pl.BlockSpec(memory_space=pltpu.SMEM)
    shape = lambda *s, dtype=BF16: jax.ShapeDtypeStruct(s, dtype)
    in_specs = [any_space, any_space, smem, any_space] + [
        vmem, vmem, any_space, vmem, vmem, vmem, vmem, any_space, vmem, vmem, vmem, vmem
    ]
    outs = [
        shape(4, 7, 12544), shape(4, 14, 12544),
        shape(512, C), shape(512, C), shape(2048, 256), shape(C, C), shape(C, 128), shape(512, 512),
        shape(C, C), shape(2048, 256), shape(C, C), shape(C, 256), shape(512, 512),
        shape(16, C, dtype=F32),
    ]
    dma = pltpu.SemaphoreType.DMA
    scratch = [
        pltpu.VMEM((2, 4, PX, C), F32),
        pltpu.VMEM((2, 8, PX, C), F32),
        pltpu.VMEM((2, 2, PX, C), BF16),
        pltpu.VMEM((2, 4, PX + 2 * GUARD, C), BF16),
        pltpu.VMEM((2, PX + 2 * GUARD, C), BF16),
        pltpu.VMEM((2, 3, PX + 2 * GUARD, C), BF16),
        pltpu.VMEM((2, 2, PX, C), BF16),
        pltpu.VMEM((2, PX, C), BF16),
        pltpu.VMEM((2, PX, C), BF16),
        pltpu.VMEM((2, PX, C), BF16),
        pltpu.VMEM((2, 2, 14, 12544), BF16),
        pltpu.VMEM((2, 2, 7, 12544), BF16),
        pltpu.VMEM((4096, 128), F32),
        pltpu.VMEM((4, 2304, 256), BF16),
        pltpu.VMEM((2048, 256), BF16),
        pltpu.VMEM((D, C), BF16),
        pltpu.VMEM((C, C), BF16),
        pltpu.VMEM((2, 7, 8, C), F32),
        pltpu.VMEM((2, 2, 8, C), F32),
        pltpu.VMEM((2, 8, C), F32),
        pltpu.VMEM((16, C), F32),
        pltpu.VMEM((16, C), F32),
        pltpu.VMEM((2, 2, MEMBERS, 2, C), F32),
        pltpu.VMEM((2, 2, MEMBERS, 4, C), F32),
        pltpu.VMEM((2, 2, v, 4, C), F32),
        dma((2, 2)), dma((2, 2)), dma((2, 2)), dma((2, 2)), dma((5,)), dma((5,)), dma((5,)),
    ]
    return pl.pallas_call(
        functools.partial(main_kernel, n_dp),
        out_shape=outs,
        in_specs=in_specs,
        out_specs=[any_space] * 13 + [vmem],
        scratch_shapes=scratch,
        compiler_params=pltpu.CompilerParams(
            collective_id=1, has_side_effects=True, vmem_limit_bytes=64 << 20
        ),
    )(*args)


def widen(values):
    shape = values.shape
    values = values.reshape(shape[:-1] + (shape[-1] // 28, 28))
    values = jnp.pad(values, [(0, 0)] * len(shape) + [(0, 4)])
    return values.reshape(shape[:-1] + (-1,))


def rows_to(values, count):
    return jnp.pad(values, ((0, count - values.shape[0]), (0, 0)))


def pack_wu(values):
    parts = values.reshape(-1, 448)
    return rows_to(widen(parts), 16)


SHAPES = (
    (DIN, D), (9 * 56, D), (D, D), (D, SE0), (SE0, D), (DIN, D), (D, D), (9 * 56, D), (D, D),
    (D, SE1), (SE1, D),
)


def pack_rows(values):
    wide = widen(values.reshape(SHARDS, -1, D))
    rows = wide.shape[1]
    return jnp.pad(wide, ((0, 0), (0, -rows % 16), (0, 0))).reshape(-1, C)


def pack_conv(values):
    wide = widen(values.reshape(SHARDS, 63, 224))
    return jnp.pad(wide, ((0, 0), (0, 1), (0, 0))).reshape(-1, 256)


def pack_down(values, width):
    narrow = values.reshape(SHARDS, 28, width)
    return jnp.pad(narrow, ((0, 0), (0, 4), (0, -width % 128))).reshape(C, -1)


def pack_up(values, rows):
    return rows_to(widen(values.reshape(rows, D)), rows + -rows % 128)


def unwiden(values):
    shape = values.shape
    return values.reshape(shape[:-1] + (shape[-1] // 32, 32))[..., :28].reshape(shape[:-1] + (-1,))


def unpack_rows(values, rows):
    return unwiden(values.reshape(SHARDS, -1, C)[:, :rows]).reshape(-1)


def unpack_conv(values):
    return unwiden(values.reshape(SHARDS, 64, 256)[:, :63]).reshape(-1)


def unpack_down(values, width):
    return values.reshape(SHARDS, 32, -1)[:, :28, :width].reshape(-1)


def unpack_up(values, rows):
    return unwiden(values.reshape(SHARDS, 16, 512)[:, : 2 * rows // SHARDS]).reshape(-1)


def local(
    features, crop_side, upstream,
    entry_in, entry_group, entry_out, entry_down, entry_up, shortcut_weight,
    body_in, body_group, body_out, body_down, body_up,
    norm_gain, norm_shift, shortcut_gain, shortcut_shift,
):
    section = lax.axis_index("section")
    n_dp = lax.axis_size("dp")
    shards = (
        entry_in, entry_group, entry_out, entry_down, entry_up, shortcut_weight,
        body_in, body_group, body_out, body_down, body_up,
    )
    together = lax.all_gather(jnp.concatenate(shards), ("section", "dp"), axis=0, tiled=False)
    whole = []
    start = 0
    for shard in shards:
        whole.append(together[:, start : start + shard.shape[0]])
        start += shard.shape[0]
    gains, shifts, short_gain, short_shift = (
        lax.all_gather(part, "section", axis=0, tiled=True)
        for part in (norm_gain, norm_shift, shortcut_gain, shortcut_shift)
    )
    params = jnp.concatenate(
        [
            gains.reshape(6, D), shifts.reshape(6, D), short_gain.astype(F32)[None],
            short_shift.astype(F32)[None], jnp.zeros((2, D), F32),
        ]
    )
    expand = jnp.asarray(lane_maps(), BF16)
    (
        output, d_features, g_wa0, g_ws, g_k0, g_wc0, g_wd0, g_wu0, g_wa1, g_k1, g_wc1, g_wd1,
        g_wu1, norms,
    ) = main_call(
        n_dp, features, upstream, crop_side, expand, pack_rows(whole[0]), pack_rows(whole[5]),
        pack_conv(whole[1]), pack_rows(whole[2]), pack_down(whole[3], SE0),
        pack_up(whole[4], SE0), pack_rows(whole[6]), pack_conv(whole[7]), pack_rows(whole[8]),
        pack_down(whole[9], SE1), pack_up(whole[10], SE1), widen(params),
    )
    order = (
        unpack_rows(g_wa0, 14), unpack_conv(g_k0), unpack_rows(g_wc0, 28),
        unpack_down(g_wd0, SE0), unpack_up(g_wu0, SE0), unpack_rows(g_ws, 14),
        unpack_rows(g_wa1, 28), unpack_conv(g_k1), unpack_rows(g_wc1, 28),
        unpack_down(g_wd1, SE1), unpack_up(g_wu1, SE1),
    )
    devices = 2 * n_dp
    packed = jnp.concatenate([one.reshape(devices, -1) for one in order], 1).astype(F32)
    summed = lax.psum_scatter(packed, ("section", "dp"), scatter_dimension=0, tiled=False)
    weight_out = []
    start = 0
    for shard in shards:
        weight_out.append(summed[start : start + shard.shape[0]])
        start += shard.shape[0]
    rows = unwiden(norms)
    own = lambda at: lax.dynamic_slice_in_dim(rows, at + 3 * section, 3, 0)[None]
    width = shortcut_gain.shape[0]
    short = lax.dynamic_slice_in_dim(rows[12:14], section * width, width, 1)
    return (output, d_features, *weight_out, own(0), own(6), short[0], short[1])


def solution(mesh):
    rows = P("dp", "section", None)
    flat = P(("section", "dp"))
    params = (P("section", None, None), P("section", None, None), P("section"), P("section"))
    return jax.shard_map(
        local,
        mesh=mesh,
        in_specs=(rows, P("dp"), rows) + (flat,) * 11 + params,
        out_specs=(rows, rows) + (flat,) * 11 + params,
        check_vma=False,
    )
```

time: 1980 us -> 1240 us (0.63)
  blocking collectives: 877 us -> 314 us
  waiting for transfers between devices: 407 us -> 181 us
  matrix products: 199 us -> 0 us
  local copies, waits for them, and re-layouts: 354 us -> 552 us
  Pallas kernels: 0 us -> 166 us
  other arithmetic: 110 us -> 0 us
    psum x13 -> x0, blocking collectives: 871 us -> none  [the longest x2 148 us: block_forward(): sums_a = lax.psum(two_sums(inner, mask_u), 'dp')]
    unnamed x1 -> x2, blocking collectives: 2.45 us -> 310 us
    unnamed x4 -> x2, waiting for transfers between devices: 407 us -> 181 us
    another operation x21 -> x20, local copies, waits for them, and re-layouts: 3.07 us -> 192 us  [the longest x9 101 us: widen(): values = values.reshape(shape[:-1] + (shape[-1] // 28, 28))]
    pallas_call x0 -> x1, Pallas kernels: none -> 166 us  [main_call(): pl.pallas_call(functools.partial(main_kernel, n_dp), out_shape=outs, in_s...]
    conv_general_dilated x6 -> x0, matrix products: 144 us -> none  [conv(): lax.conv_general_dilated(x, kernel, (stride, stride), ((1, 1), (1, 1)), d...]
    pad x0 -> x21, local copies, waits for them, and re-layouts: none -> 57.3 us  [the longest x10 40.4 us: widen(): values = jnp.pad(values, [(0, 0)] * len(shape) + [(0, 4)])]
    dot_general x27 -> x0, matrix products: 54.9 us -> none  [the longest x5 15 us: px_dot(): jnp.einsum('khwc,cd->khwd', values, weight, preferred_element_type=F32)]
  transfers between devices with their start and end apart: 6 -> 1, of which waited for: 2 -> 1; matrix products, arithmetic and copies ran while one was open for 4% -> 0% of each run, Pallas kernels for 0% -> 0%
where the time goes in v2:
time: 1240 us; the launch traced here: 1230 us
  local copies, waits for them, and re-layouts  552 us (45%)
  blocking collectives  314 us (25%)
  waiting for transfers between devices  181 us (15%)
  Pallas kernels  166 us (13%)
  between operations  15.6 us (1%)
    unnamed x2, blocking collectives  310 us
    unnamed x2, waiting for transfers between devices  181 us
    pallas_call x1, Pallas kernels, main_call(): pl.pallas_call(functools.partial(main_kernel, n_dp), out_shape=outs, in_s...  166 us
    unnamed x98, local copies, waits for them, and re-layouts  119 us
    another operation x9, local copies, waits for them, and re-layouts, widen(): values = values.reshape(shape[:-1] + (shape[-1] // 28, 28))  101 us
    another operation x11, local copies, waits for them, and re-layouts, local(): one.reshape(devices, -1)  90.5 us
    reshape x8, local copies, waits for them, and re-layouts, widen(): return values.reshape(shape[:-1] + (-1,))  46.6 us
    slice x9, local copies, waits for them, and re-layouts, unwiden(): values.reshape(shape[:-1] + (shape[-1] // 32, 32))[..., :28]  44.7 us
  transfers between devices with their start and end apart: 1, of which 1 were waited for; matrix products, arithmetic and copies ran while one was open for 0% of the time, Pallas kernels for 0%

profile of v2, /device:TPU:0, one launch (start us, length us, event | category | flops | bytes accessed | tf_op | source)
XLA Modules:
  0.0 1228.0 jit_solution(12853136873416049854)
XLA Ops:
  7.2 10.0 concatenate.22
  40.0 181.1 %all-reduce.29.cloned.1.call-done = bf16[4716544]{0:T(1024)(128)(2,1)} async-done(((bf16[4716544]{0:T(1024)(128)(2,1)}), bf16[4716544]{0:T(1024)(128)(2,1)}) %all-reduce.29.cloned.1.call-update) | async-done | bytes 9433104
  221.0 16.1 %reshape.234 = bf16[32,147392]{1,0:T(8,128)(2,1)} reshape(bf16[4716544]{0:T(1024)(128)(2,1)} %all-reduce.29.cloned.1.call-done) | data formatting | bytes 18866176 | tf_op jit(solution)/shard_map/all_gather | solution.py:1042
  269.2 10.6 reshape_reshape.34
  304.0 11.2 reshape_reshape.33
  340.6 20.6 %reshape_reshape.40 = bf16[32,28,32,28]{3,2,1,0:T(8,128)(2,1)} reshape(bf16[32,25088]{1,0:T(8,128)(2,1)S(1)} %copy-done.5) | data formatting | bytes 3211264 | tf_op jit(solution)/shard_map/reshape;reshape | solution.py:969
  361.2 8.2 pad.91
  369.3 9.9 reshape.251
  379.2 21.1 %reshape_reshape.38 = bf16[32,28,32,28]{3,2,1,0:T(8,128)(2,1)} reshape(bf16[32,25088]{1,0:T(8,128)(2,1)} %get-tuple-element.112) | data formatting | bytes 3211264 | tf_op jit(solution)/shard_map/reshape;reshape | solution.py:969
  400.3 8.2 pad.87
  408.5 11.0 reshape.250
  419.4 21.3 %reshape_reshape.36 = bf16[32,28,32,28]{3,2,1,0:T(8,128)(2,1)} reshape(bf16[32,25088]{1,0:T(8,128)(2,1)} %get-tuple-element.113) | data formatting | bytes 3211264 | tf_op jit(solution)/shard_map/reshape;reshape | solution.py:969
  440.7 8.2 pad.82
  448.9 11.0 reshape.249
  476.9 165.8 %shard_map.314 = (bf16[4,7,12544]{2,1,0:T(8,128)(2,1)}, bf16[4,14,12544]{2,1,0:T(8,128)(2,1)}, bf16[512,1024]{1,0:T(8,128)(2,1)}, bf16[512,1024]{1,0:T(8,128)(2,...) custom-call(bf16[4,14,12544]{2,1,0:T(8,128)(2,1)} %copy.102.features, ...), custom_call_target="tpu_custom_call" | custom-call | tf_op jit(solution)/shard_map/pallas_call | solution.py:955
  709.0 8.1 reshape_reshape_reshape.31
  726.0 8.1 reshape_reshape_reshape.27
  734.2 7.0 reshape.226
  741.2 8.3 copy.119
  749.5 17.2 %reshape_reshape_reshape.34 = bf16[32,25088]{1,0:T(8,128)(2,1)S(1)} reshape(bf16[32,28,32,28]{3,2,1,0:T(8,128)(2,1)} %copy.119) | data formatting | bytes 3211264 | tf_op jit(solution)/shard_map/reshape;reshape;reshape | solution.py:1075
  766.7 7.0 reshape.222
  773.7 8.2 copy.115
  782.0 17.8 %reshape_reshape_reshape.32 = bf16[32,25088]{1,0:T(8,128)(2,1)} reshape(bf16[32,28,32,28]{3,2,1,0:T(8,128)(2,1)} %copy.115) | data formatting | bytes 3211264 | tf_op jit(solution)/shard_map/reshape;reshape;reshape | solution.py:1075
  799.8 7.0 reshape.215
  806.8 8.2 copy.109
  815.1 18.0 %reshape_reshape_reshape.29 = bf16[32,25088]{1,0:T(8,128)(2,1)} reshape(bf16[32,28,32,28]{3,2,1,0:T(8,128)(2,1)} %copy.109) | data formatting | bytes 3211264 | tf_op jit(solution)/shard_map/reshape;reshape;reshape | solution.py:1075
  840.0 11.6 dynamic-update-slice.5
  858.8 6.4 dynamic-update-slice.8
  865.2 11.2 dynamic-update-slice.9
  876.4 6.5 dynamic-update-slice.10
  882.9 11.1 dynamic-update-slice.11
  901.5 307.4 %all-reduce.30 = f32[32,147392]{1,0:T(8,128)} all-reduce(bf16[32,147392]{1,0:T(8,128)(2,1)} %dynamic-update-slice.13), channel_id=3, replica_groups=mesh['section'=2,'dp'=16] {'section','dp'}, use_global_device_ids=true, to_apply=%region_0.1.clone | all-reduce | flops 4716544 | bytes 28299264
  (168 shorter events, 229.0 us)
Async XLA Ops:
  7.2 213.8 %all-reduce.29.cloned.1.call-start = ((), (), s32[]{:S(2)}) async-start(), calls=%async_computation | async-start | bytes 18866176
  27.3 0.7 copy-start.27
  27.3 1.9 copy-start.25
  27.3 2.2 copy-start.26
  27.3 5.1 copy-start.23
  27.3 5.1 copy-start.24
  27.3 10.2 copy-start.20
  27.4 11.3 copy-start.17
  320.2 6.2 copy-start.10
  337.6 3.0 copy-start.5
  448.9 11.0 copy-start.18
  459.9 9.9 copy-start.8
  462.3 8.6 copy-start.7
  469.7 3.9 copy-start
  471.9 3.3 copy-start.1
  642.7 7.9 copy-start.21
  642.7 9.4 copy-start.22
  661.6 10.8 copy-start.13
  666.7 3.4 copy-start.14
  670.1 4.5 copy-start.12
  694.7 5.6 copy-start.9
  721.0 13.2 %copy-start.4 = (bf16[32,28,1024]{2,0,1:T(8,128)(2,1)S(1)}, bf16[32,28,1024]{2,0,1:T(8,128)(2,1)}, u32[]{:S(2)}) copy-start(bf16[32,28,1024]{2,0,1:T(8,128)(2,1)} %copy.136) | copy-start | bytes 5505028
  749.5 17.2 %copy-start.3 = (bf16[32,28,1024]{2,0,1:T(8,128)(2,1)S(1)}, bf16[32,28,1024]{2,0,1:T(8,128)(2,1)}, u32[]{:S(2)}) copy-start(bf16[32,28,1024]{2,0,1:T(8,128)(2,1)} %copy.134) | copy-start | bytes 5505028
  782.0 17.8 %copy-start.2 = (bf16[32,28,1024]{2,0,1:T(8,128)(2,1)S(1)}, bf16[32,28,1024]{2,0,1:T(8,128)(2,1)}, u32[]{:S(2)}) copy-start(bf16[32,28,1024]{2,0,1:T(8,128)(2,1)} %copy.131) | copy-start | bytes 5505028
  815.1 18.0 %copy-start.11 = (bf16[32,12544]{1,0:T(8,128)(2,1)S(1)}, bf16[32,12544]{1,0:T(8,128)(2,1)}, u32[]{:S(2)}) copy-start(bf16[32,12544]{1,0:T(8,128)(2,1)} %reshape_reshape_reshape.27) | copy-start | bytes 2408452
  833.0 18.6 %copy-start.19 = (bf16[32,3136]{1,0:T(8,128)(2,1)S(1)}, bf16[32,3136]{1,0:T(8,128)(2,1)}, u32[]{:S(2)}) copy-start(bf16[32,3136]{1,0:T(8,128)(2,1)} %reshape_reshape.42) | copy-start | bytes 602116
  834.0 31.2 %copy-start.6 = (bf16[32,25088]{1,0:T(8,128)(2,1)S(1)}, bf16[32,25088]{1,0:T(8,128)(2,1)}, u32[]{:S(2)}) copy-start(bf16[32,25088]{1,0:T(8,128)(2,1)} %reshape_reshape_reshape.32) | copy-start | bytes 4816900
  876.4 17.6 %copy-start.15 = (bf16[32,6272]{1,0:T(8,128)(2,1)S(1)}, bf16[32,6272]{1,0:T(8,128)(2,1)}, u32[]{:S(2)}) copy-start(bf16[32,6272]{1,0:T(8,128)(2,1)} %reshape_reshape.43) | copy-start | bytes 1204228
  876.4 21.6 %copy-start.16 = (bf16[32,6272]{1,0:T(8,128)(2,1)S(1)}, bf16[32,6272]{1,0:T(8,128)(2,1)}, u32[]{:S(2)}) copy-start(bf16[32,6272]{1,0:T(8,128)(2,1)} %reshape_reshape_reshape.35) | copy-start | bytes 1204228
Sparse Core Ops, SparseCore 0:
  27.5 193.4 all-reduce.28

commit v3 on v2

--- a/solution.py
+++ b/solution.py
@@ -23,6 +23,14 @@
 GUARD = 16
 MEMBERS = 16
 SHARDS = 32
+ROWS = {
+    "wa0": (0, 16), "k0": (16, 16), "ws": (32, 16), "misc0": (48, 16), "wc0": (64, 32),
+    "wa1": (96, 32), "k1": (128, 16), "misc1": (144, 16), "wc1": (160, 32),
+}
+ORDER = ("wa0", "k0", "ws", "wd0", "wu0", "wc0", "wa1", "k1", "wd1", "wu1", "wc1")
+LINES = (98, 112, 98, 28, 28, 196, 196, 112, 49, 49, 196)
+GATHERS = ((0, 16), (16, 48), (48, 96), (96, 144), (144, 192))
+SCATTERS = ((144, 192), (96, 144), (32, 96), (16, 32), (0, 16))
 
 
 def dot(a, b, dims):
@@ -83,11 +91,13 @@
 
 
 def main_kernel(
-    n_dp, features, upstream, side_ref, expand, wa0, ws, k0, wc0, wd0, wu0, wa1, k1, wc1, wd1,
-    wu1, params, out, grad, g_wa0, g_ws, g_k0, g_wc0, g_wd0, g_wu0, g_wa1, g_k1, g_wc1, g_wd1,
-    g_wu1, norms,
-    inn, pool, u_buf, a0, a1, d_buf, ga, hid, dp_buf, ds_buf, x_buf, up_buf, fs, kd, kr, e_buf,
-    wg, st, sv, cn, ng, ng_in, ar2, ar4, arv, asend, arecv, vsend, vrecv, xsend, xrecv, lsem,
+    n_dp, features, upstream, side_ref, expand, gain_in, shift_in, short_gain_in, short_shift_in,
+    l_wa0, l_k0, l_ws, l_wd0, l_wu0, l_wc0, l_wa1, l_k1, l_wd1, l_wu1, l_wc1,
+    out, grad, o_wa0, o_k0, o_ws, o_wd0, o_wu0, o_wc0, o_wa1, o_k1, o_wd1, o_wu1, o_wc1,
+    gain_out, shift_out, short_gain_out, short_shift_out, land_d, land_c, land_b, land_a,
+    inn, pool, u_buf, a0, a1, d_buf, ga, hid, dp_buf, x_buf, up_buf, fs, kd, e_buf,
+    w, wd0, wu0, wd1, wu1, stage, params, pair, st, sv, cn, ng, ng_in, ar2, ar4, arv,
+    asend, arecv, vsend, vrecv, xsend, xrecv, lsem, gsend, grecv, rsend, rrecv,
 ):
     section = lax.axis_index("section")
     me = lax.axis_index("dp")
@@ -126,28 +136,32 @@
 
     mine = pl.ds(2 * section, 2)
     theirs = pl.ds(2 * other, 2)
+    load_map = local_copy(expand.at[1], e_buf, 2)
     copies = [
         to_sibling(features.at[theirs], x_buf.at[section], 0),
         to_sibling(upstream.at[theirs], up_buf.at[section], 1),
         local_copy(features.at[mine], x_buf.at[section], 0),
         local_copy(upstream.at[mine], up_buf.at[section], 1),
-        local_copy(expand.at[0], e_buf, 2),
-        local_copy(k0, kr, 3),
     ]
+    load_map.start()
     for copy in copies:
         copy.start()
 
     fs[...] = jnp.zeros_like(fs)
     ng[...] = jnp.zeros_like(ng)
     guard = jnp.zeros((GUARD, C), BF16)
-    for ref, count in ((a0, 4), (d_buf, 3)):
+    for ref, count in ((a0, 4), (d_buf, 2)):
         for c in range(2):
             for k in range(count):
                 ref[c, k, 0:GUARD] = guard
                 ref[c, k, GUARD + PX :] = guard
     for c in range(2):
-        a1[c, 0:GUARD] = guard
-        a1[c, GUARD + PX :] = guard
+        for ref in (a1, dp_buf):
+            ref[c, 0:GUARD] = guard
+            ref[c, GUARD + PX :] = guard
+
+    def dp_of(c):
+        return dp_buf[c, GUARD : GUARD + PX]
 
     def half_side(c):
         return side_ref[2 * section + c] // 2
@@ -163,7 +177,7 @@
         return (half * half).astype(F32)
 
     def ar_slots(rows, n):
-        return (ar2 if rows == 2 else ar4).at[n % 2]
+        return ar2.at[n % 2] if rows == 2 else ar4
 
     def ar_start(n, c, rows):
         slots = ar_slots(len(rows), n).at[c]
@@ -250,12 +264,44 @@
     def inverse_in(c):
         return cn[c, 2:3]
 
-    def build_conv(raw):
+    def place(shard):
+        return shard // 16, lax.rem(shard // 4, 4), lax.rem(shard, 4)
+
+    def cols_of(name, lanes):
+        at, count = ROWS[name]
+        value = w[:, :, :, at : at + count, lanes]
+        return value.reshape(SHARDS * count, value.shape[-1])
+
+    def rows_index(name, n):
+        at, count = ROWS[name]
+        if count == 16:
+            return (n, slice(None), slice(None), slice(at, at + 16))
+        return (n // 2, pl.ds(2 * lax.rem(n, 2), 2), slice(None), slice(at, at + 32))
+
+    def rows_of(name, n):
+        return w[rows_index(name, n)].reshape(256, C)
+
+    def put_rows(name, n, value):
+        shape = (4, 4, 16, C) if ROWS[name][1] == 16 else (2, 4, 32, C)
+        w[rows_index(name, n)] = value.astype(BF16).reshape(shape)
+
+    def shard_rows(name, shard):
+        at, count = ROWS[name]
+        return w[(*place(shard), slice(at, at + count))].astype(F32)
+
+    def put_shard(name, shard, value):
+        at, count = ROWS[name]
+        w[(*place(shard), slice(at, at + count))] = value.astype(BF16)
+
+    def tile(k):
+        return slice(128 * k, 128 * k + 128)
+
+    def build_conv(name):
         def shard(s):
-            for k in range(2):
-                fs[pl.ds(2048 * k + 63 * s, 64)] = raw[
-                    pl.ds(pl.multiple_of(64 * s, 64), 64), 128 * k : 128 * k + 128
-                ].astype(F32)
+            rows = shard_rows(name, s)
+            for a in range(4):
+                for k in range(2):
+                    fs[pl.ds(2048 * k + 63 * s + a, 16, stride=4)] = rows[:, tile(2 * a + k)]
 
         loop(SHARDS, shard)
         lane = lax.broadcasted_iota(jnp.int32, (64, 256), 1) // 64
@@ -284,15 +330,41 @@
 
         loop(4, block)
 
+    def build_small(b):
+        wd, wu = (wd0, wu0) if b == 0 else (wd1, wu1)
+        fs[...] = jnp.zeros_like(fs)
+
+        def shard(s):
+            rows = shard_rows("misc0" if b == 0 else "misc1", s)
+            if b == 0:
+                for k in range(8):
+                    fs[pl.ds(32 * s + k, 4, stride=8)] = rows[0:4, tile(k)]
+                    fs[pl.ds(1024 + 256 * (k % 4) + 7 * s + k // 4, 4, stride=2)] = rows[
+                        8:12, tile(k)
+                    ]
+            else:
+                for k in range(8):
+                    fs[pl.ds(1024 * (k % 2) + 32 * s + k // 2, 7, stride=4)] = rows[0:7, tile(k)]
+                    fs[pl.ds(2048 + 256 * k + 7 * s, 7)] = rows[8:15, tile(k)]
+
+        loop(SHARDS, shard)
+        for k in range(1 + b):
+            wd[:, tile(k)] = fs[1024 * k : 1024 * k + 1024].astype(BF16)
+        gap = jnp.zeros((4, 128), F32)
+        for g in range(4 + 4 * b):
+            for k in range(8):
+                if b == 0:
+                    start = 1024 + 256 * (k % 4) + 56 * g + k // 4
+                    part = fs[pl.ds(start, 28, stride=2)]
+                else:
+                    start = 2048 + 256 * k + 28 * g
+                    part = fs[start : start + 28]
+                wu[32 * g : 32 * g + 32, tile(k)] = jnp.concatenate([part, gap], 0).astype(BF16)
+
     def taps0():
         for a in range(3):
             for b in range(3):
                 yield a * 3 + b, (0 if a == 1 else 1), (0 if b == 1 else 1), a, b
-
-    def emit(dst, shape):
-        copy = local_copy(wg.at[pl.ds(0, shape)], dst, 4)
-        copy.start()
-        copy.wait()
 
     def both(ref_of):
         return jnp.concatenate([ref_of(0), ref_of(1)], 0)
@@ -308,7 +380,7 @@
         sv[b, c, 3:4] = gating
         return gating
 
-    def gate(c, b, index, conv_k, wd, wu, wc, proj_k):
+    def gate(c, b, index, conv_k, wd, wu, name, proj_k):
         a, shift = affine(c, index)
 
         def pool_chunk(j, sums):
@@ -326,16 +398,16 @@
         loop(14, gate_chunk)
 
         def project(n):
-            pool[c, proj_k, :, col(n)] = nn(ga[b, c], wc[:, col(n)])
+            pool[c, proj_k, :, col(n)] = nn(ga[b, c], cols_of(name, col(n)))
 
         loop(4, project)
         return moment_sums(c, lambda j: pool[c, proj_k, chunk(j)])
 
-    def ungate(c, b, index, conv_k, wd, wu, wc):
+    def ungate(c, b, index, conv_k, wd, wu, name):
         width = wd.shape[1]
 
         def back(n):
-            pool[c, 7, :, col(n)] = nt(dp_buf[c], wc[col(n)])
+            pool[c, 7, :, col(n)] = nt(dp_of(c), rows_of(name, n))
 
         loop(4, back)
         a, shift = affine(c, index)
@@ -364,8 +436,8 @@
 
         return each_column(2, slope_chunk)
 
-    def small_grads(b, wd, g_wd, g_wu):
-        width = wd.shape[1]
+    def small_grads(b):
+        width = 128 + 128 * b
 
         def pairs(x_row, x_width, y_row, y_width):
             xs, ys = [], []
@@ -376,26 +448,34 @@
                 ys += [yh[0], yl[0], yh[0]]
             return tn(stacked(xs), stacked(ys))
 
-        wg[:, 0:width] = pairs(0, C, 5, width).astype(BF16)
-        copy = local_copy(wg.at[:, pl.ds(0, width)], g_wd, 4)
-        copy.start()
+        grad_down = pairs(0, C, 5, width)
+        for k in range(1 + b):
+            fs[1024 * k : 1024 * k + 1024] = grad_down[:, tile(k)]
         grad_up = pairs(2, width, 4, C)
-        rows = SE0 if b == 0 else SE1
-        per = 2 * rows // SHARDS
-        for h in range(2):
-            for k in range(4):
-                fs[pl.ds(512 * k + h, rows, stride=2)] = grad_up[
-                    0:rows, 512 * h + 128 * k : 512 * h + 128 * k + 128
-                ]
-        copy.wait()
-        for s in range(SHARDS):
-            for k in range(4):
-                wg[16 * s : 16 * s + 16, 128 * k : 128 * k + 128] = fs[
-                    512 * k + per * s : 512 * k + per * s + 16
-                ].astype(BF16)
-        copy = local_copy(wg.at[pl.ds(0, 512), pl.ds(0, 512)], g_wu, 4)
-        copy.start()
-        copy.wait()
+        for g in range(4 + 4 * b):
+            for k in range(8):
+                part = grad_up[32 * g : 32 * g + 28, tile(k)]
+                if b == 0:
+                    fs[pl.ds(1024 + 256 * (k % 4) + 56 * g + k // 4, 28, stride=2)] = part
+                else:
+                    fs[2048 + 256 * k + 28 * g : 2048 + 256 * k + 28 * g + 28] = part
+
+        def shard(s):
+            tiles = []
+            for k in range(8):
+                if b == 0:
+                    count = 4
+                    first = fs[pl.ds(32 * s + k, 4, stride=8)]
+                    second = fs[pl.ds(1024 + 256 * (k % 4) + 7 * s + k // 4, 4, stride=2)]
+                else:
+                    count = 7
+                    first = fs[pl.ds(1024 * (k % 2) + 32 * s + k // 2, 7, stride=4)]
+                    second = fs[pl.ds(2048 + 256 * k + 7 * s, 7)]
+                gap = jnp.zeros((8 - count, 128), F32)
+                tiles.append(jnp.concatenate([first, gap, second, gap], 0))
+            put_shard("misc0" if b == 0 else "misc1", s, jnp.concatenate(tiles, 1))
+
+        loop(SHARDS, shard)
 
     def norm_coefficients(c, index, totals, inverse, gain_row, kind):
         center, scaling = hat_of(c, index)
@@ -407,7 +487,7 @@
         offset = -a * (totals[0] * inverse) - slope * center
         return a, slope, offset
 
-    def conv_grad(act_of, v_of, dst):
+    def conv_grad(act_of, v_of, name):
         lane = lax.broadcasted_iota(jnp.int32, (64, 256), 1) // 64
 
         def block(a):
@@ -426,22 +506,204 @@
         loop(4, block)
 
         def shard(s):
-            for k in range(2):
-                kr[pl.ds(pl.multiple_of(64 * s, 64), 64), 128 * k : 128 * k + 128] = fs[
-                    pl.ds(2048 * k + 63 * s, 64)
-                ].astype(BF16)
+            tiles = [
+                fs[pl.ds(2048 * k + 63 * s + a, 16, stride=4)] for a in range(4) for k in range(2)
+            ]
+            put_shard(name, s, jnp.concatenate(tiles, 1))
 
         loop(SHARDS, shard)
-        copy = local_copy(kr, dst, 3)
-        copy.start()
-        copy.wait()
-
-    def outer(left_of, right_of, tiles, dst):
-        def tile(m):
-            wg[col(m)] = tn(both(lambda c: left_of(c, col(m))), both(right_of)).astype(BF16)
-
-        loop(tiles, tile)
-        emit(dst, tiles * 256)
+
+    def outer(left_of, right_of, name):
+        def block(m):
+            put_rows(name, m, tn(both(lambda c: left_of(c, col(m))), both(right_of)))
+
+        loop(SHARDS * ROWS[name][1] // 256, block)
+
+    z, yx = digit // 4, lax.rem(digit, 4)
+    bits = (1 + section, 2 - section)
+
+    def flip(bit):
+        return yx + bit * (1 - 2 * lax.rem(yx // bit, 2))
+
+    def push(src, dst, to, sends, recvs):
+        pltpu.make_async_remote_copy(
+            src_ref=src, dst_ref=dst, send_sem=sends, recv_sem=recvs,
+            device_id=(section, to * v + rest), device_id_type=MESH,
+        ).start()
+
+    def push_sibling(src, dst, sends, recvs):
+        pltpu.make_async_remote_copy(
+            src_ref=src, dst_ref=dst, send_sem=sends, recv_sem=recvs,
+            device_id=(other, me), device_id_type=MESH,
+        ).start()
+
+    def arrive(ref, sem):
+        pltpu.make_async_copy(ref, ref, sem).wait()
+
+    def gather(k, phase):
+        start, stop = GATHERS[k]
+        rows = pl.ds(start, stop - start)
+        sent = w.at[section, :, :, rows]
+        if phase > 0:
+            sem = grecv.at[k, phase - 1]
+            if phase == 1:
+                arrive(w.at[section, pl.ds(0, 3), 0, rows], sem)
+            elif phase == 2:
+                arrive(sent.at[:, 0], sem)
+            elif phase == 3:
+                arrive(sent.at[:, pl.ds(0, 2)], sem)
+            else:
+                arrive(sent, sem)
+        if phase == 4:
+            arrive(w.at[section, pl.ds(0, 3), 0, rows], gsend.at[k, 0])
+            arrive(sent.at[:, 0], gsend.at[k, 1])
+            arrive(sent.at[:, pl.ds(0, 2)], gsend.at[k, 2])
+            arrive(sent, gsend.at[k, 3])
+            return
+        sems = (gsend.at[k, phase], grecv.at[k, phase])
+        if phase == 0:
+            own = w.at[section, z, yx, rows]
+            for hop in range(1, 4):
+                push(own, own, lax.rem(z + hop, 4) * 4 + yx, *sems)
+        elif phase == 1:
+            push(sent.at[:, yx], sent.at[:, yx], z * 4 + flip(bits[0]), *sems)
+        elif phase == 2:
+            for at in (yx, flip(bits[0])):
+                push(sent.at[:, at], sent.at[:, at], z * 4 + flip(bits[1]), *sems)
+        else:
+            push_sibling(sent, sent, *sems)
+
+    def add_landed(land, rows, blocks, start, count):
+        def fetch(at):
+            return local_copy(
+                land.at[pl.ds(2 * at, 2), rows],
+                stage.at[pl.ds(2 * (at % 2), 2), pl.ds(0, count)], 3 + at % 2,
+            )
+
+        fetch(0).start()
+        for at in range(len(blocks) // 2):
+            if 2 * at + 2 < len(blocks):
+                fetch(at + 1).start()
+            fetch(at).wait()
+            for near in range(2):
+                def strip(i):
+                    here = pl.ds(pl.multiple_of(start + 16 * i, 16), 16)
+                    there = pl.ds(pl.multiple_of(16 * i, 16), 16)
+                    index = (section, *blocks[2 * at + near], here)
+                    w[index] = (
+                        w[index].astype(F32) + stage[2 * (at % 2) + near, there].astype(F32)
+                    ).astype(BF16)
+
+                loop(count // 16, strip)
+
+    def scatter(k, phase):
+        start, stop = SCATTERS[k]
+        count = stop - start
+        rows = pl.ds(start, count)
+        part = w.at[section, :, :, rows]
+        first, second = flip(bits[1]), flip(bits[0])
+        if phase == 1:
+            arrive(land_d.at[:, rows], rrecv.at[k, 0])
+            blocks = [(zz, near) for zz in range(4) for near in range(4)]
+            add_landed(land_d, rows, blocks, start, count)
+        elif phase == 2:
+            arrive(land_c.at[:, rows], rrecv.at[k, 1])
+            blocks = [(zz, near) for zz in range(4) for near in (yx, second)]
+            add_landed(land_c, rows, blocks, start, count)
+        elif phase == 3:
+            arrive(land_b.at[:, rows], rrecv.at[k, 2])
+            add_landed(land_b, rows, [(zz, yx) for zz in range(4)], start, count)
+        elif phase == 4:
+            arrive(land_a.at[pl.ds(0, 3), rows], rrecv.at[k, 3])
+            copies = [
+                local_copy(land_a.at[at, rows], stage.at[at, pl.ds(0, count)], 3 + at)
+                for at in range(3)
+            ]
+            for copy in copies:
+                copy.start()
+            total = w[section, z, yx, start:stop].astype(F32)
+            for at in range(3):
+                copies[at].wait()
+                total = total + stage[at, 0:count].astype(F32)
+            pool[0, 4, start:stop] = total
+            arrive(land_d.at[:, rows], rsend.at[k, 0])
+            arrive(land_c.at[:, rows], rsend.at[k, 1])
+            arrive(land_b.at[:, rows], rsend.at[k, 2])
+            arrive(land_a.at[pl.ds(0, 3), rows], rsend.at[k, 3])
+            return
+        sems = (rsend.at[k, phase], rrecv.at[k, phase])
+        if phase == 0:
+            for zz in range(4):
+                push_sibling(w.at[other, zz, :, rows], land_d.at[pl.ds(4 * zz, 4), rows], *sems)
+        elif phase == 1:
+            for zz in range(4):
+                to = z * 4 + first
+                push(w.at[section, zz, first, rows], land_c.at[2 * zz, rows], to, *sems)
+                push(
+                    w.at[section, zz, first + second - yx, rows], land_c.at[2 * zz + 1, rows], to,
+                    *sems,
+                )
+        elif phase == 2:
+            push(part.at[:, second], land_b.at[:, rows], z * 4 + second, *sems)
+        else:
+            for hop in range(1, 4):
+                to = lax.rem(z + hop, 4)
+                push(
+                    w.at[section, to, yx, rows], land_a.at[hop - 1, rows], to * 4 + yx, *sems
+                )
+
+    shares = {}
+    at = 0
+    for name, ref, count in (
+        ("wa0", l_wa0, 14), ("k0", l_k0, 16), ("ws", l_ws, 14), ("wd0", l_wd0, 4),
+        ("wu0", l_wu0, 4), ("wc0", l_wc0, 28), ("wa1", l_wa1, 28), ("k1", l_k1, 16),
+        ("wd1", l_wd1, 7), ("wu1", l_wu1, 7), ("wc1", l_wc1, 28),
+    ):
+        fs[at : at + ref.shape[0]] = ref[...].astype(F32)
+        value = jnp.concatenate([fs[pl.ds(at + k, count, stride=7)] for k in range(7)], 1)
+        room = 8 if count < 8 else count + -count % 16
+        if room > count:
+            value = jnp.concatenate([value, jnp.zeros((room - count, D), F32)], 0)
+        shares[name] = value
+        at += ref.shape[0] + -ref.shape[0] % 8
+    load_map.wait()
+    own_rows = jnp.concatenate([shares[name] for name in ORDER], 0).astype(BF16)
+    for n in range(4):
+        lanes = slice(256 * n, 256 * n + 256)
+        w[section, z, yx, :, lanes] = nn(own_rows, e_buf[:, lanes]).astype(BF16)
+    gather(0, 0)
+    gather(1, 0)
+
+    halves = jnp.concatenate(
+        [short_gain_in[...].astype(F32), short_shift_in[...].astype(F32)], 1
+    )
+    pair[section] = jnp.concatenate(
+        [gain_in[0], shift_in[0], halves, jnp.zeros((1, D), F32)], 0
+    )
+    swap = to_sibling(pair.at[section], pair.at[section], 3)
+    swap.start()
+    swap.wait()
+    first, second = pair[0], pair[1]
+    short_gain_row = jnp.concatenate([first[6:7, 0:DIN], second[6:7, 0:DIN]], 1)
+    short_shift_row = jnp.concatenate([first[6:7, DIN:], second[6:7, DIN:]], 1)
+    rows = jnp.concatenate(
+        [
+            first[0:3], second[0:3], first[3:6], second[3:6], short_gain_row, short_shift_row,
+            jnp.zeros((2, D), F32),
+        ],
+        0,
+    )
+
+    def thirds(value):
+        high = value.astype(BF16)
+        left = value - high.astype(F32)
+        middle = left.astype(BF16)
+        return jnp.concatenate([high, middle, (left - middle.astype(F32)).astype(BF16)], 0)
+
+    wide = nn(thirds(rows), e_buf[...])
+    params[...] = wide[0:16] + wide[16:32] + wide[32:48]
+    gather(0, 1)
+    gather(2, 0)
 
     for copy in copies:
         copy.wait()
@@ -449,12 +711,27 @@
     def gather_slices(ref, rows):
         pad = jnp.zeros((16 - rows, D), BF16)
         return jnp.concatenate(
-            [
-                jnp.concatenate([ref[:, D * j : D * j + D], pad], 0)
-                for j in range(OUT)
-            ],
-            0,
+            [jnp.concatenate([ref[:, D * j : D * j + D], pad], 0) for j in range(OUT)], 0
         )
+
+    def cotangent(c):
+        for h in range(2):
+            x = gather_slices(up_buf.at[h, c], 7)
+            for n in range(4):
+                y = nn(x, e_buf[:, 256 * n : 256 * n + 256])
+                for j in range(OUT):
+                    count = 16 if h == 0 else 7
+                    pool[c, 3, 16 * j + 7 * h : 16 * j + 7 * h + count, 256 * n : 256 * n + 256] = y[
+                        16 * j : 16 * j + count
+                    ]
+
+    loop(2, cotangent)
+    load_map = local_copy(expand.at[0], e_buf, 2)
+    load_map.start()
+    gather(0, 2)
+    gather(1, 1)
+    fs[...] = jnp.zeros_like(fs)
+    load_map.wait()
 
     def phases(c):
         for h in range(2):
@@ -475,11 +752,23 @@
 
             loop(14, take)
 
+    phases(0)
+    gather(0, 3)
+    gather(1, 2)
+    gather(3, 0)
+    phases(1)
+    load_map = local_copy(expand.at[1], e_buf, 2)
+    load_map.start()
+    gather(0, 4)
+    gather(1, 3)
+    gather(2, 1)
+
+    def entry_inner(c):
         for q in range(2):
             for r in range(2):
                 def product(n):
                     inn[c, 2 * q + r, :, col(n)] = nn(
-                        u_buf[c, q, :, 512 * r : 512 * r + 512], wa0[:, col(n)]
+                        u_buf[c, q, :, 512 * r : 512 * r + 512], cols_of("wa0", col(n))
                     )
 
                 loop(4, product)
@@ -498,26 +787,13 @@
         own = jnp.zeros((1, C), F32) + crop_count(c)
         ar_start(0, c, [sums[0], sums[1], own, own])
 
-    loop(2, phases)
-    load = local_copy(expand.at[1], e_buf, 2)
-    load.start()
-    build_conv(kr)
-    again = local_copy(k1, kr, 3)
-    again.start()
-    load.wait()
-
-    def cotangent(c):
-        for h in range(2):
-            x = gather_slices(up_buf.at[h, c], 7)
-            for n in range(4):
-                y = nn(x, e_buf[:, 256 * n : 256 * n + 256])
-                for j in range(OUT):
-                    count = 16 if h == 0 else 7
-                    pool[c, 3, 16 * j + 7 * h : 16 * j + 7 * h + count, 256 * n : 256 * n + 256] = y[
-                        16 * j : 16 * j + count
-                    ]
-
-    loop(2, cotangent)
+    loop(2, entry_inner)
+    gather(2, 2)
+    gather(4, 0)
+    gather(1, 4)
+    build_conv("k0")
+    gather(2, 3)
+    gather(3, 1)
 
     def entry_conv(c):
         totals = ar_wait(0, c, 4)
@@ -554,21 +830,27 @@
 
     def strided(c):
         def product(n):
-            pool[c, 2, :, col(n)] = nn(u_buf[c, 0, :, 0:512], ws[:, col(n)])
+            pool[c, 2, :, col(n)] = nn(u_buf[c, 0, :, 0:512], cols_of("ws", col(n)))
 
         loop(4, product)
 
     loop(2, strided)
-    again.wait()
+    gather(2, 4)
+    gather(3, 2)
+    gather(4, 1)
+    build_small(0)
 
     def entry_gate(c):
         totals = ar_wait(1, c, 2)
         set_stats(c, 1, totals, inverse_out(c), 1)
-        sums = gate(c, 0, 1, 0, wd0, wu0, wc0, 1)
+        sums = gate(c, 0, 1, 0, wd0, wu0, "wc0", 1)
         ar_start(2, c, sums + moment_sums(c, lambda j: pool[c, 2, chunk(j)]))
 
     loop(2, entry_gate)
-    build_conv(kr)
+    gather(3, 3)
+    gather(4, 2)
+    gather(3, 4)
+    build_conv("k1")
 
     def entry_pre(c, j):
         a, shift = affine(c, 2)
@@ -589,7 +871,7 @@
         loop(14, finish)
 
         def product(n):
-            pool[c, 4, :, col(n)] = nn(hid[c], wa1[:, col(n)])
+            pool[c, 4, :, col(n)] = nn(hid[c], cols_of("wa1", col(n)))
 
         loop(4, product)
         ar_start(3, c, moment_sums(c, lambda j: pool[c, 4, chunk(j)]))
@@ -620,10 +902,13 @@
         ar_start(4, c, moment_sums(c, lambda j: pool[c, 5, chunk(j)]))
 
     loop(2, body_conv)
+    gather(4, 3)
+    gather(4, 4)
+    build_small(1)
 
     def body_gate(c):
         set_stats(c, 5, ar_wait(4, c, 2), inverse_out(c), 4)
-        ar_start(5, c, gate(c, 1, 5, 5, wd1, wu1, wc1, 6))
+        ar_start(5, c, gate(c, 1, 5, 5, wd1, wu1, "wc1", 6))
 
     loop(2, body_gate)
 
@@ -637,7 +922,7 @@
             z = value * a + shift + hid[c, chunk(j)].astype(F32)
             mask = keep(c, j)
             s = sig(z)
-            dp_buf[c, chunk(j)] = (mask * (z * s)).astype(BF16)
+            dp_buf[c, chunk(j, GUARD)] = (mask * (z * s)).astype(BF16)
             d_pre = pool[c, 3, chunk(j)] * (mask * slope_of(z, s))
             pool[c, 3, chunk(j)] = d_pre
             return (sums[0] + fold(d_pre), sums[1] + fold(d_pre * ((value - center) * scaling)))
@@ -645,6 +930,7 @@
         ar_start(6, c, each_column(2, finish))
 
     loop(2, body_out)
+    load_map.wait()
 
     def narrow(value, store):
         for start, width in ((0, 256), (256, 256), (512, 256), (768, 128)):
@@ -658,7 +944,7 @@
                         16 * j + 7 * h : 16 * j + 7 * h + 7
                     ].astype(BF16)
 
-        narrow(dp_buf[c], store)
+        narrow(dp_of(c), store)
 
     loop(2, body_emit)
     out_copies = [
@@ -674,16 +960,17 @@
 
         def project(j):
             value = pool[c, 6, chunk(j)]
-            dp_buf[c, chunk(j)] = (
+            dp_buf[c, chunk(j, GUARD)] = (
                 keep(c, j) * (a * pool[c, 3, chunk(j)] + slope * value + offset)
             ).astype(BF16)
 
         loop(14, project)
-        ar_start(7, c, ungate(c, 1, 5, 5, wd1, wu1, wc1))
+        ar_start(7, c, ungate(c, 1, 5, 5, wd1, wu1, "wc1"))
 
     loop(2, body_back_out)
-    outer(lambda c, l: ga[1, c, :, l], lambda c: dp_buf[c], 4, g_wc1)
-    small_grads(1, wd1, g_wd1, g_wu1)
+    outer(lambda c, l: ga[1, c, :, l], dp_of, "wc1")
+    small_grads(1)
+    scatter(0, 0)
 
     def conv_cotangent(c, index, conv_k, a, slope, offset, versions):
         def body(j):
@@ -691,13 +978,14 @@
             d_buf[c, 0, chunk(j, GUARD)] = d.astype(BF16)
             d_buf[c, 1, chunk(j, GUARD)] = pltpu.roll(d, 15, 0).astype(BF16)
             if versions == 3:
-                d_buf[c, 2, chunk(j, GUARD)] = pltpu.roll(d, 1, 0).astype(BF16)
+                dp_buf[c, chunk(j, GUARD)] = pltpu.roll(d, 1, 0).astype(BF16)
 
         loop(14, body)
 
     def v_body(c, tap, lanes):
         ta, tb = tap // 3, tap % 3
-        return d_buf[c, (1, 0, 2)[ta], 32 - 16 * tb : 32 - 16 * tb + PX, lanes]
+        ref = (d_buf.at[c, 1], d_buf.at[c, 0], dp_buf.at[c])[ta]
+        return ref[32 - 16 * tb : 32 - 16 * tb + PX, lanes]
 
     def v_entry(c, tap, lanes):
         ta, tb = tap // 3, tap % 3
@@ -728,15 +1016,14 @@
         ar_start(8, c, each_column(2, body))
 
     loop(2, body_back_conv)
-    again = local_copy(k0, kr, 3)
-    conv_grad(lambda c, tap, l: a1[c, GUARD : GUARD + PX, l], v_body, g_k1)
-    again.start()
+    conv_grad(lambda c, tap, l: a1[c, GUARD : GUARD + PX, l], v_body, "k1")
+    scatter(0, 1)
 
     def body_back_in(c):
         a, slope, offset = norm_coefficients(c, 4, ar_wait(8, c, 2), inverse_out(c), 3, 0)
 
         def body(j):
-            dp_buf[c, chunk(j)] = (
+            dp_buf[c, chunk(j, GUARD)] = (
                 keep(c, j) * (a * pool[c, 7, chunk(j)] + slope * pool[c, 4, chunk(j)] + offset)
             ).astype(BF16)
 
@@ -744,7 +1031,7 @@
 
         def back(n):
             pool[c, 3, :, col(n)] = (
-                (nt(dp_buf[c], wa1[col(n)]) + pool[c, 3, :, col(n)]).astype(BF16).astype(F32)
+                (nt(dp_of(c), rows_of("wa1", n)) + pool[c, 3, :, col(n)]).astype(BF16).astype(F32)
             )
 
         loop(4, back)
@@ -765,9 +1052,10 @@
         ar_start(9, c, sums + [sums[0]])
 
     loop(2, body_back_in)
-    outer(lambda c, l: hid[c, :, l], lambda c: dp_buf[c], 4, g_wa1)
-    again.wait()
-    build_conv(kr)
+    outer(lambda c, l: hid[c, :, l], dp_of, "wa1")
+    scatter(1, 0)
+    scatter(0, 2)
+    build_conv("k0")
 
     def entry_back_out(c):
         totals = ar_wait(9, c, 4)
@@ -777,20 +1065,28 @@
         def project(j):
             mask = keep(c, j)
             d = pool[c, 3, chunk(j)]
-            dp_buf[c, chunk(j)] = (
+            dp_buf[c, chunk(j, GUARD)] = (
                 mask * (a * d + slope * pool[c, 1, chunk(j)] + offset)
             ).astype(BF16)
-            ds_buf[c, chunk(j)] = (
+            hid[c, chunk(j)] = (
                 mask * (short[0] * d + short[1] * pool[c, 2, chunk(j)] + short[2])
             ).astype(BF16)
 
         loop(14, project)
-        ar_start(10, c, ungate(c, 0, 1, 0, wd0, wu0, wc0))
+
+        def back(n):
+            pool[c, 2, :, col(n)] = nt(hid[c], rows_of("ws", n))
+
+        loop(2, back)
+        ar_start(10, c, ungate(c, 0, 1, 0, wd0, wu0, "wc0"))
 
     loop(2, entry_back_out)
-    outer(lambda c, l: ga[0, c, :, l], lambda c: dp_buf[c], 4, g_wc0)
-    outer(lambda c, l: u_buf[c, 0, :, l], lambda c: ds_buf[c], 2, g_ws)
-    small_grads(0, wd0, g_wd0, g_wu0)
+    outer(lambda c, l: ga[0, c, :, l], dp_of, "wc0")
+    outer(lambda c, l: u_buf[c, 0, :, l], lambda c: hid[c], "ws")
+    small_grads(0)
+    scatter(2, 0)
+    scatter(1, 1)
+    scatter(0, 3)
 
     def entry_back_conv(c):
         a, slope, offset = norm_coefficients(c, 1, ar_wait(10, c, 2), inverse_out(c), 1, 0)
@@ -830,7 +1126,10 @@
         r = 0 if tap % 3 == 1 else 1
         return a0[c, 2 * q + r, GUARD : GUARD + PX, lanes]
 
-    conv_grad(act_entry, v_entry, g_k0)
+    conv_grad(act_entry, v_entry, "k0")
+    scatter(3, 0)
+    scatter(2, 1)
+    scatter(1, 2)
     for copy in out_copies:
         copy.wait()
 
@@ -845,40 +1144,11 @@
                 ).astype(BF16)
 
         loop(14, body)
-        for q in range(2):
-            for r in range(2):
-                def back(n):
-                    total = nt(a0[c, 2 * q + r, GUARD : GUARD + PX], wa0[col(n)])
-                    if q == 0 and r == 0:
-                        total = total + nt(ds_buf[c], ws[col(n)])
-                    at = pl.ds(pl.multiple_of(512 * r + 256 * n, 256), 256)
-                    ga[0, c, :, at] = total.astype(BF16)
-
-                loop(2, back)
-
-            def store(start, width, y):
-                for j in range(OUT):
-                    for k in range(width // 128):
-                        fs[pl.ds(512 * (start // 128 + k) + 32 * j + q, 14, stride=2)] = y[
-                            16 * j : 16 * j + 14, 128 * k : 128 * k + 128
-                        ]
-
-            narrow(ga[0, c], store)
-        for h in range(2):
-            for j in range(OUT):
-                for k in range(7):
-                    x_buf[h, c, :, D * j + 128 * k : D * j + 128 * k + 128] = fs[
-                        512 * k + 32 * j + 14 * h : 512 * k + 32 * j + 14 * h + 14
-                    ].astype(BF16)
 
     loop(2, entry_back_in)
-    last = [
-        to_sibling(x_buf.at[other], grad.at[mine], 4),
-        local_copy(x_buf.at[section], grad.at[mine], 0),
-        to_sibling(ng, ng_in, 3),
-    ]
-    for copy in last:
-        copy.start()
+    scatter(0, 4)
+    swap = to_sibling(ng, ng_in, 3)
+    swap.start()
 
     def input_grad(m):
         total = None
@@ -890,13 +1160,98 @@
                     both(lambda c: a0[c, 2 * q + r, GUARD : GUARD + PX]),
                 )
                 total = term if total is None else total + term
-        wg[col(m)] = total.astype(BF16)
-
-    loop(2, input_grad)
-    emit(g_wa0, 512)
+        return total
+
+    def entry_back_input(c):
+        for q in range(2):
+            for r in range(2):
+                def back(n):
+                    total = nt(a0[c, 2 * q + r, GUARD : GUARD + PX], rows_of("wa0", n))
+                    if q == 0 and r == 0:
+                        total = total + pool[c, 2, :, col(n)]
+                    at = pl.ds(pl.multiple_of(512 * r + 256 * n, 256), 256)
+                    d_buf[c, q, 0:PX, at] = total.astype(BF16)
+
+                loop(2, back)
+
+    loop(2, entry_back_input)
+
+    def input_block(m):
+        put_rows("wa0", m, input_grad(m))
+
+    loop(2, input_block)
+    scatter(4, 0)
+    scatter(3, 1)
+
+    def entry_emit(c):
+        for q in range(2):
+            def store(start, width, y):
+                for j in range(OUT):
+                    for k in range(width // 128):
+                        fs[pl.ds(512 * (start // 128 + k) + 32 * j + q, 14, stride=2)] = y[
+                            16 * j : 16 * j + 14, 128 * k : 128 * k + 128
+                        ]
+
+            narrow(d_buf[c, q, 0:PX], store)
+        for h in range(2):
+            for j in range(OUT):
+                for k in range(7):
+                    x_buf[h, c, :, D * j + 128 * k : D * j + 128 * k + 128] = fs[
+                        512 * k + 32 * j + 14 * h : 512 * k + 32 * j + 14 * h + 14
+                    ].astype(BF16)
+
+    entry_emit(0)
+    scatter(4, 1)
+    scatter(3, 2)
+    scatter(2, 2)
+    scatter(1, 3)
+    entry_emit(1)
+    load_map = local_copy(expand.at[1], e_buf, 2)
+    load_map.start()
+    last = [
+        to_sibling(x_buf.at[other], grad.at[mine], 4),
+        local_copy(x_buf.at[section], grad.at[mine], 0),
+    ]
+    for copy in last:
+        copy.start()
+    scatter(4, 2)
+    scatter(3, 3)
+    scatter(2, 3)
+    scatter(1, 4)
+    scatter(4, 3)
+    scatter(2, 4)
+    scatter(3, 4)
+    scatter(4, 4)
+    load_map.wait()
+    swap.wait()
+    total = thirds(ng[...] + ng_in[...])
+    total = nt(total, e_buf[...])
+    total = total[0:16] + total[16:32] + total[32:48]
+
+    def own(top, low):
+        return jnp.where(section == 0, top, low)
+
+    gain_out[0] = own(total[0:3], total[3:6])
+    shift_out[0] = own(total[6:9], total[9:12])
+    short_gain_out[...] = own(total[12:13, 0:DIN], total[12:13, DIN:])
+    short_shift_out[...] = own(total[13:14, 0:DIN], total[13:14, DIN:])
+    total = pool[0, 4, 0:192]
+    high = total.astype(BF16)
+    low = (total - high.astype(F32)).astype(BF16)
+    final = nt(high, e_buf[...]) + nt(low, e_buf[...])
+    for name, ref, count in (
+        ("wa0", o_wa0, 14), ("k0", o_k0, 16), ("ws", o_ws, 14), ("wd0", o_wd0, 4),
+        ("wu0", o_wu0, 4), ("wc0", o_wc0, 28), ("wa1", o_wa1, 28), ("k1", o_k1, 16),
+        ("wd1", o_wd1, 7), ("wu1", o_wu1, 7), ("wc1", o_wc1, 28),
+    ):
+        if name[1] in "du":
+            at = ROWS["misc" + name[2]][0] + (8 if name[1] == "u" else 0)
+        else:
+            at = ROWS[name][0]
+        for k in range(7):
+            ref[pl.ds(k, count, stride=7)] = final[at : at + count, 128 * k : 128 * k + 128]
     for copy in last:
         copy.wait()
-    norms[...] = ng[...] + ng_in[...]
 
 
 def lane_maps():
@@ -914,14 +1269,12 @@
     vmem = pl.BlockSpec(memory_space=pltpu.VMEM)
     smem = pl.BlockSpec(memory_space=pltpu.SMEM)
     shape = lambda *s, dtype=BF16: jax.ShapeDtypeStruct(s, dtype)
-    in_specs = [any_space, any_space, smem, any_space] + [
-        vmem, vmem, any_space, vmem, vmem, vmem, vmem, any_space, vmem, vmem, vmem, vmem
-    ]
+    flat = [shape(count, 128, dtype=F32) for count in LINES]
     outs = [
-        shape(4, 7, 12544), shape(4, 14, 12544),
-        shape(512, C), shape(512, C), shape(2048, 256), shape(C, C), shape(C, 128), shape(512, 512),
-        shape(C, C), shape(2048, 256), shape(C, C), shape(C, 256), shape(512, 512),
-        shape(16, C, dtype=F32),
+        shape(4, 7, 12544), shape(4, 14, 12544), *flat,
+        shape(1, 3, D, dtype=F32), shape(1, 3, D, dtype=F32),
+        shape(1, DIN, dtype=F32), shape(1, DIN, dtype=F32),
+        shape(16, 192, C), shape(8, 192, C), shape(4, 192, C), shape(3, 192, C),
     ]
     dma = pltpu.SemaphoreType.DMA
     scratch = [
@@ -930,101 +1283,44 @@
         pltpu.VMEM((2, 2, PX, C), BF16),
         pltpu.VMEM((2, 4, PX + 2 * GUARD, C), BF16),
         pltpu.VMEM((2, PX + 2 * GUARD, C), BF16),
-        pltpu.VMEM((2, 3, PX + 2 * GUARD, C), BF16),
+        pltpu.VMEM((2, 2, PX + 2 * GUARD, C), BF16),
         pltpu.VMEM((2, 2, PX, C), BF16),
         pltpu.VMEM((2, PX, C), BF16),
-        pltpu.VMEM((2, PX, C), BF16),
-        pltpu.VMEM((2, PX, C), BF16),
+        pltpu.VMEM((2, PX + 2 * GUARD, C), BF16),
         pltpu.VMEM((2, 2, 14, 12544), BF16),
         pltpu.VMEM((2, 2, 7, 12544), BF16),
         pltpu.VMEM((4096, 128), F32),
         pltpu.VMEM((4, 2304, 256), BF16),
-        pltpu.VMEM((2048, 256), BF16),
         pltpu.VMEM((D, C), BF16),
-        pltpu.VMEM((C, C), BF16),
+        pltpu.VMEM((2, 4, 4, 192, C), BF16),
+        pltpu.VMEM((C, 128), BF16),
+        pltpu.VMEM((128, C), BF16),
+        pltpu.VMEM((C, 256), BF16),
+        pltpu.VMEM((256, C), BF16),
+        pltpu.VMEM((4, 64, C), BF16),
+        pltpu.VMEM((16, C), F32),
+        pltpu.VMEM((2, 8, D), F32),
         pltpu.VMEM((2, 7, 8, C), F32),
         pltpu.VMEM((2, 2, 8, C), F32),
         pltpu.VMEM((2, 8, C), F32),
         pltpu.VMEM((16, C), F32),
         pltpu.VMEM((16, C), F32),
         pltpu.VMEM((2, 2, MEMBERS, 2, C), F32),
-        pltpu.VMEM((2, 2, MEMBERS, 4, C), F32),
+        pltpu.VMEM((2, MEMBERS, 4, C), F32),
         pltpu.VMEM((2, 2, v, 4, C), F32),
-        dma((2, 2)), dma((2, 2)), dma((2, 2)), dma((2, 2)), dma((5,)), dma((5,)), dma((5,)),
+        dma((2, 2)), dma((2, 2)), dma((2, 2)), dma((2, 2)), dma((5,)), dma((5,)), dma((6,)),
+        dma((5, 4)), dma((5, 4)), dma((5, 4)), dma((5, 4)),
     ]
     return pl.pallas_call(
         functools.partial(main_kernel, n_dp),
         out_shape=outs,
-        in_specs=in_specs,
-        out_specs=[any_space] * 13 + [vmem],
+        in_specs=[any_space, any_space, smem, any_space] + [vmem] * 15,
+        out_specs=[any_space] * 2 + [vmem] * 15 + [any_space] * 4,
         scratch_shapes=scratch,
         compiler_params=pltpu.CompilerParams(
             collective_id=1, has_side_effects=True, vmem_limit_bytes=64 << 20
         ),
     )(*args)
-
-
-def widen(values):
-    shape = values.shape
-    values = values.reshape(shape[:-1] + (shape[-1] // 28, 28))
-    values = jnp.pad(values, [(0, 0)] * len(shape) + [(0, 4)])
-    return values.reshape(shape[:-1] + (-1,))
-
-
-def rows_to(values, count):
-    return jnp.pad(values, ((0, count - values.shape[0]), (0, 0)))
-
-
-def pack_wu(values):
-    parts = values.reshape(-1, 448)
-    return rows_to(widen(parts), 16)
-
-
-SHAPES = (
-    (DIN, D), (9 * 56, D), (D, D), (D, SE0), (SE0, D), (DIN, D), (D, D), (9 * 56, D), (D, D),
-    (D, SE1), (SE1, D),
-)
-
-
-def pack_rows(values):
-    wide = widen(values.reshape(SHARDS, -1, D))
-    rows = wide.shape[1]
-    return jnp.pad(wide, ((0, 0), (0, -rows % 16), (0, 0))).reshape(-1, C)
-
-
-def pack_conv(values):
-    wide = widen(values.reshape(SHARDS, 63, 224))
-    return jnp.pad(wide, ((0, 0), (0, 1), (0, 0))).reshape(-1, 256)
-
-
-def pack_down(values, width):
-    narrow = values.reshape(SHARDS, 28, width)
-    return jnp.pad(narrow, ((0, 0), (0, 4), (0, -width % 128))).reshape(C, -1)
-
-
-def pack_up(values, rows):
-    return rows_to(widen(values.reshape(rows, D)), rows + -rows % 128)
-
-
-def unwiden(values):
-    shape = values.shape
-    return values.reshape(shape[:-1] + (shape[-1] // 32, 32))[..., :28].reshape(shape[:-1] + (-1,))
-
-
-def unpack_rows(values, rows):
-    return unwiden(values.reshape(SHARDS, -1, C)[:, :rows]).reshape(-1)
-
-
-def unpack_conv(values):
-    return unwiden(values.reshape(SHARDS, 64, 256)[:, :63]).reshape(-1)
-
-
-def unpack_down(values, width):
-    return values.reshape(SHARDS, 32, -1)[:, :28, :width].reshape(-1)
-
-
-def unpack_up(values, rows):
-    return unwiden(values.reshape(SHARDS, 16, 512)[:, : 2 * rows // SHARDS]).reshape(-1)
 
 
 def local(
@@ -1033,57 +1329,42 @@
     body_in, body_group, body_out, body_down, body_up,
     norm_gain, norm_shift, shortcut_gain, shortcut_shift,
 ):
-    section = lax.axis_index("section")
     n_dp = lax.axis_size("dp")
+    v = n_dp // MEMBERS
+    groups = [[v * member + k for k in range(v)] for member in range(MEMBERS)]
     shards = (
-        entry_in, entry_group, entry_out, entry_down, entry_up, shortcut_weight,
-        body_in, body_group, body_out, body_down, body_up,
+        entry_in, entry_group, shortcut_weight, entry_down, entry_up, entry_out,
+        body_in, body_group, body_down, body_up, body_out,
     )
-    together = lax.all_gather(jnp.concatenate(shards), ("section", "dp"), axis=0, tiled=False)
-    whole = []
-    start = 0
-    for shard in shards:
-        whole.append(together[:, start : start + shard.shape[0]])
-        start += shard.shape[0]
-    gains, shifts, short_gain, short_shift = (
-        lax.all_gather(part, "section", axis=0, tiled=True)
-        for part in (norm_gain, norm_shift, shortcut_gain, shortcut_shift)
+
+    def lines(shard, count):
+        if v > 1:
+            shard = lax.all_gather(shard, "dp", axis_index_groups=groups, axis=0, tiled=True)
+        return jnp.pad(shard, (0, 128 * count - shard.shape[0])).reshape(count, 128)
+
+    results = main_call(
+        n_dp, features, upstream, crop_side, jnp.asarray(lane_maps(), BF16), norm_gain,
+        norm_shift, shortcut_gain[None], shortcut_shift[None],
+        *(lines(shard, count) for shard, count in zip(shards, LINES)),
     )
-    params = jnp.concatenate(
-        [
-            gains.reshape(6, D), shifts.reshape(6, D), short_gain.astype(F32)[None],
-            short_shift.astype(F32)[None], jnp.zeros((2, D), F32),
-        ]
+    output, d_features = results[:2]
+
+    def share(values, shard):
+        values = values.reshape(-1)[: v * shard.shape[0]]
+        if v > 1:
+            values = lax.psum_scatter(
+                values, "dp", scatter_dimension=0, axis_index_groups=groups, tiled=True
+            )
+        return values
+
+    wa0, k0, ws, wd0, wu0, wc0, wa1, k1, wd1, wu1, wc1 = (
+        share(values, shard) for values, shard in zip(results[2:13], shards)
     )
-    expand = jnp.asarray(lane_maps(), BF16)
-    (
-        output, d_features, g_wa0, g_ws, g_k0, g_wc0, g_wd0, g_wu0, g_wa1, g_k1, g_wc1, g_wd1,
-        g_wu1, norms,
-    ) = main_call(
-        n_dp, features, upstream, crop_side, expand, pack_rows(whole[0]), pack_rows(whole[5]),
-        pack_conv(whole[1]), pack_rows(whole[2]), pack_down(whole[3], SE0),
-        pack_up(whole[4], SE0), pack_rows(whole[6]), pack_conv(whole[7]), pack_rows(whole[8]),
-        pack_down(whole[9], SE1), pack_up(whole[10], SE1), widen(params),
+    gains, shifts, short_gain, short_shift = results[13:17]
+    return (
+        output, d_features, wa0, k0, wc0, wd0, wu0, ws, wa1, k1, wc1, wd1, wu1, gains, shifts,
+        short_gain[0], short_shift[0],
     )
-    order = (
-        unpack_rows(g_wa0, 14), unpack_conv(g_k0), unpack_rows(g_wc0, 28),
-        unpack_down(g_wd0, SE0), unpack_up(g_wu0, SE0), unpack_rows(g_ws, 14),
-        unpack_rows(g_wa1, 28), unpack_conv(g_k1), unpack_rows(g_wc1, 28),
-        unpack_down(g_wd1, SE1), unpack_up(g_wu1, SE1),
-    )
-    devices = 2 * n_dp
-    packed = jnp.concatenate([one.reshape(devices, -1) for one in order], 1).astype(F32)
-    summed = lax.psum_scatter(packed, ("section", "dp"), scatter_dimension=0, tiled=False)
-    weight_out = []
-    start = 0
-    for shard in shards:
-        weight_out.append(summed[start : start + shard.shape[0]])
-        start += shard.shape[0]
-    rows = unwiden(norms)
-    own = lambda at: lax.dynamic_slice_in_dim(rows, at + 3 * section, 3, 0)[None]
-    width = shortcut_gain.shape[0]
-    short = lax.dynamic_slice_in_dim(rows[12:14], section * width, width, 1)
-    return (output, d_features, *weight_out, own(0), own(6), short[0], short[1])
 
 
 def solution(mesh):

time: 1240 us -> 311 us (0.25)
  local copies, waits for them, and re-layouts: 552 us -> 26.3 us
  blocking collectives: 314 us -> 0 us
  waiting for transfers between devices: 181 us -> 0 us
  Pallas kernels: 166 us -> 282 us
  between operations: 15.6 us -> 0.77 us
    unnamed x2 -> x0, blocking collectives: 310 us -> none
    another operation x20 -> x0, local copies, waits for them, and re-layouts: 192 us -> none  [the longest x9 101 us: widen(): values = values.reshape(shape[:-1] + (shape[-1] // 28, 28))]
    unnamed x2 -> x0, waiting for transfers between devices: 181 us -> none
    pallas_call x1, Pallas kernels: 166 us -> 282 us  [main_call(): pl.pallas_call(functools.partial(main_kernel, n_dp), out_shape=outs, in_s...]
    unnamed x98 -> x51, local copies, waits for them, and re-layouts: 119 us -> 20.9 us
    reshape x19 -> x2, local copies, waits for them, and re-layouts: 80.7 us -> 2.71 us  [lines(): return jnp.pad(shard, (0, 128 * count - shard.shape[0])).reshape(count, 128)]
    slice x23 -> x0, local copies, waits for them, and re-layouts: 72 us -> none  [the longest x9 44.7 us: unwiden(): values.reshape(shape[:-1] + (shape[-1] // 32, 32))[..., :28]]
    pad x21 -> x0, local copies, waits for them, and re-layouts: 57.3 us -> none  [the longest x10 40.4 us: widen(): values = jnp.pad(values, [(0, 0)] * len(shape) + [(0, 4)])]
  transfers between devices with their start and end apart: 1 -> 0, of which waited for: 1 -> 0; matrix products, arithmetic and copies ran while one was open for 0% -> 0% of each run, Pallas kernels for 0% -> 0%
where the time goes in v3:
time: 311 us; the launch traced here: 309 us
  Pallas kernels  282 us (91%)
  local copies, waits for them, and re-layouts  26.3 us (8%)
    pallas_call x1, Pallas kernels, main_call(): pl.pallas_call(functools.partial(main_kernel, n_dp), out_shape=outs, in_s...  282 us
    unnamed x51, local copies, waits for them, and re-layouts  20.9 us

profile of v3, /device:TPU:0, one launch (start us, length us, event | category | flops | bytes accessed | tf_op | source)
XLA Modules:
  0.0 309.0 jit_solution(8560617951274960057)
XLA Ops:
  0.7 0.0 copy-start.1
  0.7 1.4 broadcast_in_dim.6.short_gain_in
  2.0 1.3 broadcast_in_dim.7.short_shift_in
  3.3 1.3 copy.38.gain_in
  4.6 1.3 copy.39.shift_in
  5.9 1.3 pad_bitcast_fusion.2
  7.2 1.4 pad_bitcast_fusion
  8.6 2.1 copy.37.upstream
  10.7 0.0 copy-done.1
  10.7 1.3 copy.36.features
  12.0 281.9 %shard_map.314 = (bf16[4,7,12544]{2,1,0:T(8,128)(2,1)}, bf16[4,14,12544]{2,1,0:T(8,128)(2,1)}, f32[98,128]{1,0:T(8,128)}, f32[112,128]{1,0:T(8,128)}, f32[98,128...) custom-call(bf16[4,14,12544]{2,1,0:T(8,128)(2,1)} %copy.36.features,, ...), custom_call_target="tpu_custom_call" | custom-call | tf_op jit(solution)/shard_map/pallas_call | solution.py:1314
  293.9 0.0 copy-start
  293.9 2.4 copy.40
  296.3 1.3 copy.42
  297.6 1.3 copy.43
  299.0 0.0 copy-done
  299.0 0.0 copy-start.7
  299.1 1.8 copy.41
  300.9 0.6 copy.57
  301.5 0.6 copy.58
  302.1 0.6 copy.59
  302.8 0.6 copy.60
  303.4 0.6 copy.61
  304.0 0.6 copy.62
  304.6 0.6 copy.63
  305.3 0.6 copy.64
  305.9 0.6 copy.65
  306.6 0.0 copy-done.10
  306.6 0.6 copy.66
  307.2 0.6 copy.67
  307.8 0.6 copy.68
  308.4 0.6 copy.69
  (24 shorter events, 0.0 us)
Async XLA Ops:
  0.7 10.0 %copy-start.1 = (bf16[4,14,12544]{2,0,1:T(4,128)(2,1)S(1)}, bf16[4,14,12544]{2,0,1:T(4,128)(2,1)}, u32[]{:S(2)}) copy-start(bf16[4,14,12544]{2,0,1:T(4,128)(2,1)} %param.19) | copy-start | bytes 4214788
  293.9 5.1 %copy-start = (bf16[4,14,12544]{2,1,0:T(8,128)(2,1)S(1)}, bf16[4,14,12544]{2,1,0:T(8,128)(2,1)}, u32[]{:S(2)}) copy-start(bf16[4,14,12544]{2,1,0:T(8,128)(2,1)} %get-tuple-element.52) | copy-start | bytes 4214788
  296.3 4.6 %copy-start.8 = (f32[98,128]{1,0:T(8,128)S(1)}, f32[98,128]{1,0:T(8,128)}, u32[]{:S(2)}) copy-start(f32[98,128]{1,0:T(8,128)} %get-tuple-element.36) | copy-start | bytes 150532
  296.3 5.2 %copy-start.6 = (f32[112,128]{1,0:T(8,128)S(1)}, f32[112,128]{1,0:T(8,128)}, u32[]{:S(2)}) copy-start(f32[112,128]{1,0:T(8,128)} %get-tuple-element.37) | copy-start | bytes 172036
  299.0 3.2 %copy-start.4 = (f32[196,128]{1,0:T(8,128)S(1)}, f32[196,128]{1,0:T(8,128)}, u32[]{:S(2)}) copy-start(f32[196,128]{1,0:T(8,128)} %get-tuple-element.38) | copy-start | bytes 301060
  299.0 3.8 %copy-start.12 = (f32[28,128]{1,0:T(8,128)S(1)}, f32[28,128]{1,0:T(8,128)}, u32[]{:S(2)}) copy-start(f32[28,128]{1,0:T(8,128)} %get-tuple-element.39) | copy-start | bytes 43012
  299.0 4.4 %copy-start.11 = (f32[28,128]{1,0:T(8,128)S(1)}, f32[28,128]{1,0:T(8,128)}, u32[]{:S(2)}) copy-start(f32[28,128]{1,0:T(8,128)} %get-tuple-element.40) | copy-start | bytes 43012
  299.0 5.0 %copy-start.7 = (f32[98,128]{1,0:T(8,128)S(1)}, f32[98,128]{1,0:T(8,128)}, u32[]{:S(2)}) copy-start(f32[98,128]{1,0:T(8,128)} %get-tuple-element.41) | copy-start | bytes 150532
  299.0 5.6 %copy-start.3 = (f32[196,128]{1,0:T(8,128)S(1)}, f32[196,128]{1,0:T(8,128)}, u32[]{:S(2)}) copy-start(f32[196,128]{1,0:T(8,128)} %get-tuple-element.42) | copy-start | bytes 301060
  299.0 6.3 %copy-start.5 = (f32[112,128]{1,0:T(8,128)S(1)}, f32[112,128]{1,0:T(8,128)}, u32[]{:S(2)}) copy-start(f32[112,128]{1,0:T(8,128)} %get-tuple-element.43) | copy-start | bytes 172036
  299.0 6.9 %copy-start.2 = (f32[196,128]{1,0:T(8,128)S(1)}, f32[196,128]{1,0:T(8,128)}, u32[]{:S(2)}) copy-start(f32[196,128]{1,0:T(8,128)} %get-tuple-element.44) | copy-start | bytes 301060
  299.0 7.5 %copy-start.10 = (f32[49,128]{1,0:T(8,128)S(1)}, f32[49,128]{1,0:T(8,128)}, u32[]{:S(2)}) copy-start(f32[49,128]{1,0:T(8,128)} %get-tuple-element.45) | copy-start | bytes 75268
  299.0 8.2 %copy-start.9 = (f32[49,128]{1,0:T(8,128)S(1)}, f32[49,128]{1,0:T(8,128)}, u32[]{:S(2)}) copy-start(f32[49,128]{1,0:T(8,128)} %get-tuple-element.46) | copy-start | bytes 75268
  299.0 8.8 %copy-start.14 = (f32[1,448]{1,0:T(1,128)S(1)}, f32[1,448]{1,0:T(1,128)}, u32[]{:S(2)}) copy-start(f32[1,448]{1,0:T(1,128)} %get-tuple-element.49) | copy-start | bytes 5380
  299.0 9.3 %copy-start.13 = (f32[1,448]{1,0:T(1,128)S(1)}, f32[1,448]{1,0:T(1,128)}, u32[]{:S(2)}) copy-start(f32[1,448]{1,0:T(1,128)} %get-tuple-element.50) | copy-start | bytes 5380

commit v4 on v3

--- a/solution.py
+++ b/solution.py
@@ -25,12 +25,63 @@
 SHARDS = 32
 ROWS = {
     "wa0": (0, 16), "k0": (16, 16), "ws": (32, 16), "misc0": (48, 16), "wc0": (64, 32),
-    "wa1": (96, 32), "k1": (128, 16), "misc1": (144, 16), "wc1": (160, 32),
+    "k1": (96, 16), "wa1": (112, 32), "misc1": (144, 16), "wc1": (160, 32),
 }
-ORDER = ("wa0", "k0", "ws", "wd0", "wu0", "wc0", "wa1", "k1", "wd1", "wu1", "wc1")
+ORDER = ("wa0", "k0", "ws", "wd0", "wu0", "wc0", "k1", "wa1", "wd1", "wu1", "wc1")
 LINES = (98, 112, 98, 28, 28, 196, 196, 112, 49, 49, 196)
-GATHERS = ((0, 16), (16, 48), (48, 96), (96, 144), (144, 192))
-SCATTERS = ((144, 192), (96, 144), (32, 96), (16, 32), (0, 16))
+GATHERS = ((0, 16), (16, 32), (32, 64), (64, 96), (96, 112), (112, 144), (144, 192))
+SCATTERS = (
+    (144, 192), (96, 112), (112, 144), (64, 96), (32, 64), (16, 32), (0, 16)
+)
+CHAINED = 5
+GATHER_PLAN = {
+    "own": ((0, 0), (1, 0), (2, 0)),
+    "ph1": ((0, 1), (3, 0)),
+    "need_wa0": ((0, 2), (1, 1), (0, 3), (2, 1), (4, 0), (5, 0), (0, 4), (1, 2)),
+    "in0b": ((6, 0),),
+    "in0": ((3, 1),),
+    "in1a": ((2, 2),),
+    "in1b": ((4, 1),),
+    "in1": ((1, 3),),
+    "need_k0": ((1, 4),),
+    "bk0": ((3, 2),),
+    "conv0a": ((5, 1),),
+    "conv1a": ((2, 3),),
+    "conv1": ((4, 2),),
+    "need_ws": ((2, 4),),
+    "str1": ((6, 1),),
+    "need_wc0": ((3, 3), (3, 4), (5, 2)),
+    "gate0": ((4, 3),),
+    "gate1": ((6, 2),),
+    "need_k1": ((4, 4),),
+    "need_wa1": ((5, 3), (5, 4)),
+    "bconv0": ((6, 3),),
+    "need_wc1": ((6, 4),),
+}
+SCATTER_PLAN = {
+    "small1": ((0, 0),),
+    "bback0": ((0, 1),),
+    "k1": ((1, 0),),
+    "bin1a": ((0, 2), (1, 1)),
+    "wa1": ((2, 0),),
+    "eback0": ((0, 3),),
+    "eback1a": ((1, 2), (2, 1)),
+    "wc0": ((3, 0),),
+    "small0": ((4, 0),),
+    "econv0b": ((1, 3),),
+    "econv0": ((0, 4), (2, 2), (3, 1)),
+    "econv1b": ((1, 4),),
+    "econv1": ((2, 3),),
+    "k0": ((5, 0),),
+    "wa0": ((5, 1), (3, 2), (4, 1), (6, 0)),
+    "input0": ((3, 3),),
+    "input1a": ((6, 1),),
+    "emit0": ((2, 4),),
+    "emit1a": ((5, 2),),
+    "tail": (
+        (4, 2), (6, 2), (5, 3), (3, 4), (4, 3), (6, 3), (5, 4), (4, 4), (6, 4),
+    ),
+}
 
 
 def dot(a, b, dims):
@@ -94,10 +145,10 @@
     n_dp, features, upstream, side_ref, expand, gain_in, shift_in, short_gain_in, short_shift_in,
     l_wa0, l_k0, l_ws, l_wd0, l_wu0, l_wc0, l_wa1, l_k1, l_wd1, l_wu1, l_wc1,
     out, grad, o_wa0, o_k0, o_ws, o_wd0, o_wu0, o_wc0, o_wa1, o_k1, o_wd1, o_wu1, o_wc1,
-    gain_out, shift_out, short_gain_out, short_shift_out, land_d, land_c, land_b, land_a,
+    gain_out, shift_out, short_gain_out, short_shift_out,
     inn, pool, u_buf, a0, a1, d_buf, ga, hid, dp_buf, x_buf, up_buf, fs, kd, e_buf,
     w, wd0, wu0, wd1, wu1, stage, params, pair, st, sv, cn, ng, ng_in, ar2, ar4, arv,
-    asend, arecv, vsend, vrecv, xsend, xrecv, lsem, gsend, grecv, rsend, rrecv,
+    asend, arecv, vsend, vrecv, xsend, xrecv, lsem, gsend, grecv, rsend, rrecv, free,
 ):
     section = lax.axis_index("section")
     me = lax.axis_index("dp")
@@ -123,8 +174,6 @@
     if v > 1:
         loop(v - 1, greet_near)
     pl.semaphore_signal(barrier, inc=1, device_id=(other, me), device_id_type=MESH)
-    pl.semaphore_wait(barrier, MEMBERS + v - 1)
-
     def local_copy(src, dst, sem=0):
         return pltpu.make_async_copy(src, dst, lsem.at[sem])
 
@@ -138,27 +187,11 @@
     theirs = pl.ds(2 * other, 2)
     load_map = local_copy(expand.at[1], e_buf, 2)
     copies = [
-        to_sibling(features.at[theirs], x_buf.at[section], 0),
-        to_sibling(upstream.at[theirs], up_buf.at[section], 1),
         local_copy(features.at[mine], x_buf.at[section], 0),
         local_copy(upstream.at[mine], up_buf.at[section], 1),
     ]
-    load_map.start()
-    for copy in copies:
+    for copy in [load_map] + copies:
         copy.start()
-
-    fs[...] = jnp.zeros_like(fs)
-    ng[...] = jnp.zeros_like(ng)
-    guard = jnp.zeros((GUARD, C), BF16)
-    for ref, count in ((a0, 4), (d_buf, 2)):
-        for c in range(2):
-            for k in range(count):
-                ref[c, k, 0:GUARD] = guard
-                ref[c, k, GUARD + PX :] = guard
-    for c in range(2):
-        for ref in (a1, dp_buf):
-            ref[c, 0:GUARD] = guard
-            ref[c, GUARD + PX :] = guard
 
     def dp_of(c):
         return dp_buf[c, GUARD : GUARD + PX]
@@ -418,6 +451,7 @@
             return (sums[0] + fold(pool[c, 7, chunk(j)] * excited),)
 
         d_gate = each_column(1, gate_chunk)[0]
+        poll_crop(c, ("eback" if b == 0 else "bout", "a"))
         gating = sv[b, c, 3:4]
         d_raw = d_gate * gating * (1.0 - gating)
         raw = sv[b, c, 1:2, 0:width]
@@ -573,84 +607,137 @@
         else:
             push_sibling(sent, sent, *sems)
 
-    def add_landed(land, rows, blocks, start, count):
-        def fetch(at):
-            return local_copy(
-                land.at[pl.ds(2 * at, 2), rows],
-                stage.at[pl.ds(2 * (at % 2), 2), pl.ds(0, count)], 3 + at % 2,
-            )
-
-        fetch(0).start()
-        for at in range(len(blocks) // 2):
-            if 2 * at + 2 < len(blocks):
-                fetch(at + 1).start()
-            fetch(at).wait()
-            for near in range(2):
-                def strip(i):
-                    here = pl.ds(pl.multiple_of(start + 16 * i, 16), 16)
-                    there = pl.ds(pl.multiple_of(16 * i, 16), 16)
-                    index = (section, *blocks[2 * at + near], here)
-                    w[index] = (
-                        w[index].astype(F32) + stage[2 * (at % 2) + near, there].astype(F32)
-                    ).astype(BF16)
-
-                loop(count // 16, strip)
+    def poll(point):
+        for k, phase in GATHER_PLAN.get(point, ()):
+            gather(k, phase)
+        for k, phase in SCATTER_PLAN.get(point, ()):
+            scatter(k, phase)
+
+    def poll_crop(c, point):
+        for one in range(2):
+            name = point[0] + str(one) + point[1]
+            if name in GATHER_PLAN or name in SCATTER_PLAN:
+                pl.when(c == one)(lambda: poll(name))
+
+    def crops(body, point=None):
+        def run(c):
+            body(c)
+            if point is not None:
+                poll_crop(c, (point, ""))
+
+        loop(2, run)
+
+    def landing(k, phase, block, count):
+        last = k - CHAINED
+        if phase == 0:
+            if k < 4:
+                return e_buf.at[pl.ds(pl.multiple_of(block * count, 16), count)]
+            ref = a1 if k == 4 else hid if last == 0 else ga.at[0]
+            return ref.at[
+                block // 8, pl.ds(pl.multiple_of(lax.rem(block, 8) * count, 16), count)
+            ]
+        if phase == 1:
+            if last < 0:
+                return ga.at[1, block // 4, pl.ds(block % 4 * count, count)]
+            ref = hid if last == 0 else ga.at[0]
+            return ref.at[block // 4, pl.ds(128 + block % 4 * 16, 16)]
+        if phase == 2:
+            if last < 0:
+                return wu1.at[pl.ds(block * count, count)]
+            ref = ga.at[0] if last == 0 else hid
+            return ref.at[block // 2, pl.ds(192 + block % 2 * 16, 16)]
+        if last >= 0:
+            return wu0.at[pl.ds(64 * last + 16 * block, 16)]
+        if k % 2:
+            return wu1.at[pl.ds(160 + block * count, count)]
+        return stage.at[block, pl.ds(0, count)]
+
+    def landed(k, phase, count):
+        return w.at[section, pl.ds(0, (4, 2, 1, 1)[phase]), pl.ds(0, (4, 4, 4, 3)[phase]), pl.ds(0, count)]
+
+    def add_landed(k, phase, block, place_of, start, count):
+        ref = landing(k, phase, block, count)
+        index = (section, *place_of(block), pl.ds(start, count))
+        w[index] = (w[index].astype(F32) + ref[...].astype(F32)).astype(BF16)
+
+    def credit(at, to):
+        pl.semaphore_signal(
+            free.at[at], inc=1, device_id=(section, to * v + rest), device_id_type=MESH
+        )
+
+    def credit_sibling(at):
+        pl.semaphore_signal(free.at[at], inc=1, device_id=(other, me), device_id_type=MESH)
+
+    def credit_z(at):
+        for hop in range(1, 4):
+            credit(at, lax.rem(z + hop, 4) * 4 + yx)
 
     def scatter(k, phase):
         start, stop = SCATTERS[k]
         count = stop - start
         rows = pl.ds(start, count)
-        part = w.at[section, :, :, rows]
         first, second = flip(bits[1]), flip(bits[0])
+        more = k + 1 < CHAINED
+        if phase > 0:
+            arrive(landed(k, phase - 1, count), rrecv.at[k, phase - 1])
         if phase == 1:
-            arrive(land_d.at[:, rows], rrecv.at[k, 0])
-            blocks = [(zz, near) for zz in range(4) for near in range(4)]
-            add_landed(land_d, rows, blocks, start, count)
+            loop(16, lambda b: add_landed(k, 0, b, lambda b: (b // 4, lax.rem(b, 4)), start, count))
+            if k < 3:
+                credit_sibling(0)
         elif phase == 2:
-            arrive(land_c.at[:, rows], rrecv.at[k, 1])
-            blocks = [(zz, near) for zz in range(4) for near in (yx, second)]
-            add_landed(land_c, rows, blocks, start, count)
+            for b in range(8):
+                add_landed(k, 1, b, lambda b: (b // 2, yx if b % 2 == 0 else second), start, count)
+            if more:
+                credit(1, z * 4 + first)
         elif phase == 3:
-            arrive(land_b.at[:, rows], rrecv.at[k, 2])
-            add_landed(land_b, rows, [(zz, yx) for zz in range(4)], start, count)
+            for b in range(4):
+                add_landed(k, 2, b, lambda b: (b, yx), start, count)
+            if more:
+                credit(2, z * 4 + second)
+            if k == 0:
+                credit_z(5)
         elif phase == 4:
-            arrive(land_a.at[pl.ds(0, 3), rows], rrecv.at[k, 3])
-            copies = [
-                local_copy(land_a.at[at, rows], stage.at[at, pl.ds(0, count)], 3 + at)
-                for at in range(3)
-            ]
-            for copy in copies:
-                copy.start()
             total = w[section, z, yx, start:stop].astype(F32)
-            for at in range(3):
-                copies[at].wait()
-                total = total + stage[at, 0:count].astype(F32)
-            pool[0, 4, start:stop] = total
-            arrive(land_d.at[:, rows], rsend.at[k, 0])
-            arrive(land_c.at[:, rows], rsend.at[k, 1])
-            arrive(land_b.at[:, rows], rsend.at[k, 2])
-            arrive(land_a.at[pl.ds(0, 3), rows], rsend.at[k, 3])
+            for b in range(3):
+                total = total + landing(k, 3, b, count)[...].astype(F32)
+            pool[0, 1, start:stop] = total
+            if k + 2 < CHAINED:
+                credit_z(5 if k % 2 else 3)
+            for sent in range(4):
+                arrive(landed(k, sent, count), rsend.at[k, sent])
             return
         sems = (rsend.at[k, phase], rrecv.at[k, phase])
         if phase == 0:
-            for zz in range(4):
-                push_sibling(w.at[other, zz, :, rows], land_d.at[pl.ds(4 * zz, 4), rows], *sems)
+            if k < 4 or k == CHAINED:
+                pl.semaphore_wait(free.at[0 if k < 4 else 4], 1)
+
+            def send(b):
+                push_sibling(
+                    w.at[other, b // 4, lax.rem(b, 4), rows], landing(k, 0, b, count), *sems
+                )
+
+            loop(16, send)
         elif phase == 1:
-            for zz in range(4):
-                to = z * 4 + first
-                push(w.at[section, zz, first, rows], land_c.at[2 * zz, rows], to, *sems)
+            if k < CHAINED:
+                pl.semaphore_wait(free.at[1], 1)
+            for b in range(8):
+                to = first if b % 2 == 0 else first + second - yx
                 push(
-                    w.at[section, zz, first + second - yx, rows], land_c.at[2 * zz + 1, rows], to,
-                    *sems,
+                    w.at[section, b // 2, to, rows], landing(k, 1, b, count), z * 4 + first, *sems
                 )
         elif phase == 2:
-            push(part.at[:, second], land_b.at[:, rows], z * 4 + second, *sems)
+            if k < CHAINED:
+                pl.semaphore_wait(free.at[2], 1)
+            for b in range(4):
+                push(
+                    w.at[section, b, second, rows], landing(k, 2, b, count), z * 4 + second, *sems
+                )
         else:
+            if k < CHAINED:
+                pl.semaphore_wait(free.at[5 if k % 2 else 3], 3)
             for hop in range(1, 4):
                 to = lax.rem(z + hop, 4)
-                push(
-                    w.at[section, to, yx, rows], land_a.at[hop - 1, rows], to * 4 + yx, *sems
-                )
+                push(w.at[section, to, yx, rows], landing(k, 3, hop - 1, count), to * 4 + yx, *sems)
 
     shares = {}
     at = 0
@@ -671,14 +758,34 @@
     for n in range(4):
         lanes = slice(256 * n, 256 * n + 256)
         w[section, z, yx, :, lanes] = nn(own_rows, e_buf[:, lanes]).astype(BF16)
-    gather(0, 0)
-    gather(1, 0)
+    pl.semaphore_wait(barrier, MEMBERS + v - 1)
+    poll("own")
+    exchange = [
+        to_sibling(upstream.at[theirs], up_buf.at[section], 1),
+        to_sibling(features.at[theirs], x_buf.at[section], 0),
+    ]
+    for copy in exchange:
+        copy.start()
+    copies = exchange + copies
+    ng[...] = jnp.zeros_like(ng)
+    guard = jnp.zeros((GUARD, C), BF16)
+    for ref, count in ((a0, 4), (d_buf, 2)):
+        for c in range(2):
+            for k in range(count):
+                ref[c, k, 0:GUARD] = guard
+                ref[c, k, GUARD + PX :] = guard
+    for c in range(2):
+        for ref in (a1, dp_buf):
+            ref[c, 0:GUARD] = guard
+            ref[c, GUARD + PX :] = guard
 
     halves = jnp.concatenate(
         [short_gain_in[...].astype(F32), short_shift_in[...].astype(F32)], 1
     )
     pair[section] = jnp.concatenate(
-        [gain_in[0], shift_in[0], halves, jnp.zeros((1, D), F32)], 0
+        [gain_in[k] for k in range(3)] + [shift_in[k] for k in range(3)]
+        + [halves, jnp.zeros((1, D), F32)],
+        0,
     )
     swap = to_sibling(pair.at[section], pair.at[section], 3)
     swap.start()
@@ -702,8 +809,7 @@
 
     wide = nn(thirds(rows), e_buf[...])
     params[...] = wide[0:16] + wide[16:32] + wide[32:48]
-    gather(0, 1)
-    gather(2, 0)
+    poll("params")
 
     for copy in copies:
         copy.wait()
@@ -725,11 +831,9 @@
                         16 * j : 16 * j + count
                     ]
 
-    loop(2, cotangent)
+    crops(cotangent, "cot")
     load_map = local_copy(expand.at[0], e_buf, 2)
     load_map.start()
-    gather(0, 2)
-    gather(1, 1)
     fs[...] = jnp.zeros_like(fs)
     load_map.wait()
 
@@ -752,16 +856,10 @@
 
             loop(14, take)
 
-    phases(0)
-    gather(0, 3)
-    gather(1, 2)
-    gather(3, 0)
-    phases(1)
+    crops(phases, "ph")
     load_map = local_copy(expand.at[1], e_buf, 2)
     load_map.start()
-    gather(0, 4)
-    gather(1, 3)
-    gather(2, 1)
+    poll("need_wa0")
 
     def entry_inner(c):
         for q in range(2):
@@ -772,6 +870,7 @@
                     )
 
                 loop(4, product)
+            poll_crop(c, ("in", "ab"[q]))
 
         def body(j, sums):
             mask = keep(c, j)
@@ -787,13 +886,10 @@
         own = jnp.zeros((1, C), F32) + crop_count(c)
         ar_start(0, c, [sums[0], sums[1], own, own])
 
-    loop(2, entry_inner)
-    gather(2, 2)
-    gather(4, 0)
-    gather(1, 4)
+    crops(entry_inner, "in")
+    poll("need_k0")
     build_conv("k0")
-    gather(2, 3)
-    gather(3, 1)
+    poll("bk0")
 
     def entry_conv(c):
         totals = ar_wait(0, c, 4)
@@ -815,6 +911,8 @@
 
         loop(14, activate)
 
+        poll_crop(c, ("conv", "a"))
+
         def convolve(n):
             patches = []
             for tap, q, r, ta, tb in taps0():
@@ -826,7 +924,8 @@
         loop(4, convolve)
         ar_start(1, c, moment_sums(c, lambda j: pool[c, 0, chunk(j)]))
 
-    loop(2, entry_conv)
+    crops(entry_conv, "conv")
+    poll("need_ws")
 
     def strided(c):
         def product(n):
@@ -834,11 +933,9 @@
 
         loop(4, product)
 
-    loop(2, strided)
-    gather(2, 4)
-    gather(3, 2)
-    gather(4, 1)
+    crops(strided, "str")
     build_small(0)
+    poll("need_wc0")
 
     def entry_gate(c):
         totals = ar_wait(1, c, 2)
@@ -846,11 +943,10 @@
         sums = gate(c, 0, 1, 0, wd0, wu0, "wc0", 1)
         ar_start(2, c, sums + moment_sums(c, lambda j: pool[c, 2, chunk(j)]))
 
-    loop(2, entry_gate)
-    gather(3, 3)
-    gather(4, 2)
-    gather(3, 4)
+    crops(entry_gate, "gate")
+    poll("need_k1")
     build_conv("k1")
+    poll("need_wa1")
 
     def entry_pre(c, j):
         a, shift = affine(c, 2)
@@ -876,7 +972,7 @@
         loop(4, product)
         ar_start(3, c, moment_sums(c, lambda j: pool[c, 4, chunk(j)]))
 
-    loop(2, entry_out)
+    crops(entry_out, "out")
 
     def body_conv(c):
         set_stats(c, 4, ar_wait(3, c, 2), inverse_out(c), 3)
@@ -901,9 +997,8 @@
         loop(4, convolve)
         ar_start(4, c, moment_sums(c, lambda j: pool[c, 5, chunk(j)]))
 
-    loop(2, body_conv)
-    gather(4, 3)
-    gather(4, 4)
+    crops(body_conv, "bconv")
+    poll("need_wc1")
     build_small(1)
 
     def body_gate(c):
@@ -950,10 +1045,11 @@
     out_copies = [
         to_sibling(up_buf.at[other], out.at[mine], 2),
         local_copy(up_buf.at[section], out.at[mine], 1),
-        local_copy(expand.at[0], e_buf, 2),
     ]
     for copy in out_copies:
         copy.start()
+
+    credit_sibling(0)
 
     def body_back_out(c):
         a, slope, offset = norm_coefficients(c, 6, ar_wait(6, c, 2), inverse_out(c), 5, 0)
@@ -967,10 +1063,13 @@
         loop(14, project)
         ar_start(7, c, ungate(c, 1, 5, 5, wd1, wu1, "wc1"))
 
-    loop(2, body_back_out)
+    crops(body_back_out, "bout")
+    credit(2, z * 4 + flip(bits[0]))
+    credit_z(3)
     outer(lambda c, l: ga[1, c, :, l], dp_of, "wc1")
+    credit(1, z * 4 + flip(bits[1]))
     small_grads(1)
-    scatter(0, 0)
+    poll("small1")
 
     def conv_cotangent(c, index, conv_k, a, slope, offset, versions):
         def body(j):
@@ -1003,6 +1102,7 @@
             pool[c, 7, :, col(n)] = total
 
         loop(4, back)
+        poll_crop(c, ("bback", "a"))
         a, shift = affine(c, 4)
         center, scaling = hat_of(c, 4)
 
@@ -1015,9 +1115,9 @@
 
         ar_start(8, c, each_column(2, body))
 
-    loop(2, body_back_conv)
+    crops(body_back_conv, "bback")
     conv_grad(lambda c, tap, l: a1[c, GUARD : GUARD + PX, l], v_body, "k1")
-    scatter(0, 1)
+    poll("k1")
 
     def body_back_in(c):
         a, slope, offset = norm_coefficients(c, 4, ar_wait(8, c, 2), inverse_out(c), 3, 0)
@@ -1035,6 +1135,7 @@
             )
 
         loop(4, back)
+        poll_crop(c, ("bin", "a"))
         center, scaling = hat_of(c, 2)
         short_center, short_scaling = hat_of(c, 3)
 
@@ -1051,10 +1152,9 @@
         sums = each_column(3, pre)
         ar_start(9, c, sums + [sums[0]])
 
-    loop(2, body_back_in)
+    crops(body_back_in, "bin")
     outer(lambda c, l: hid[c, :, l], dp_of, "wa1")
-    scatter(1, 0)
-    scatter(0, 2)
+    poll("wa1")
     build_conv("k0")
 
     def entry_back_out(c):
@@ -1080,13 +1180,13 @@
         loop(2, back)
         ar_start(10, c, ungate(c, 0, 1, 0, wd0, wu0, "wc0"))
 
-    loop(2, entry_back_out)
+    crops(entry_back_out, "eback")
     outer(lambda c, l: ga[0, c, :, l], dp_of, "wc0")
+    poll("wc0")
     outer(lambda c, l: u_buf[c, 0, :, l], lambda c: hid[c], "ws")
+    credit_sibling(4)
     small_grads(0)
-    scatter(2, 0)
-    scatter(1, 1)
-    scatter(0, 3)
+    poll("small0")
 
     def entry_back_conv(c):
         a, slope, offset = norm_coefficients(c, 1, ar_wait(10, c, 2), inverse_out(c), 1, 0)
@@ -1102,6 +1202,7 @@
                     pool[c, 4 + 2 * q + r, :, col(n)] = total
 
                 loop(4, back)
+            poll_crop(c, ("econv", "ab"[q]))
         a, shift = affine(c, 0)
         center, scaling = hat_of(c, 0)
 
@@ -1119,7 +1220,7 @@
 
         ar_start(11, c, each_column(2, body))
 
-    loop(2, entry_back_conv)
+    crops(entry_back_conv, "econv")
 
     def act_entry(c, tap, lanes):
         q = 0 if tap // 3 == 1 else 1
@@ -1127,9 +1228,9 @@
         return a0[c, 2 * q + r, GUARD : GUARD + PX, lanes]
 
     conv_grad(act_entry, v_entry, "k0")
-    scatter(3, 0)
-    scatter(2, 1)
-    scatter(1, 2)
+    poll("k0")
+    load_map = local_copy(expand.at[0], e_buf, 2)
+    load_map.start()
     for copy in out_copies:
         copy.wait()
 
@@ -1146,7 +1247,6 @@
         loop(14, body)
 
     loop(2, entry_back_in)
-    scatter(0, 4)
     swap = to_sibling(ng, ng_in, 3)
     swap.start()
 
@@ -1162,26 +1262,28 @@
                 total = term if total is None else total + term
         return total
 
+    def input_block(m):
+        dp_buf[m] = rows_of("wa0", m)
+        put_rows("wa0", m, input_grad(m))
+
+    loop(2, input_block)
+    poll("wa0")
+
     def entry_back_input(c):
         for q in range(2):
             for r in range(2):
                 def back(n):
-                    total = nt(a0[c, 2 * q + r, GUARD : GUARD + PX], rows_of("wa0", n))
+                    total = nt(a0[c, 2 * q + r, GUARD : GUARD + PX], dp_buf[n])
                     if q == 0 and r == 0:
                         total = total + pool[c, 2, :, col(n)]
                     at = pl.ds(pl.multiple_of(512 * r + 256 * n, 256), 256)
                     d_buf[c, q, 0:PX, at] = total.astype(BF16)
 
                 loop(2, back)
-
-    loop(2, entry_back_input)
-
-    def input_block(m):
-        put_rows("wa0", m, input_grad(m))
-
-    loop(2, input_block)
-    scatter(4, 0)
-    scatter(3, 1)
+            if q == 0:
+                poll_crop(c, ("input", "a"))
+
+    crops(entry_back_input, "input")
 
     def entry_emit(c):
         for q in range(2):
@@ -1193,6 +1295,7 @@
                         ]
 
             narrow(d_buf[c, q, 0:PX], store)
+        poll_crop(c, ("emit", "a"))
         for h in range(2):
             for j in range(OUT):
                 for k in range(7):
@@ -1200,12 +1303,8 @@
                         512 * k + 32 * j + 14 * h : 512 * k + 32 * j + 14 * h + 14
                     ].astype(BF16)
 
-    entry_emit(0)
-    scatter(4, 1)
-    scatter(3, 2)
-    scatter(2, 2)
-    scatter(1, 3)
-    entry_emit(1)
+    load_map.wait()
+    crops(entry_emit, "emit")
     load_map = local_copy(expand.at[1], e_buf, 2)
     load_map.start()
     last = [
@@ -1214,14 +1313,7 @@
     ]
     for copy in last:
         copy.start()
-    scatter(4, 2)
-    scatter(3, 3)
-    scatter(2, 3)
-    scatter(1, 4)
-    scatter(4, 3)
-    scatter(2, 4)
-    scatter(3, 4)
-    scatter(4, 4)
+    poll("tail")
     load_map.wait()
     swap.wait()
     total = thirds(ng[...] + ng_in[...])
@@ -1231,11 +1323,12 @@
     def own(top, low):
         return jnp.where(section == 0, top, low)
 
-    gain_out[0] = own(total[0:3], total[3:6])
-    shift_out[0] = own(total[6:9], total[9:12])
+    for k in range(3):
+        gain_out[k] = own(total[k : k + 1], total[k + 3 : k + 4])
+        shift_out[k] = own(total[k + 6 : k + 7], total[k + 9 : k + 10])
     short_gain_out[...] = own(total[12:13, 0:DIN], total[12:13, DIN:])
     short_shift_out[...] = own(total[13:14, 0:DIN], total[13:14, DIN:])
-    total = pool[0, 4, 0:192]
+    total = pool[0, 1, 0:192]
     high = total.astype(BF16)
     low = (total - high.astype(F32)).astype(BF16)
     final = nt(high, e_buf[...]) + nt(low, e_buf[...])
@@ -1272,9 +1365,8 @@
     flat = [shape(count, 128, dtype=F32) for count in LINES]
     outs = [
         shape(4, 7, 12544), shape(4, 14, 12544), *flat,
-        shape(1, 3, D, dtype=F32), shape(1, 3, D, dtype=F32),
+        shape(3, 1, D, dtype=F32), shape(3, 1, D, dtype=F32),
         shape(1, DIN, dtype=F32), shape(1, DIN, dtype=F32),
-        shape(16, 192, C), shape(8, 192, C), shape(4, 192, C), shape(3, 192, C),
     ]
     dma = pltpu.SemaphoreType.DMA
     scratch = [
@@ -1297,7 +1389,7 @@
         pltpu.VMEM((128, C), BF16),
         pltpu.VMEM((C, 256), BF16),
         pltpu.VMEM((256, C), BF16),
-        pltpu.VMEM((4, 64, C), BF16),
+        pltpu.VMEM((3, 48, C), BF16),
         pltpu.VMEM((16, C), F32),
         pltpu.VMEM((2, 8, D), F32),
         pltpu.VMEM((2, 7, 8, C), F32),
@@ -1308,14 +1400,14 @@
         pltpu.VMEM((2, 2, MEMBERS, 2, C), F32),
         pltpu.VMEM((2, MEMBERS, 4, C), F32),
         pltpu.VMEM((2, 2, v, 4, C), F32),
-        dma((2, 2)), dma((2, 2)), dma((2, 2)), dma((2, 2)), dma((5,)), dma((5,)), dma((6,)),
-        dma((5, 4)), dma((5, 4)), dma((5, 4)), dma((5, 4)),
+        dma((2, 2)), dma((2, 2)), dma((2, 2)), dma((2, 2)), dma((5,)), dma((5,)), dma((4,)),
+        dma((7, 4)), dma((7, 4)), dma((7, 4)), dma((7, 4)), pltpu.SemaphoreType.REGULAR((6,)),
     ]
     return pl.pallas_call(
         functools.partial(main_kernel, n_dp),
         out_shape=outs,
         in_specs=[any_space, any_space, smem, any_space] + [vmem] * 15,
-        out_specs=[any_space] * 2 + [vmem] * 15 + [any_space] * 4,
+        out_specs=[any_space] * 2 + [vmem] * 15,
         scratch_shapes=scratch,
         compiler_params=pltpu.CompilerParams(
             collective_id=1, has_side_effects=True, vmem_limit_bytes=64 << 20
@@ -1343,8 +1435,9 @@
         return jnp.pad(shard, (0, 128 * count - shard.shape[0])).reshape(count, 128)
 
     results = main_call(
-        n_dp, features, upstream, crop_side, jnp.asarray(lane_maps(), BF16), norm_gain,
-        norm_shift, shortcut_gain[None], shortcut_shift[None],
+        n_dp, features, upstream, crop_side, jnp.asarray(lane_maps(), BF16),
+        norm_gain.transpose(1, 0, 2), norm_shift.transpose(1, 0, 2), shortcut_gain[None],
+        shortcut_shift[None],
         *(lines(shard, count) for shard, count in zip(shards, LINES)),
     )
     output, d_features = results[:2]
@@ -1362,7 +1455,8 @@
     )
     gains, shifts, short_gain, short_shift = results[13:17]
     return (
-        output, d_features, wa0, k0, wc0, wd0, wu0, ws, wa1, k1, wc1, wd1, wu1, gains, shifts,
+        output, d_features, wa0, k0, wc0, wd0, wu0, ws, wa1, k1, wc1, wd1, wu1,
+        gains.transpose(1, 0, 2), shifts.transpose(1, 0, 2),
         short_gain[0], short_shift[0],
     )
 

time: 311 us -> 256 us (0.82)
  Pallas kernels: 282 us -> 231 us
    pallas_call x1, Pallas kernels: 282 us -> 231 us  [main_call(): pl.pallas_call(functools.partial(main_kernel, n_dp), out_shape=outs, in_s...]
where the time goes in v4:
time: 256 us
  Pallas kernels  231 us (90%)
  local copies, waits for them, and re-layouts  23.7 us (9%)
    pallas_call x1, Pallas kernels, main_call(): pl.pallas_call(functools.partial(main_kernel, n_dp), out_shape=outs, in_s...  231 us
    unnamed x51, local copies, waits for them, and re-layouts  18.4 us

profile of v4, /device:TPU:0, one launch (start us, length us, event | category | flops | bytes accessed | tf_op | source)
XLA Modules:
  0.0 255.9 jit_solution(12355831304148680370)
XLA Ops:
  0.7 1.4 broadcast_in_dim.6.short_gain_in
  2.0 1.3 broadcast_in_dim.7.short_shift_in
  3.3 1.3 pad_bitcast_fusion.2
  4.6 1.4 pad_bitcast_fusion
  6.0 2.1 copy.37.upstream
  8.1 1.3 copy.36.features
  9.4 231.3 %shard_map.314 = (bf16[4,7,12544]{2,1,0:T(8,128)(2,1)}, bf16[4,14,12544]{2,1,0:T(8,128)(2,1)}, f32[98,128]{1,0:T(8,128)}, f32[112,128]{1,0:T(8,128)}, f32[98,128...) custom-call(bf16[4,14,12544]{2,1,0:T(8,128)(2,1)} %copy.36.features,, ...), custom_call_target="tpu_custom_call" | custom-call | tf_op jit(solution)/shard_map/pallas_call | solution.py:1406
  240.8 2.3 copy.38
  243.1 0.0 copy-start.10
  243.1 0.0 copy-start.6
  243.1 0.0 copy-start.2
  243.1 0.0 copy-start.4
  243.1 0.0 copy-start.1
  243.1 0.0 copy-start.9
  243.1 0.0 copy-start.8
  243.1 0.0 copy-start.13
  243.2 3.4 %copy.39 = bf16[4,14,12544]{2,0,1:T(4,128)(2,1)} copy(bf16[4,14,12544]{2,1,0:T(8,128)(2,1)} %get-tuple-element.52) | data formatting | bytes 2809856
  246.6 0.6 copy.55
  247.2 0.6 copy.56
  247.8 0.6 copy.57
  248.5 0.6 copy.58
  249.1 0.6 copy.59
  249.7 0.6 copy.60
  250.3 0.6 copy.61
  251.0 0.6 copy.62
  251.6 0.6 copy.63
  252.3 0.6 copy.64
  252.9 0.6 copy.65
  253.5 0.6 copy.66
  254.1 0.6 copy.67
  254.7 0.6 copy.68
  255.3 0.6 copy.69
  (24 shorter events, 0.0 us)
Async XLA Ops:
  0.7 7.4 %copy-start = (bf16[4,14,12544]{2,0,1:T(4,128)(2,1)S(1)}, bf16[4,14,12544]{2,0,1:T(4,128)(2,1)}, u32[]{:S(2)}) copy-start(bf16[4,14,12544]{2,0,1:T(4,128)(2,1)} %param.19) | copy-start | bytes 4214788
  243.0 3.5 %copy-start.7 = (f32[98,128]{1,0:T(8,128)S(1)}, f32[98,128]{1,0:T(8,128)}, u32[]{:S(2)}) copy-start(f32[98,128]{1,0:T(8,128)} %get-tuple-element.36) | copy-start | bytes 150532
  243.0 4.2 %copy-start.5 = (f32[112,128]{1,0:T(8,128)S(1)}, f32[112,128]{1,0:T(8,128)}, u32[]{:S(2)}) copy-start(f32[112,128]{1,0:T(8,128)} %get-tuple-element.37) | copy-start | bytes 172036
  243.0 4.8 %copy-start.3 = (f32[196,128]{1,0:T(8,128)S(1)}, f32[196,128]{1,0:T(8,128)}, u32[]{:S(2)}) copy-start(f32[196,128]{1,0:T(8,128)} %get-tuple-element.38) | copy-start | bytes 301060
  243.0 5.4 %copy-start.11 = (f32[28,128]{1,0:T(8,128)S(1)}, f32[28,128]{1,0:T(8,128)}, u32[]{:S(2)}) copy-start(f32[28,128]{1,0:T(8,128)} %get-tuple-element.39) | copy-start | bytes 43012
  243.1 6.0 %copy-start.10 = (f32[28,128]{1,0:T(8,128)S(1)}, f32[28,128]{1,0:T(8,128)}, u32[]{:S(2)}) copy-start(f32[28,128]{1,0:T(8,128)} %get-tuple-element.40) | copy-start | bytes 43012
  243.1 6.6 %copy-start.6 = (f32[98,128]{1,0:T(8,128)S(1)}, f32[98,128]{1,0:T(8,128)}, u32[]{:S(2)}) copy-start(f32[98,128]{1,0:T(8,128)} %get-tuple-element.41) | copy-start | bytes 150532
  243.1 7.3 %copy-start.2 = (f32[196,128]{1,0:T(8,128)S(1)}, f32[196,128]{1,0:T(8,128)}, u32[]{:S(2)}) copy-start(f32[196,128]{1,0:T(8,128)} %get-tuple-element.42) | copy-start | bytes 301060
  243.1 7.9 %copy-start.4 = (f32[112,128]{1,0:T(8,128)S(1)}, f32[112,128]{1,0:T(8,128)}, u32[]{:S(2)}) copy-start(f32[112,128]{1,0:T(8,128)} %get-tuple-element.43) | copy-start | bytes 172036
  243.1 8.5 %copy-start.1 = (f32[196,128]{1,0:T(8,128)S(1)}, f32[196,128]{1,0:T(8,128)}, u32[]{:S(2)}) copy-start(f32[196,128]{1,0:T(8,128)} %get-tuple-element.44) | copy-start | bytes 301060
  243.1 9.2 %copy-start.9 = (f32[49,128]{1,0:T(8,128)S(1)}, f32[49,128]{1,0:T(8,128)}, u32[]{:S(2)}) copy-start(f32[49,128]{1,0:T(8,128)} %get-tuple-element.45) | copy-start | bytes 75268
  243.1 9.8 %copy-start.8 = (f32[49,128]{1,0:T(8,128)S(1)}, f32[49,128]{1,0:T(8,128)}, u32[]{:S(2)}) copy-start(f32[49,128]{1,0:T(8,128)} %get-tuple-element.46) | copy-start | bytes 75268
  243.1 10.4 %copy-start.13 = (f32[3,1,896]{2,1,0:T(1,128)S(1)}, f32[3,1,896]{2,1,0:T(1,128)}, u32[]{:S(2)}) copy-start(f32[3,1,896]{2,1,0:T(1,128)} %get-tuple-element.47) | copy-start | bytes 32260
  243.1 11.0 %copy-start.12 = (f32[3,1,896]{2,1,0:T(1,128)S(1)}, f32[3,1,896]{2,1,0:T(1,128)}, u32[]{:S(2)}) copy-start(f32[3,1,896]{2,1,0:T(1,128)} %get-tuple-element.48) | copy-start | bytes 32260
  243.1 11.6 %copy-start.15 = (f32[1,448]{1,0:T(1,128)S(1)}, f32[1,448]{1,0:T(1,128)}, u32[]{:S(2)}) copy-start(f32[1,448]{1,0:T(1,128)} %get-tuple-element.49) | copy-start | bytes 5380
  243.2 12.1 %copy-start.14 = (f32[1,448]{1,0:T(1,128)S(1)}, f32[1,448]{1,0:T(1,128)}, u32[]{:S(2)}) copy-start(f32[1,448]{1,0:T(1,128)} %get-tuple-element.50) | copy-start | bytes 5380

commit v5 on v4

--- a/solution.py
+++ b/solution.py
@@ -142,14 +142,27 @@
 
 
 def main_kernel(
-    n_dp, features, upstream, side_ref, expand, gain_in, shift_in, short_gain_in, short_shift_in,
+    n_dp, features, upstream, side_ref, expand, gain_in, shift_in, short_in,
     l_wa0, l_k0, l_ws, l_wd0, l_wu0, l_wc0, l_wa1, l_k1, l_wd1, l_wu1, l_wc1,
-    out, grad, o_wa0, o_k0, o_ws, o_wd0, o_wu0, o_wc0, o_wa1, o_k1, o_wd1, o_wu1, o_wc1,
-    gain_out, shift_out, short_gain_out, short_shift_out,
+    out, grad, result,
     inn, pool, u_buf, a0, a1, d_buf, ga, hid, dp_buf, x_buf, up_buf, fs, kd, e_buf,
-    w, wd0, wu0, wd1, wu1, stage, params, pair, st, sv, cn, ng, ng_in, ar2, ar4, arv,
-    asend, arecv, vsend, vrecv, xsend, xrecv, lsem, gsend, grecv, rsend, rrecv, free,
+    w, wd0, wu0, wd1, wu1, stage, params, pair, st, sv, cn, ng, ng_in, ar2, ar4, arh, arv,
+    v_gain, v_shift, v_short, v_wa0, v_k0, v_ws, v_wd0, v_wu0, v_wc0, v_wa1, v_k1, v_wd1, v_wu1,
+    v_wc1, isem, asend, arecv, vsend, vrecv, xsend, xrecv, lsem, gsend, grecv, rsend, rrecv, free,
 ):
+    loads = [
+        pltpu.make_async_copy(src, dst, isem.at[at])
+        for at, (src, dst) in enumerate(
+            (
+                (l_wa0, v_wa0), (l_k0, v_k0), (l_ws, v_ws), (l_wd0, v_wd0), (l_wu0, v_wu0),
+                (l_wc0, v_wc0), (l_wa1, v_wa1), (l_k1, v_k1), (l_wd1, v_wd1), (l_wu1, v_wu1),
+                (l_wc1, v_wc1), (gain_in, v_gain), (shift_in, v_shift), (short_in, v_short),
+            )
+        )
+    ]
+    load_map = pltpu.make_async_copy(expand.at[1], e_buf, isem.at[14])
+    for copy in loads + [load_map]:
+        copy.start()
     section = lax.axis_index("section")
     me = lax.axis_index("dp")
     v = n_dp // MEMBERS
@@ -185,12 +198,11 @@
 
     mine = pl.ds(2 * section, 2)
     theirs = pl.ds(2 * other, 2)
-    load_map = local_copy(expand.at[1], e_buf, 2)
     copies = [
         local_copy(features.at[mine], x_buf.at[section], 0),
         local_copy(upstream.at[mine], up_buf.at[section], 1),
     ]
-    for copy in [load_map] + copies:
+    for copy in copies:
         copy.start()
 
     def dp_of(c):
@@ -209,12 +221,20 @@
         half = half_side(c)
         return (half * half).astype(F32)
 
-    def ar_slots(rows, n):
-        return ar2.at[n % 2] if rows == 2 else ar4
+    def ar_slots(n, c):
+        if n >= 6:
+            return arh.at[n % 2, c, :, pl.ds(0, 32 if n == 9 else 16)]
+        return ar4.at[c] if n == 2 else ar2.at[n % 2, c]
 
     def ar_start(n, c, rows):
-        slots = ar_slots(len(rows), n).at[c]
-        slots[digit] = jnp.concatenate(rows, 0)
+        slots = ar_slots(n, c)
+        if n >= 6:
+            tiles = [row[:, 128 * k : 128 * k + 128] for row in rows for k in range(8)]
+            if n == 9:
+                tiles.append(jnp.zeros((8, 128), F32))
+            slots[digit] = jnp.concatenate(tiles, 0).astype(BF16)
+        else:
+            slots[digit] = jnp.concatenate(rows, 0)
 
         def send(hop):
             pltpu.make_async_remote_copy(
@@ -226,13 +246,21 @@
         loop(MEMBERS - 1, send)
 
     def ar_wait(n, c, rows):
-        slots = ar_slots(rows, n).at[c]
+        slots = ar_slots(n, c)
         arrived = slots.at[pl.ds(0, MEMBERS - 1)]
         pltpu.make_async_copy(arrived, arrived, asend.at[n % 2, c]).wait()
         pltpu.make_async_copy(arrived, arrived, arecv.at[n % 2, c]).wait()
-        total = slots[0]
+        total = slots[0].astype(F32)
         for k in range(1, MEMBERS):
-            total = total + slots[k]
+            total = total + slots[k].astype(F32)
+        if n >= 6:
+            total = jnp.concatenate(
+                [
+                    jnp.concatenate([total[8 * r + k : 8 * r + k + 1] for k in range(8)], 1)
+                    for r in range(rows)
+                ],
+                0,
+            )
         if v > 1:
             again = arv.at[n % 2, c]
             spare = [jnp.zeros((4 - rows, C), F32)] if rows < 4 else []
@@ -739,12 +767,14 @@
                 to = lax.rem(z + hop, 4)
                 push(w.at[section, to, yx, rows], landing(k, 3, hop - 1, count), to * 4 + yx, *sems)
 
+    for copy in loads:
+        copy.wait()
     shares = {}
     at = 0
     for name, ref, count in (
-        ("wa0", l_wa0, 14), ("k0", l_k0, 16), ("ws", l_ws, 14), ("wd0", l_wd0, 4),
-        ("wu0", l_wu0, 4), ("wc0", l_wc0, 28), ("wa1", l_wa1, 28), ("k1", l_k1, 16),
-        ("wd1", l_wd1, 7), ("wu1", l_wu1, 7), ("wc1", l_wc1, 28),
+        ("wa0", v_wa0, 14), ("k0", v_k0, 16), ("ws", v_ws, 14), ("wd0", v_wd0, 4),
+        ("wu0", v_wu0, 4), ("wc0", v_wc0, 28), ("wa1", v_wa1, 28), ("k1", v_k1, 16),
+        ("wd1", v_wd1, 7), ("wu1", v_wu1, 7), ("wc1", v_wc1, 28),
     ):
         fs[at : at + ref.shape[0]] = ref[...].astype(F32)
         value = jnp.concatenate([fs[pl.ds(at + k, count, stride=7)] for k in range(7)], 1)
@@ -779,11 +809,10 @@
             ref[c, 0:GUARD] = guard
             ref[c, GUARD + PX :] = guard
 
-    halves = jnp.concatenate(
-        [short_gain_in[...].astype(F32), short_shift_in[...].astype(F32)], 1
-    )
+    short = v_short[...].astype(F32)
+    halves = jnp.concatenate([short[k : k + 1] for k in range(7)], 1)
     pair[section] = jnp.concatenate(
-        [gain_in[k] for k in range(3)] + [shift_in[k] for k in range(3)]
+        [v_gain[k] for k in range(3)] + [v_shift[k] for k in range(3)]
         + [halves, jnp.zeros((1, D), F32)],
         0,
     )
@@ -801,12 +830,6 @@
         0,
     )
 
-    def thirds(value):
-        high = value.astype(BF16)
-        left = value - high.astype(F32)
-        middle = left.astype(BF16)
-        return jnp.concatenate([high, middle, (left - middle.astype(F32)).astype(BF16)], 0)
-
     wide = nn(thirds(rows), e_buf[...])
     params[...] = wide[0:16] + wide[16:32] + wide[32:48]
     poll("params")
@@ -883,8 +906,8 @@
             return (first, second)
 
         sums = each_column(2, body)
-        own = jnp.zeros((1, C), F32) + crop_count(c)
-        ar_start(0, c, [sums[0], sums[1], own, own])
+        spare = lax.broadcasted_iota(jnp.int32, (1, C), 1) == 28
+        ar_start(0, c, [jnp.where(spare, crop_count(c), sums[0]), sums[1]])
 
     crops(entry_inner, "in")
     poll("need_k0")
@@ -892,10 +915,13 @@
     poll("bk0")
 
     def entry_conv(c):
-        totals = ar_wait(0, c, 4)
-        cn[c, 0:1] = totals[2]
-        cn[c, 1:2] = 1.0 / totals[2]
-        cn[c, 2:3] = 0.25 / totals[2]
+        totals = ar_wait(0, c, 2)
+        count = jnp.zeros((1, C), F32) + totals[0][:, 28:29]
+        cn[c, 0:1] = count
+        cn[c, 1:2] = 1.0 / count
+        cn[c, 2:3] = 0.25 / count
+        spare = lax.broadcasted_iota(jnp.int32, (1, C), 1) == 28
+        totals[0] = jnp.where(spare, 0.0, totals[0])
         set_stats(c, 0, totals, inverse_in(c), 0)
         a, shift = affine(c, 0)
 
@@ -1150,7 +1176,7 @@
             )
 
         sums = each_column(3, pre)
-        ar_start(9, c, sums + [sums[0]])
+        ar_start(9, c, sums)
 
     crops(body_back_in, "bin")
     outer(lambda c, l: hid[c, :, l], dp_of, "wa1")
@@ -1158,7 +1184,7 @@
     build_conv("k0")
 
     def entry_back_out(c):
-        totals = ar_wait(9, c, 4)
+        totals = ar_wait(9, c, 3)
         a, slope, offset = norm_coefficients(c, 2, totals[0:2], inverse_out(c), 2, 0)
         short = norm_coefficients(c, 3, [totals[0], totals[2]], inverse_out(c), 12, 0)
 
@@ -1305,37 +1331,55 @@
 
     load_map.wait()
     crops(entry_emit, "emit")
-    load_map = local_copy(expand.at[1], e_buf, 2)
-    load_map.start()
     last = [
         to_sibling(x_buf.at[other], grad.at[mine], 4),
         local_copy(x_buf.at[section], grad.at[mine], 0),
     ]
     for copy in last:
         copy.start()
+    swap.wait()
+    ng[...] = ng[...] + ng_in[...]
+    last.append(local_copy(ng, result.at[pl.ds(192, 16)], 1))
+    last[-1].start()
     poll("tail")
-    load_map.wait()
-    swap.wait()
-    total = thirds(ng[...] + ng_in[...])
-    total = nt(total, e_buf[...])
+    last.append(local_copy(pool.at[0, 1, pl.ds(0, 192)], result.at[pl.ds(0, 192)], 2))
+    last[-1].start()
+    for copy in last:
+        copy.wait()
+
+
+def thirds(value):
+    high = value.astype(BF16)
+    left = value - high.astype(F32)
+    middle = left.astype(BF16)
+    return jnp.concatenate([high, middle, (left - middle.astype(F32)).astype(BF16)], 0)
+
+
+def final_kernel(result, narrow_map, *refs):
+    flat_out, (gain_out, shift_out, short_gain_out, short_shift_out) = refs[:11], refs[11:15]
+    flat, (gain, shift, short_gain, short_shift), sems = refs[15:26], refs[26:30], refs[30]
+    section = lax.axis_index("section")
+    total = nt(thirds(result[192:208]), narrow_map[...])
     total = total[0:16] + total[16:32] + total[32:48]
 
     def own(top, low):
         return jnp.where(section == 0, top, low)
 
     for k in range(3):
-        gain_out[k] = own(total[k : k + 1], total[k + 3 : k + 4])
-        shift_out[k] = own(total[k + 6 : k + 7], total[k + 9 : k + 10])
-    short_gain_out[...] = own(total[12:13, 0:DIN], total[12:13, DIN:])
-    short_shift_out[...] = own(total[13:14, 0:DIN], total[13:14, DIN:])
-    total = pool[0, 1, 0:192]
+        gain[k] = own(total[k : k + 1], total[k + 3 : k + 4])
+        shift[k] = own(total[k + 6 : k + 7], total[k + 9 : k + 10])
+    short_gain[...] = own(total[12:13, 0:DIN], total[12:13, DIN:])
+    short_shift[...] = own(total[13:14, 0:DIN], total[13:14, DIN:])
+    total = result[0:192]
     high = total.astype(BF16)
     low = (total - high.astype(F32)).astype(BF16)
-    final = nt(high, e_buf[...]) + nt(low, e_buf[...])
-    for name, ref, count in (
-        ("wa0", o_wa0, 14), ("k0", o_k0, 16), ("ws", o_ws, 14), ("wd0", o_wd0, 4),
-        ("wu0", o_wu0, 4), ("wc0", o_wc0, 28), ("wa1", o_wa1, 28), ("k1", o_k1, 16),
-        ("wd1", o_wd1, 7), ("wu1", o_wu1, 7), ("wc1", o_wc1, 28),
+    final = nt(high, narrow_map[...]) + nt(low, narrow_map[...])
+    for (name, count), ref in zip(
+        (
+            ("wa0", 14), ("k0", 16), ("ws", 14), ("wd0", 4), ("wu0", 4), ("wc0", 28), ("wa1", 28),
+            ("k1", 16), ("wd1", 7), ("wu1", 7), ("wc1", 28),
+        ),
+        flat,
     ):
         if name[1] in "du":
             at = ROWS["misc" + name[2]][0] + (8 if name[1] == "u" else 0)
@@ -1343,8 +1387,30 @@
             at = ROWS[name][0]
         for k in range(7):
             ref[pl.ds(k, count, stride=7)] = final[at : at + count, 128 * k : 128 * k + 128]
-    for copy in last:
+    copies = [
+        pltpu.make_async_copy(src, dst, sems.at[at])
+        for at, (src, dst) in enumerate(
+            zip((*flat, gain, shift, short_gain, short_shift), (*flat_out, gain_out, shift_out, short_gain_out, short_shift_out))
+        )
+    ]
+    for copy in copies:
+        copy.start()
+    for copy in copies:
         copy.wait()
+
+
+def final_call(result, narrow_map):
+    vmem = pl.BlockSpec(memory_space=pltpu.VMEM)
+    shapes = [(count, 128) for count in LINES] + [(3, 1, D), (3, 1, D), (1, DIN), (1, DIN)]
+    return pl.pallas_call(
+        final_kernel,
+        out_shape=[jax.ShapeDtypeStruct(shape, F32) for shape in shapes],
+        in_specs=[vmem, vmem],
+        out_specs=[pl.BlockSpec(memory_space=pl.ANY)] * 15,
+        scratch_shapes=[pltpu.VMEM(shape, F32) for shape in shapes]
+        + [pltpu.SemaphoreType.DMA((15,))],
+        compiler_params=pltpu.CompilerParams(vmem_limit_bytes=16 << 20),
+    )(result, narrow_map)
 
 
 def lane_maps():
@@ -1359,14 +1425,10 @@
 def main_call(n_dp, *args):
     v = n_dp // MEMBERS
     any_space = pl.BlockSpec(memory_space=pl.ANY)
-    vmem = pl.BlockSpec(memory_space=pltpu.VMEM)
     smem = pl.BlockSpec(memory_space=pltpu.SMEM)
     shape = lambda *s, dtype=BF16: jax.ShapeDtypeStruct(s, dtype)
-    flat = [shape(count, 128, dtype=F32) for count in LINES]
     outs = [
-        shape(4, 7, 12544), shape(4, 14, 12544), *flat,
-        shape(3, 1, D, dtype=F32), shape(3, 1, D, dtype=F32),
-        shape(1, DIN, dtype=F32), shape(1, DIN, dtype=F32),
+        shape(4, 7, 12544), shape(4, 14, 12544), shape(208, C, dtype=F32),
     ]
     dma = pltpu.SemaphoreType.DMA
     scratch = [
@@ -1399,15 +1461,20 @@
         pltpu.VMEM((16, C), F32),
         pltpu.VMEM((2, 2, MEMBERS, 2, C), F32),
         pltpu.VMEM((2, MEMBERS, 4, C), F32),
+        pltpu.VMEM((2, 2, MEMBERS, 32, 128), BF16),
         pltpu.VMEM((2, 2, v, 4, C), F32),
-        dma((2, 2)), dma((2, 2)), dma((2, 2)), dma((2, 2)), dma((5,)), dma((5,)), dma((4,)),
+        pltpu.VMEM((3, 1, D), F32),
+        pltpu.VMEM((3, 1, D), F32),
+        pltpu.VMEM((7, 128), BF16),
+        *[pltpu.VMEM((count, 128), BF16) for count in LINES],
+        dma((15,)), dma((2, 2)), dma((2, 2)), dma((2, 2)), dma((2, 2)), dma((5,)), dma((5,)), dma((4,)),
         dma((7, 4)), dma((7, 4)), dma((7, 4)), dma((7, 4)), pltpu.SemaphoreType.REGULAR((6,)),
     ]
     return pl.pallas_call(
         functools.partial(main_kernel, n_dp),
         out_shape=outs,
-        in_specs=[any_space, any_space, smem, any_space] + [vmem] * 15,
-        out_specs=[any_space] * 2 + [vmem] * 15,
+        in_specs=[any_space, any_space, smem] + [any_space] * 15,
+        out_specs=[any_space] * 3,
         scratch_shapes=scratch,
         compiler_params=pltpu.CompilerParams(
             collective_id=1, has_side_effects=True, vmem_limit_bytes=64 << 20
@@ -1434,13 +1501,14 @@
             shard = lax.all_gather(shard, "dp", axis_index_groups=groups, axis=0, tiled=True)
         return jnp.pad(shard, (0, 128 * count - shard.shape[0])).reshape(count, 128)
 
-    results = main_call(
-        n_dp, features, upstream, crop_side, jnp.asarray(lane_maps(), BF16),
-        norm_gain.transpose(1, 0, 2), norm_shift.transpose(1, 0, 2), shortcut_gain[None],
-        shortcut_shift[None],
+    maps = jnp.asarray(lane_maps(), BF16)
+    output, d_features, result = main_call(
+        n_dp, features, upstream, crop_side, maps,
+        norm_gain.transpose(1, 0, 2), norm_shift.transpose(1, 0, 2),
+        jnp.concatenate([shortcut_gain, shortcut_shift]).reshape(7, 128),
         *(lines(shard, count) for shard, count in zip(shards, LINES)),
     )
-    output, d_features = results[:2]
+    results = final_call(result, jnp.asarray(lane_maps()[1], BF16))
 
     def share(values, shard):
         values = values.reshape(-1)[: v * shard.shape[0]]
@@ -1451,9 +1519,9 @@
         return values
 
     wa0, k0, ws, wd0, wu0, wc0, wa1, k1, wd1, wu1, wc1 = (
-        share(values, shard) for values, shard in zip(results[2:13], shards)
+        share(values, shard) for values, shard in zip(results[:11], shards)
     )
-    gains, shifts, short_gain, short_shift = results[13:17]
+    gains, shifts, short_gain, short_shift = results[11:15]
     return (
         output, d_features, wa0, k0, wc0, wd0, wu0, ws, wa1, k1, wc1, wd1, wu1,
         gains.transpose(1, 0, 2), shifts.transpose(1, 0, 2),

time: 256 us -> 238 us (0.930)
  local copies, waits for them, and re-layouts: 23.7 us -> 11.8 us
  Pallas kernels: 231 us -> 224 us
    pallas_call x1, Pallas kernels: 231 us -> 221 us  [main_call(): pl.pallas_call(functools.partial(main_kernel, n_dp), out_shape=outs, in_s...]
    unnamed x51 -> x12, local copies, waits for them, and re-layouts: 18.4 us -> 9.05 us
    pallas_call x0 -> x1, Pallas kernels: none -> 2.75 us  [final_call(): pl.pallas_call(final_kernel, out_shape=[jax.ShapeDtypeStruct(shape, F32)...]
    broadcast_in_dim x2 -> x0, local copies, waits for them, and re-layouts: 2.63 us -> none  [the longest x1 1.37 us: local(): shortcut_gain[None]]
where the time goes in v5:
time: 238 us; the launch traced here: 237 us
  Pallas kernels  224 us (94%)
  local copies, waits for them, and re-layouts  11.8 us (5%)
    pallas_call x1, Pallas kernels, main_call(): pl.pallas_call(functools.partial(main_kernel, n_dp), out_shape=outs, in_s...  221 us
    unnamed x12, local copies, waits for them, and re-layouts  9.05 us

profile of v5, /device:TPU:0, one launch (start us, length us, event | category | flops | bytes accessed | tf_op | source)
XLA Modules:
  0.0 237.4 jit_solution(15977562438516769094)
XLA Ops:
  0.7 0.0 copy-start.3
  0.7 1.5 maximum_bitcast_fusion.short_in
  2.1 1.3 pad_bitcast_fusion.2
  3.4 1.4 pad_bitcast_fusion
  4.8 2.1 copy.38.upstream
  6.9 0.0 copy-done.3
  6.9 1.3 copy.37.features
  8.2 220.8 %shard_map.323 = (bf16[4,7,12544]{2,1,0:T(8,128)(2,1)}, bf16[4,14,12544]{2,1,0:T(8,128)(2,1)}, f32[208,1024]{1,0:T(8,128)}) custom-call(bf16[4,14,12544]{2,1,0:T(8,128)(2,1)} %copy.37.features, bf16[4,7,12544]{2,1,0:T(8,128)(2,1)} %copy.38.upstream, s32[4]{0:T(128)} %side_ref.1, bf16[2,896,1024]{2,1,0:T(8,128)(2,1)} %constant.7.clone.expand, ...), custom_call_target="tpu_custom_call" | custom-call | tf_op jit(solution)/shard_map/pallas_call | solution.py:1473
  229.0 0.0 copy-start.1
  229.0 2.4 copy.39
  231.3 0.0 copy-done.1
  231.3 0.0 copy-start
  231.3 1.5 copy-done
  232.8 0.0 copy-start.2
  232.8 2.7 %shard_map.324 = (f32[98,128]{1,0:T(8,128)}, f32[112,128]{1,0:T(8,128)}, f32[98,128]{1,0:T(8,128)}, f32[28,128]{1,0:T(8,128)}, f32[28,128]{1,0:T(8,128)}, /*inde...) custom-call(f32[208,1024]{1,0:T(8,128)S(1)} %copy-done.1, ...), custom_call_target="tpu_custom_call" | custom-call | tf_op jit(solution)/shard_map/pallas_call | solution.py:1405
  235.6 0.0 copy-done.2
  235.6 1.8 copy.40
Async XLA Ops:
  0.7 6.2 %copy-start.3 = (bf16[4,14,12544]{2,0,1:T(4,128)(2,1)S(1)}, bf16[4,14,12544]{2,0,1:T(4,128)(2,1)}, u32[]{:S(2)}) copy-start(bf16[4,14,12544]{2,0,1:T(4,128)(2,1)} %param.20) | copy-start | bytes 4214788
  229.0 2.4 copy-start.1
  231.3 1.5 copy-start
  232.8 2.8 %copy-start.2 = (bf16[4,14,12544]{2,1,0:T(8,128)(2,1)S(1)}, bf16[4,14,12544]{2,1,0:T(8,128)(2,1)}, u32[]{:S(2)}) copy-start(bf16[4,14,12544]{2,1,0:T(8,128)(2,1)} %get-tuple-element.54) | copy-start | bytes 4214788

commit v6 on v5

--- a/solution.py
+++ b/solution.py
@@ -22,12 +22,14 @@
 PX = 224
 GUARD = 16
 MEMBERS = 16
+SHORT = 12
 SHARDS = 32
 ROWS = {
     "wa0": (0, 16), "k0": (16, 16), "ws": (32, 16), "misc0": (48, 16), "wc0": (64, 32),
     "k1": (96, 16), "wa1": (112, 32), "misc1": (144, 16), "wc1": (160, 32),
 }
 ORDER = ("wa0", "k0", "ws", "wd0", "wu0", "wc0", "k1", "wa1", "wd1", "wu1", "wc1")
+ORDER_IN = ("wa0", "k0", "ws", "wd0", "wu0", "wc0", "wa1", "k1", "wd1", "wu1", "wc1")
 LINES = (98, 112, 98, 28, 28, 196, 196, 112, 49, 49, 196)
 GATHERS = ((0, 16), (16, 32), (32, 64), (64, 96), (96, 112), (112, 144), (144, 192))
 SCATTERS = (
@@ -35,52 +37,64 @@
 )
 CHAINED = 5
 GATHER_PLAN = {
-    "own": ((0, 0), (1, 0), (2, 0)),
-    "ph1": ((0, 1), (3, 0)),
-    "need_wa0": ((0, 2), (1, 1), (0, 3), (2, 1), (4, 0), (5, 0), (0, 4), (1, 2)),
-    "in0b": ((6, 0),),
-    "in0": ((3, 1),),
-    "in1a": ((2, 2),),
+    "own": ((0, 0),),
+    "params": ((1, 0),),
+    "cot0": ((2, 0), (3, 0), (0, 1), (4, 0), (0, 2)),
+    "cot1": ((1, 1), (0, 3)),
+    "map": ((2, 1), (5, 0)),
+    "ph0": ((0, 4), (1, 2)),
+    "ph1": ((1, 3),),
+    "in0b": ((2, 2), (3, 1)),
+    "in0": ((2, 3),),
+    "need_wa0": ((0, 5),),
+    "in1a": ((1, 4),),
+    "in1": ((1, 5), (6, 0), (3, 2), (5, 1), (3, 3)),
     "in1b": ((4, 1),),
-    "in1": ((1, 3),),
-    "need_k0": ((1, 4),),
-    "bk0": ((3, 2),),
-    "conv0a": ((5, 1),),
-    "conv1a": ((2, 3),),
-    "conv1": ((4, 2),),
-    "need_ws": ((2, 4),),
+    "conv1a": ((2, 4),),
+    "bk0": ((4, 2),),
+    "conv0a": ((4, 3),),
+    "need_ws": ((3, 4), (2, 5)),
+    "conv1": ((5, 2),),
+    "str0": ((5, 3),),
     "str1": ((6, 1),),
-    "need_wc0": ((3, 3), (3, 4), (5, 2)),
-    "gate0": ((4, 3),),
-    "gate1": ((6, 2),),
-    "need_k1": ((4, 4),),
-    "need_wa1": ((5, 3), (5, 4)),
-    "bconv0": ((6, 3),),
-    "need_wc1": ((6, 4),),
+    "need_wc0": ((3, 5), (4, 4)),
+    "gate1": ((5, 4),),
+    "need_k1": ((6, 2),),
+    "out0": ((6, 3),),
+    "need_wa1": ((5, 5),),
+    "gate1a": ((4, 5),),
+    "bconv0a": ((6, 4),),
+    "bconv1": ((6, 5),),
 }
 SCATTER_PLAN = {
     "small1": ((0, 0),),
     "bback0": ((0, 1),),
-    "k1": ((1, 0),),
-    "bin1a": ((0, 2), (1, 1)),
-    "wa1": ((2, 0),),
-    "eback0": ((0, 3),),
-    "eback1a": ((1, 2), (2, 1)),
-    "wc0": ((3, 0),),
-    "small0": ((4, 0),),
-    "econv0b": ((1, 3),),
-    "econv0": ((0, 4), (2, 2), (3, 1)),
-    "econv1b": ((1, 4),),
-    "econv1": ((2, 3),),
+    "bback1": ((0, 2),),
+    "bin0a": ((1, 0),),
+    "bin1a": ((0, 3),),
+    "wa1": ((1, 1),),
+    "bk0b": ((1, 2),),
+    "eback0a": ((0, 4), (2, 0)),
+    "eback0": ((1, 3),),
+    "eback1a": ((2, 1),),
+    "eback1": ((2, 2),),
+    "wc0": ((1, 4),),
+    "small0": ((4, 0), (3, 0)),
+    "econv0a": ((2, 3),),
+    "econv0": ((0, 5), (1, 5)),
+    "econv0b": ((3, 1), (3, 2)),
+    "econv1a": ((2, 4),),
+    "econv1b": ((3, 3),),
+    "econv1": ((4, 1), (4, 2)),
+    "d": ((3, 4),),
     "k0": ((5, 0),),
-    "wa0": ((5, 1), (3, 2), (4, 1), (6, 0)),
-    "input0": ((3, 3),),
-    "input1a": ((6, 1),),
-    "emit0": ((2, 4),),
-    "emit1a": ((5, 2),),
-    "tail": (
-        (4, 2), (6, 2), (5, 3), (3, 4), (4, 3), (6, 3), (5, 4), (4, 4), (6, 4),
-    ),
+    "wa0": ((4, 3), (5, 1), (6, 0), (5, 2)),
+    "input0a": ((2, 5), (6, 1), (6, 2)),
+    "input0": ((4, 4), (5, 3), (6, 3), (5, 4)),
+    "emit0a": ((4, 5), (3, 5)),
+    "input1": ((6, 4),),
+    "emit1a": ((5, 5),),
+    "tail": ((6, 5),),
 }
 
 
@@ -106,6 +120,15 @@
 
 def slope_of(z, s):
     return s * (1.0 + z * (1.0 - s))
+
+
+def silu_half(h):
+    return h * (1.0 + jnp.tanh(h))
+
+
+def slope_half(h):
+    t = jnp.tanh(h)
+    return (1.0 + t) * (1.0 + h * (1.0 - t))
 
 
 def split_rows(rows):
@@ -142,12 +165,12 @@
 
 
 def main_kernel(
-    n_dp, features, upstream, side_ref, expand, gain_in, shift_in, short_in,
+    n_dp, features, upstream, side_ref, expand, gain_in, shift_in, short_gain_in, short_shift_in,
     l_wa0, l_k0, l_ws, l_wd0, l_wu0, l_wc0, l_wa1, l_k1, l_wd1, l_wu1, l_wc1,
     out, grad, result,
     inn, pool, u_buf, a0, a1, d_buf, ga, hid, dp_buf, x_buf, up_buf, fs, kd, e_buf,
-    w, wd0, wu0, wd1, wu1, stage, params, pair, st, sv, cn, ng, ng_in, ar2, ar4, arh, arv,
-    v_gain, v_shift, v_short, v_wa0, v_k0, v_ws, v_wd0, v_wu0, v_wc0, v_wa1, v_k1, v_wd1, v_wu1,
+    w, wd0, wu0, wd1, wu1, stage, params, pair, st, sv, cn, ng, ng_in, ar2, ars, arh, arv,
+    v_gain, v_shift, v_short_gain, v_short_shift, v_wa0, v_k0, v_ws, v_wd0, v_wu0, v_wc0, v_wa1, v_k1, v_wd1, v_wu1,
     v_wc1, isem, asend, arecv, vsend, vrecv, xsend, xrecv, lsem, gsend, grecv, rsend, rrecv, free,
 ):
     loads = [
@@ -156,11 +179,12 @@
             (
                 (l_wa0, v_wa0), (l_k0, v_k0), (l_ws, v_ws), (l_wd0, v_wd0), (l_wu0, v_wu0),
                 (l_wc0, v_wc0), (l_wa1, v_wa1), (l_k1, v_k1), (l_wd1, v_wd1), (l_wu1, v_wu1),
-                (l_wc1, v_wc1), (gain_in, v_gain), (shift_in, v_shift), (short_in, v_short),
+                (l_wc1, v_wc1), (gain_in, v_gain), (shift_in, v_shift),
+                (short_gain_in, v_short_gain), (short_shift_in, v_short_shift),
             )
         )
     ]
-    load_map = pltpu.make_async_copy(expand.at[1], e_buf, isem.at[14])
+    load_map = pltpu.make_async_copy(expand.at[1], e_buf, isem.at[15])
     for copy in loads + [load_map]:
         copy.start()
     section = lax.axis_index("section")
@@ -211,10 +235,10 @@
     def half_side(c):
         return side_ref[2 * section + c] // 2
 
-    def keep(c, j):
+    def keep(c, j, weight=1.0):
         half = half_side(c)
         bound = jnp.where(j < half, half, 0)
-        tile = (lax.broadcasted_iota(jnp.int32, (16, 128), 0) < bound).astype(F32)
+        tile = jnp.where(lax.broadcasted_iota(jnp.int32, (16, 128), 0) < bound, weight, 0.0)
         return jnp.concatenate([tile] * (C // 128), 1)
 
     def crop_count(c):
@@ -222,13 +246,16 @@
         return (half * half).astype(F32)
 
     def ar_slots(n, c):
-        if n >= 6:
+        if 6 <= n < SHORT:
             return arh.at[n % 2, c, :, pl.ds(0, 32 if n == 9 else 16)]
-        return ar4.at[c] if n == 2 else ar2.at[n % 2, c]
+        return ars.at[c] if n == SHORT else ar2.at[n % 2, c]
+
+    def ar_lane(n):
+        return 2 if n == SHORT else n % 2
 
     def ar_start(n, c, rows):
         slots = ar_slots(n, c)
-        if n >= 6:
+        if 6 <= n < SHORT:
             tiles = [row[:, 128 * k : 128 * k + 128] for row in rows for k in range(8)]
             if n == 9:
                 tiles.append(jnp.zeros((8, 128), F32))
@@ -238,8 +265,8 @@
 
         def send(hop):
             pltpu.make_async_remote_copy(
-                src_ref=slots.at[digit], dst_ref=slots.at[digit], send_sem=asend.at[n % 2, c],
-                recv_sem=arecv.at[n % 2, c], device_id=(section, member(hop + 1)),
+                src_ref=slots.at[digit], dst_ref=slots.at[digit], send_sem=asend.at[ar_lane(n), c],
+                recv_sem=arecv.at[ar_lane(n), c], device_id=(section, member(hop + 1)),
                 device_id_type=MESH,
             ).start()
 
@@ -248,12 +275,12 @@
     def ar_wait(n, c, rows):
         slots = ar_slots(n, c)
         arrived = slots.at[pl.ds(0, MEMBERS - 1)]
-        pltpu.make_async_copy(arrived, arrived, asend.at[n % 2, c]).wait()
-        pltpu.make_async_copy(arrived, arrived, arecv.at[n % 2, c]).wait()
+        pltpu.make_async_copy(arrived, arrived, asend.at[ar_lane(n), c]).wait()
+        pltpu.make_async_copy(arrived, arrived, arecv.at[ar_lane(n), c]).wait()
         total = slots[0].astype(F32)
         for k in range(1, MEMBERS):
             total = total + slots[k].astype(F32)
-        if n >= 6:
+        if 6 <= n < SHORT:
             total = jnp.concatenate(
                 [
                     jnp.concatenate([total[8 * r + k : 8 * r + k + 1] for k in range(8)], 1)
@@ -262,21 +289,21 @@
                 0,
             )
         if v > 1:
-            again = arv.at[n % 2, c]
+            again = arv.at[ar_lane(n), c]
             spare = [jnp.zeros((4 - rows, C), F32)] if rows < 4 else []
             again[rest] = jnp.concatenate([total] + spare, 0)
 
             def send(hop):
                 pltpu.make_async_remote_copy(
-                    src_ref=again.at[rest], dst_ref=again.at[rest], send_sem=vsend.at[n % 2, c],
-                    recv_sem=vrecv.at[n % 2, c], device_id=(section, near(hop + 1)),
+                    src_ref=again.at[rest], dst_ref=again.at[rest], send_sem=vsend.at[ar_lane(n), c],
+                    recv_sem=vrecv.at[ar_lane(n), c], device_id=(section, near(hop + 1)),
                     device_id_type=MESH,
                 ).start()
 
             loop(v - 1, send)
             arrived = again.at[pl.ds(0, v - 1)]
-            pltpu.make_async_copy(arrived, arrived, vsend.at[n % 2, c]).wait()
-            pltpu.make_async_copy(arrived, arrived, vrecv.at[n % 2, c]).wait()
+            pltpu.make_async_copy(arrived, arrived, vsend.at[ar_lane(n), c]).wait()
+            pltpu.make_async_copy(arrived, arrived, vrecv.at[ar_lane(n), c]).wait()
             total = again[0]
             for k in range(1, v):
                 total = total + again[k]
@@ -294,6 +321,9 @@
     def each_column(count, body):
         sums = lax.fori_loop(0, 14, body, zeros(count))
         return [down(one) for one in sums]
+
+    def scaled(sums, *factors):
+        return [sums[0]] + [one * factor for one, factor in zip(sums[1:], factors)]
 
     def moment_sums(c, value_of):
         def body(j, sums):
@@ -312,9 +342,10 @@
         st[c, index, 1:2] = scaling
         st[c, index, 2:3] = gain
         st[c, index, 3:4] = params[shift_row : shift_row + 1] - center * gain
+        st[c, index, 4:6] = st[c, index, 2:4] * 0.5
 
     def affine(c, index):
-        return st[c, index, 2:3], st[c, index, 3:4]
+        return st[c, index, 4:5], st[c, index, 5:6]
 
     def hat_of(c, index):
         return st[c, index, 0:1], st[c, index, 1:2]
@@ -446,12 +477,13 @@
 
         def pool_chunk(j, sums):
             z = pool[c, conv_k, chunk(j)] * a + shift
-            excited = keep(c, j) * (z * sig(z))
+            excited = keep(c, j) * silu_half(z)
             pool[c, 7, chunk(j)] = excited
             return (sums[0] + fold(excited),)
 
         pooled = each_column(1, pool_chunk)[0] / crop_count(c)
         gating = squeeze(c, b, pooled, wd, wu)
+        poll_crop(c, ("gate" if b == 0 else "bgate", "a"))
 
         def gate_chunk(j):
             ga[b, c, chunk(j)] = (pool[c, 7, chunk(j)] * gating).astype(BF16)
@@ -475,7 +507,7 @@
 
         def gate_chunk(j, sums):
             z = pool[c, conv_k, chunk(j)] * a + shift
-            excited = keep(c, j) * (z * sig(z))
+            excited = keep(c, j) * silu_half(z)
             return (sums[0] + fold(pool[c, 7, chunk(j)] * excited),)
 
         d_gate = each_column(1, gate_chunk)[0]
@@ -492,11 +524,11 @@
         def slope_chunk(j, sums):
             value = pool[c, conv_k, chunk(j)]
             z = value * a + shift
-            d = (pool[c, 7, chunk(j)] * gating + d_pool) * (keep(c, j) * slope_of(z, sig(z)))
+            d = (pool[c, 7, chunk(j)] * gating + d_pool) * (keep(c, j, 0.5) * slope_half(z))
             pool[c, 7, chunk(j)] = d
-            return (sums[0] + fold(d), sums[1] + fold(d * ((value - center) * scaling)))
-
-        return each_column(2, slope_chunk)
+            return (sums[0] + fold(d), sums[1] + fold(d * (value - center)))
+
+        return scaled(each_column(2, slope_chunk), scaling)
 
     def small_grads(b):
         width = 128 + 128 * b
@@ -606,32 +638,27 @@
         start, stop = GATHERS[k]
         rows = pl.ds(start, stop - start)
         sent = w.at[section, :, :, rows]
-        if phase > 0:
-            sem = grecv.at[k, phase - 1]
-            if phase == 1:
-                arrive(w.at[section, pl.ds(0, 3), 0, rows], sem)
-            elif phase == 2:
-                arrive(sent.at[:, 0], sem)
-            elif phase == 3:
-                arrive(sent.at[:, pl.ds(0, 2)], sem)
-            else:
-                arrive(sent, sem)
-        if phase == 4:
-            arrive(w.at[section, pl.ds(0, 3), 0, rows], gsend.at[k, 0])
-            arrive(sent.at[:, 0], gsend.at[k, 1])
-            arrive(sent.at[:, pl.ds(0, 2)], gsend.at[k, 2])
-            arrive(sent, gsend.at[k, 3])
+        amounts = (
+            w.at[section, pl.ds(0, 3), 0, rows], sent.at[:, 0], sent.at[:, pl.ds(0, 2)], sent,
+        )
+        before = (None, 0, 1, None, 2, 3)[phase]
+        if before is not None:
+            arrive(amounts[before], grecv.at[k, before])
+        if phase == 5:
+            for at in range(4):
+                arrive(amounts[at], gsend.at[k, at])
             return
-        sems = (gsend.at[k, phase], grecv.at[k, phase])
+        sem = (0, 1, 2, 2, 3)[phase]
+        sems = (gsend.at[k, sem], grecv.at[k, sem])
         if phase == 0:
             own = w.at[section, z, yx, rows]
             for hop in range(1, 4):
                 push(own, own, lax.rem(z + hop, 4) * 4 + yx, *sems)
         elif phase == 1:
             push(sent.at[:, yx], sent.at[:, yx], z * 4 + flip(bits[0]), *sems)
-        elif phase == 2:
-            for at in (yx, flip(bits[0])):
-                push(sent.at[:, at], sent.at[:, at], z * 4 + flip(bits[1]), *sems)
+        elif phase in (2, 3):
+            at = yx if phase == 2 else flip(bits[0])
+            push(sent.at[:, at], sent.at[:, at], z * 4 + flip(bits[1]), *sems)
         else:
             push_sibling(sent, sent, *sems)
 
@@ -706,25 +733,26 @@
         rows = pl.ds(start, count)
         first, second = flip(bits[1]), flip(bits[0])
         more = k + 1 < CHAINED
-        if phase > 0:
-            arrive(landed(k, phase - 1, count), rrecv.at[k, phase - 1])
+        before = (None, 0, None, 1, 2, 3)[phase]
+        if before is not None:
+            arrive(landed(k, before, count), rrecv.at[k, before])
         if phase == 1:
             loop(16, lambda b: add_landed(k, 0, b, lambda b: (b // 4, lax.rem(b, 4)), start, count))
             if k < 3:
                 credit_sibling(0)
-        elif phase == 2:
+        elif phase == 3:
             for b in range(8):
                 add_landed(k, 1, b, lambda b: (b // 2, yx if b % 2 == 0 else second), start, count)
             if more:
                 credit(1, z * 4 + first)
-        elif phase == 3:
+        elif phase == 4:
             for b in range(4):
                 add_landed(k, 2, b, lambda b: (b, yx), start, count)
             if more:
                 credit(2, z * 4 + second)
             if k == 0:
                 credit_z(5)
-        elif phase == 4:
+        elif phase == 5:
             total = w[section, z, yx, start:stop].astype(F32)
             for b in range(3):
                 total = total + landing(k, 3, b, count)[...].astype(F32)
@@ -734,7 +762,8 @@
             for sent in range(4):
                 arrive(landed(k, sent, count), rsend.at[k, sent])
             return
-        sems = (rsend.at[k, phase], rrecv.at[k, phase])
+        sem = (0, 1, 1, 2, 3)[phase]
+        sems = (rsend.at[k, sem], rrecv.at[k, sem])
         if phase == 0:
             if k < 4 or k == CHAINED:
                 pl.semaphore_wait(free.at[0 if k < 4 else 4], 1)
@@ -745,15 +774,15 @@
                 )
 
             loop(16, send)
-        elif phase == 1:
-            if k < CHAINED:
+        elif phase in (1, 2):
+            if k < CHAINED and phase == 1:
                 pl.semaphore_wait(free.at[1], 1)
-            for b in range(8):
+            for b in range(4 * phase - 4, 4 * phase):
                 to = first if b % 2 == 0 else first + second - yx
                 push(
                     w.at[section, b // 2, to, rows], landing(k, 1, b, count), z * 4 + first, *sems
                 )
-        elif phase == 2:
+        elif phase == 3:
             if k < CHAINED:
                 pl.semaphore_wait(free.at[2], 1)
             for b in range(4):
@@ -776,13 +805,23 @@
         ("wu0", v_wu0, 4), ("wc0", v_wc0, 28), ("wa1", v_wa1, 28), ("k1", v_k1, 16),
         ("wd1", v_wd1, 7), ("wu1", v_wu1, 7), ("wc1", v_wc1, 28),
     ):
-        fs[at : at + ref.shape[0]] = ref[...].astype(F32)
+        lines = LINES[ORDER_IN.index(name)]
+        if len(ref.shape) == 2:
+            fs[at : at + lines] = ref[...].astype(F32)
+        else:
+            whole, left = ref.shape[0] // 128, ref.shape[0] % 128
+            fs[at : at + whole] = ref[pl.ds(0, 128 * whole)].astype(F32).reshape(whole, 128)
+            rest_row = ref[pl.ds(128 * whole, left)].astype(F32).reshape(1, left)
+            rest_row = jnp.concatenate([rest_row, jnp.zeros((1, 128 - left), F32)], 1)
+            fs[at + whole : at + lines] = jnp.concatenate(
+                [rest_row, jnp.zeros((lines - whole - 1, 128), F32)], 0
+            )
         value = jnp.concatenate([fs[pl.ds(at + k, count, stride=7)] for k in range(7)], 1)
         room = 8 if count < 8 else count + -count % 16
         if room > count:
             value = jnp.concatenate([value, jnp.zeros((room - count, D), F32)], 0)
         shares[name] = value
-        at += ref.shape[0] + -ref.shape[0] % 8
+        at += lines + -lines % 8
     load_map.wait()
     own_rows = jnp.concatenate([shares[name] for name in ORDER], 0).astype(BF16)
     for n in range(4):
@@ -809,8 +848,9 @@
             ref[c, 0:GUARD] = guard
             ref[c, GUARD + PX :] = guard
 
-    short = v_short[...].astype(F32)
-    halves = jnp.concatenate([short[k : k + 1] for k in range(7)], 1)
+    halves = jnp.concatenate(
+        [ref[...].astype(F32).reshape(1, DIN) for ref in (v_short_gain, v_short_shift)], 1
+    )
     pair[section] = jnp.concatenate(
         [v_gain[k] for k in range(3)] + [v_shift[k] for k in range(3)]
         + [halves, jnp.zeros((1, D), F32)],
@@ -858,6 +898,7 @@
     load_map = local_copy(expand.at[0], e_buf, 2)
     load_map.start()
     fs[...] = jnp.zeros_like(fs)
+    poll("map")
     load_map.wait()
 
     def phases(c):
@@ -930,7 +971,7 @@
             for q in range(2):
                 for r in range(2):
                     z = inn[c, 2 * q + r, chunk(j)] * a + shift
-                    act = mask * (z * sig(z))
+                    act = mask * silu_half(z)
                     a0[c, 2 * q + r, chunk(j, GUARD)] = act.astype(BF16)
                     if q == 1:
                         d_buf[c, r, chunk(j, GUARD)] = pltpu.roll(act, 1, 0).astype(BF16)
@@ -958,6 +999,7 @@
             pool[c, 2, :, col(n)] = nn(u_buf[c, 0, :, 0:512], cols_of("ws", col(n)))
 
         loop(4, product)
+        ar_start(SHORT, c, moment_sums(c, lambda j: pool[c, 2, chunk(j)]))
 
     crops(strided, "str")
     build_small(0)
@@ -966,8 +1008,7 @@
     def entry_gate(c):
         totals = ar_wait(1, c, 2)
         set_stats(c, 1, totals, inverse_out(c), 1)
-        sums = gate(c, 0, 1, 0, wd0, wu0, "wc0", 1)
-        ar_start(2, c, sums + moment_sums(c, lambda j: pool[c, 2, chunk(j)]))
+        ar_start(2, c, gate(c, 0, 1, 0, wd0, wu0, "wc0", 1))
 
     crops(entry_gate, "gate")
     poll("need_k1")
@@ -982,15 +1023,15 @@
         )
 
     def entry_out(c):
-        totals = ar_wait(2, c, 4)
-        set_stats(c, 2, totals[0:2], inverse_out(c), 2)
-        set_stats(c, 3, totals[2:4], inverse_out(c), 12)
+        set_stats(c, 3, ar_wait(SHORT, c, 2), inverse_out(c), 12)
+        set_stats(c, 2, ar_wait(2, c, 2), inverse_out(c), 2)
 
         def finish(j):
             z = entry_pre(c, j)
-            hid[c, chunk(j)] = (keep(c, j) * (z * sig(z))).astype(BF16)
+            hid[c, chunk(j)] = (keep(c, j) * silu_half(z)).astype(BF16)
 
         loop(14, finish)
+        poll_crop(c, ("out", "a"))
 
         def product(n):
             pool[c, 4, :, col(n)] = nn(hid[c], cols_of("wa1", col(n)))
@@ -1006,12 +1047,13 @@
 
         def activate(j):
             z = pool[c, 4, chunk(j)] * a + shift
-            act = keep(c, j) * (z * sig(z))
+            act = keep(c, j) * silu_half(z)
             a1[c, chunk(j, GUARD)] = act.astype(BF16)
             d_buf[c, 0, chunk(j, GUARD)] = pltpu.roll(act, 1, 0).astype(BF16)
             d_buf[c, 1, chunk(j, GUARD)] = pltpu.roll(act, 15, 0).astype(BF16)
 
         loop(14, activate)
+        poll_crop(c, ("bconv", "a"))
 
         def convolve(n):
             rows = (d_buf.at[c, 0], a1.at[c], d_buf.at[c, 1])
@@ -1026,12 +1068,13 @@
     crops(body_conv, "bconv")
     poll("need_wc1")
     build_small(1)
+    poll("small1f")
 
     def body_gate(c):
         set_stats(c, 5, ar_wait(4, c, 2), inverse_out(c), 4)
         ar_start(5, c, gate(c, 1, 5, 5, wd1, wu1, "wc1", 6))
 
-    loop(2, body_gate)
+    crops(body_gate, "bgate")
 
     def body_out(c):
         set_stats(c, 6, ar_wait(5, c, 2), inverse_out(c), 5)
@@ -1040,17 +1083,19 @@
 
         def finish(j, sums):
             value = pool[c, 6, chunk(j)]
-            z = value * a + shift + hid[c, chunk(j)].astype(F32)
+            z = value * a + shift + 0.5 * hid[c, chunk(j)].astype(F32)
             mask = keep(c, j)
-            s = sig(z)
-            dp_buf[c, chunk(j, GUARD)] = (mask * (z * s)).astype(BF16)
-            d_pre = pool[c, 3, chunk(j)] * (mask * slope_of(z, s))
+            t = jnp.tanh(z)
+            dp_buf[c, chunk(j, GUARD)] = (mask * (z * (1.0 + t))).astype(BF16)
+            d_pre = pool[c, 3, chunk(j)] * (
+                mask * (0.5 * (1.0 + t) * (1.0 + z * (1.0 - t)))
+            )
             pool[c, 3, chunk(j)] = d_pre
-            return (sums[0] + fold(d_pre), sums[1] + fold(d_pre * ((value - center) * scaling)))
-
-        ar_start(6, c, each_column(2, finish))
-
-    loop(2, body_out)
+            return (sums[0] + fold(d_pre), sums[1] + fold(d_pre * (value - center)))
+
+        ar_start(6, c, scaled(each_column(2, finish), scaling))
+
+    crops(body_out, "bo")
     load_map.wait()
 
     def narrow(value, store):
@@ -1068,6 +1113,7 @@
         narrow(dp_of(c), store)
 
     loop(2, body_emit)
+    poll("bemit")
     out_copies = [
         to_sibling(up_buf.at[other], out.at[mine], 2),
         local_copy(up_buf.at[section], out.at[mine], 1),
@@ -1135,11 +1181,11 @@
         def body(j, sums):
             value = pool[c, 4, chunk(j)]
             z = value * a + shift
-            d = pool[c, 7, chunk(j)] * (keep(c, j) * slope_of(z, sig(z)))
+            d = pool[c, 7, chunk(j)] * (keep(c, j, 0.5) * slope_half(z))
             pool[c, 7, chunk(j)] = d
-            return (sums[0] + fold(d), sums[1] + fold(d * ((value - center) * scaling)))
-
-        ar_start(8, c, each_column(2, body))
+            return (sums[0] + fold(d), sums[1] + fold(d * (value - center)))
+
+        ar_start(8, c, scaled(each_column(2, body), scaling))
 
     crops(body_back_conv, "bback")
     conv_grad(lambda c, tap, l: a1[c, GUARD : GUARD + PX, l], v_body, "k1")
@@ -1167,21 +1213,22 @@
 
         def pre(j, sums):
             z = entry_pre(c, j)
-            d = pool[c, 3, chunk(j)] * (keep(c, j) * slope_of(z, sig(z)))
+            d = pool[c, 3, chunk(j)] * (keep(c, j, 0.5) * slope_half(z))
             pool[c, 3, chunk(j)] = d
             return (
                 sums[0] + fold(d),
-                sums[1] + fold(d * ((pool[c, 1, chunk(j)] - center) * scaling)),
-                sums[2] + fold(d * ((pool[c, 2, chunk(j)] - short_center) * short_scaling)),
+                sums[1] + fold(d * (pool[c, 1, chunk(j)] - center)),
+                sums[2] + fold(d * (pool[c, 2, chunk(j)] - short_center)),
             )
 
         sums = each_column(3, pre)
-        ar_start(9, c, sums)
+        ar_start(9, c, scaled(sums, scaling, short_scaling))
 
     crops(body_back_in, "bin")
     outer(lambda c, l: hid[c, :, l], dp_of, "wa1")
     poll("wa1")
     build_conv("k0")
+    poll("bk0b")
 
     def entry_back_out(c):
         totals = ar_wait(9, c, 3)
@@ -1233,18 +1280,18 @@
         center, scaling = hat_of(c, 0)
 
         def body(j, sums):
-            mask = keep(c, j)
+            mask = keep(c, j, 0.5)
             first, second = sums
             for k in range(4):
                 value = inn[c, k, chunk(j)]
                 z = value * a + shift
-                d = pool[c, 4 + k, chunk(j)] * (mask * slope_of(z, sig(z)))
+                d = pool[c, 4 + k, chunk(j)] * (mask * slope_half(z))
                 pool[c, 4 + k, chunk(j)] = d
                 first = first + fold(d)
-                second = second + fold(d * ((value - center) * scaling))
+                second = second + fold(d * (value - center))
             return (first, second)
 
-        ar_start(11, c, each_column(2, body))
+        ar_start(11, c, scaled(each_column(2, body), scaling))
 
     crops(entry_back_conv, "econv")
 
@@ -1273,6 +1320,7 @@
         loop(14, body)
 
     loop(2, entry_back_in)
+    poll("d")
     swap = to_sibling(ng, ng_in, 3)
     swap.start()
 
@@ -1460,20 +1508,21 @@
         pltpu.VMEM((16, C), F32),
         pltpu.VMEM((16, C), F32),
         pltpu.VMEM((2, 2, MEMBERS, 2, C), F32),
-        pltpu.VMEM((2, MEMBERS, 4, C), F32),
+        pltpu.VMEM((2, MEMBERS, 2, C), F32),
         pltpu.VMEM((2, 2, MEMBERS, 32, 128), BF16),
-        pltpu.VMEM((2, 2, v, 4, C), F32),
+        pltpu.VMEM((3, 2, v, 4, C), F32),
         pltpu.VMEM((3, 1, D), F32),
         pltpu.VMEM((3, 1, D), F32),
-        pltpu.VMEM((7, 128), BF16),
-        *[pltpu.VMEM((count, 128), BF16) for count in LINES],
-        dma((15,)), dma((2, 2)), dma((2, 2)), dma((2, 2)), dma((2, 2)), dma((5,)), dma((5,)), dma((4,)),
+        pltpu.VMEM((DIN,), BF16),
+        pltpu.VMEM((DIN,), BF16),
+        *[pltpu.VMEM(shard.shape, BF16) for shard in args[8:]],
+        dma((16,)), dma((3, 2)), dma((3, 2)), dma((3, 2)), dma((3, 2)), dma((5,)), dma((5,)), dma((4,)),
         dma((7, 4)), dma((7, 4)), dma((7, 4)), dma((7, 4)), pltpu.SemaphoreType.REGULAR((6,)),
     ]
     return pl.pallas_call(
         functools.partial(main_kernel, n_dp),
         out_shape=outs,
-        in_specs=[any_space, any_space, smem] + [any_space] * 15,
+        in_specs=[any_space, any_space, smem] + [any_space] * 16,
         out_specs=[any_space] * 3,
         scratch_shapes=scratch,
         compiler_params=pltpu.CompilerParams(
@@ -1499,13 +1548,13 @@
     def lines(shard, count):
         if v > 1:
             shard = lax.all_gather(shard, "dp", axis_index_groups=groups, axis=0, tiled=True)
-        return jnp.pad(shard, (0, 128 * count - shard.shape[0])).reshape(count, 128)
+        return shard.reshape(count, 128) if shard.shape[0] == 128 * count else shard
 
     maps = jnp.asarray(lane_maps(), BF16)
     output, d_features, result = main_call(
         n_dp, features, upstream, crop_side, maps,
         norm_gain.transpose(1, 0, 2), norm_shift.transpose(1, 0, 2),
-        jnp.concatenate([shortcut_gain, shortcut_shift]).reshape(7, 128),
+        shortcut_gain, shortcut_shift,
         *(lines(shard, count) for shard, count in zip(shards, LINES)),
     )
     results = final_call(result, jnp.asarray(lane_maps()[1], BF16))

time: 238 us -> 220 us (0.924)
  Pallas kernels: 224 us -> 210 us
  local copies, waits for them, and re-layouts: 11.8 us -> 9.16 us
    pallas_call x1, Pallas kernels: 221 us -> 208 us  [main_call(): pl.pallas_call(functools.partial(main_kernel, n_dp), out_shape=outs, in_s...]
    reshape x2 -> x0, local copies, waits for them, and re-layouts: 2.71 us -> none  [lines(): return jnp.pad(shard, (0, 128 * count - shard.shape[0])).reshape(count, 128)]
where the time goes in v6:
time: 220 us
  Pallas kernels  210 us (95%)
  local copies, waits for them, and re-layouts  9.16 us (4%)
    pallas_call x1, Pallas kernels, main_call(): pl.pallas_call(functools.partial(main_kernel, n_dp), out_shape=outs, in_s...  208 us
    unnamed x12, local copies, waits for them, and re-layouts  9.16 us

profile of v6, /device:TPU:0, one launch (start us, length us, event | category | flops | bytes accessed | tf_op | source)
XLA Modules:
  0.0 220.2 jit_solution(810069887853075036)
XLA Ops:
  0.7 0.0 copy-start.3
  0.7 2.2 copy.38.upstream
  2.8 0.0 copy-done.3
  2.8 1.3 copy.37.features
  4.2 207.6 %shard_map.323 = (bf16[4,7,12544]{2,1,0:T(8,128)(2,1)}, bf16[4,14,12544]{2,1,0:T(8,128)(2,1)}, f32[208,1024]{1,0:T(8,128)}) custom-call(bf16[4,14,12544]{2,1,0:T(8,128)(2,1)} %copy.37.features, bf16[4,7,12544]{2,1,0:T(8,128)(2,1)} %copy.38.upstream, s32[4]{0:T(128)} %side_ref.1, bf16[2,896,1024]{2,1,0:T(8,128)(2,1)} %constant.4.clone.expand, ...), custom_call_target="tpu_custom_call" | custom-call | tf_op jit(solution)/shard_map/pallas_call | solution.py:1522
  211.8 0.0 copy-start.1
  211.8 2.4 %copy.39 = bf16[4,7,12544]{2,0,1:T(4,128)(2,1)} copy(bf16[4,7,12544]{2,1,0:T(8,128)(2,1)} %get-tuple-element.53) | data formatting | bytes 1404928
  214.1 0.0 copy-done.1
  214.1 0.0 copy-start
  214.2 1.5 copy-done
  215.6 0.0 copy-start.2
  215.7 2.7 %shard_map.324 = (f32[98,128]{1,0:T(8,128)}, f32[112,128]{1,0:T(8,128)}, f32[98,128]{1,0:T(8,128)}, f32[28,128]{1,0:T(8,128)}, f32[28,128]{1,0:T(8,128)}, /*inde...) custom-call(f32[208,1024]{1,0:T(8,128)S(1)} %copy-done.1, ...), custom_call_target="tpu_custom_call" | custom-call | tf_op jit(solution)/shard_map/pallas_call | solution.py:1453
  218.4 0.0 copy-done.2
  218.4 1.8 copy.40
Async XLA Ops:
  0.7 2.2 copy-start.3
  211.8 2.4 %copy-start.1 = (f32[208,1024]{1,0:T(8,128)S(1)}, f32[208,1024]{1,0:T(8,128)}, u32[]{:S(2)}) copy-start(f32[208,1024]{1,0:T(8,128)} %get-tuple-element.37.result) | copy-start | bytes 2555908
  214.1 1.5 copy-start
  215.6 2.8 %copy-start.2 = (bf16[4,14,12544]{2,1,0:T(8,128)(2,1)S(1)}, bf16[4,14,12544]{2,1,0:T(8,128)(2,1)}, u32[]{:S(2)}) copy-start(bf16[4,14,12544]{2,1,0:T(8,128)(2,1)} %get-tuple-element.54) | copy-start | bytes 4214788

commit v7 on v6

--- a/solution.py
+++ b/solution.py
@@ -1403,9 +1403,18 @@
     return jnp.concatenate([high, middle, (left - middle.astype(F32)).astype(BF16)], 0)
 
 
-def final_kernel(result, narrow_map, *refs):
+def final_kernel(result_in, map_in, *refs):
     flat_out, (gain_out, shift_out, short_gain_out, short_shift_out) = refs[:11], refs[11:15]
     flat, (gain, shift, short_gain, short_shift), sems = refs[15:26], refs[26:30], refs[30]
+    result, narrow_map = refs[31:33]
+    loads = [
+        pltpu.make_async_copy(result_in, result, sems.at[15]),
+        pltpu.make_async_copy(map_in, narrow_map, sems.at[16]),
+    ]
+    for copy in loads:
+        copy.start()
+    for copy in loads:
+        copy.wait()
     section = lax.axis_index("section")
     total = nt(thirds(result[192:208]), narrow_map[...])
     total = total[0:16] + total[16:32] + total[32:48]
@@ -1448,16 +1457,15 @@
 
 
 def final_call(result, narrow_map):
-    vmem = pl.BlockSpec(memory_space=pltpu.VMEM)
     shapes = [(count, 128) for count in LINES] + [(3, 1, D), (3, 1, D), (1, DIN), (1, DIN)]
     return pl.pallas_call(
         final_kernel,
         out_shape=[jax.ShapeDtypeStruct(shape, F32) for shape in shapes],
-        in_specs=[vmem, vmem],
+        in_specs=[pl.BlockSpec(memory_space=pl.ANY)] * 2,
         out_specs=[pl.BlockSpec(memory_space=pl.ANY)] * 15,
         scratch_shapes=[pltpu.VMEM(shape, F32) for shape in shapes]
-        + [pltpu.SemaphoreType.DMA((15,))],
-        compiler_params=pltpu.CompilerParams(vmem_limit_bytes=16 << 20),
+        + [pltpu.SemaphoreType.DMA((17,)), pltpu.VMEM((208, C), F32), pltpu.VMEM((D, C), BF16)],
+        compiler_params=pltpu.CompilerParams(vmem_limit_bytes=60 << 20),
     )(result, narrow_map)
 
 

time: 220 us -> 222 us (level)
  Pallas kernels: 210 us -> 213 us
    unnamed x12 -> x8, local copies, waits for them, and re-layouts: 9.16 us -> 7.59 us
where the time goes in v7:
time: 222 us; the launch traced here: 221 us
  Pallas kernels  213 us (96%)
  local copies, waits for them, and re-layouts  7.59 us (3%)
    pallas_call x1, Pallas kernels, main_call(): pl.pallas_call(functools.partial(main_kernel, n_dp), out_shape=outs, in_s...  208 us
    unnamed x8, local copies, waits for them, and re-layouts  7.59 us
    pallas_call x1, Pallas kernels, final_call(): pl.pallas_call(final_kernel, out_shape=[jax.ShapeDtypeStruct(shape, F32)...  4.64 us

profile of v7, /device:TPU:0, one launch (start us, length us, event | category | flops | bytes accessed | tf_op | source)
XLA Modules:
  0.0 221.3 jit_solution(16336371854037837313)
XLA Ops:
  0.7 0.0 copy-start.1
  0.7 2.2 copy.38.upstream
  2.8 0.0 copy-done.1
  2.8 1.3 copy.37.features
  4.2 208.4 %shard_map.323 = (bf16[4,7,12544]{2,1,0:T(8,128)(2,1)}, bf16[4,14,12544]{2,1,0:T(8,128)(2,1)}, f32[208,1024]{1,0:T(8,128)}) custom-call(bf16[4,14,12544]{2,1,0:T(8,128)(2,1)} %copy.37.features, bf16[4,7,12544]{2,1,0:T(8,128)(2,1)} %copy.38.upstream, s32[4]{0:T(128)} %side_ref.1, bf16[2,896,1024]{2,1,0:T(8,128)(2,1)} %constant.4.clone.expand, ...), custom_call_target="tpu_custom_call" | custom-call | tf_op jit(solution)/shard_map/pallas_call | solution.py:1530
  212.6 2.3 %copy.39 = bf16[4,7,12544]{2,0,1:T(4,128)(2,1)} copy(bf16[4,7,12544]{2,1,0:T(8,128)(2,1)} %get-tuple-element.53) | data formatting | bytes 1404928
  214.9 0.0 copy-start
  214.9 4.6 %shard_map.324 = (f32[98,128]{1,0:T(8,128)}, f32[112,128]{1,0:T(8,128)}, f32[98,128]{1,0:T(8,128)}, f32[28,128]{1,0:T(8,128)}, f32[28,128]{1,0:T(8,128)}, /*inde...) custom-call(f32[208,1024]{1,0:T(8,128)} %get-tuple-element.37.result, ...), custom_call_target="tpu_custom_call" | custom-call | tf_op jit(solution)/shard_map/pallas_call | solution.py:1461
  219.5 0.0 copy-done
  219.5 1.8 copy.40
Async XLA Ops:
  0.7 2.2 copy-start.1
  214.9 4.6 %copy-start = (bf16[4,14,12544]{2,1,0:T(8,128)(2,1)S(1)}, bf16[4,14,12544]{2,1,0:T(8,128)(2,1)}, u32[]{:S(2)}) copy-start(bf16[4,14,12544]{2,1,0:T(8,128)(2,1)} %get-tuple-element.54) | copy-start | bytes 4214788
